TPU v7x, 512 devices: a whole 4x8x8 slice. The times are simulated.
512 devices in a mesh: band: 8 (over z), gx: 8 (over y_hi, core), gyz: 8 (over x, y_lo).
Axes of the slice: x: 4, y: 8 (y_hi: 4, y_lo: 2; y = y_hi * 2 + y_lo), z: 8, core: 2. Of those that a mesh axis runs over, the one named last changes fastest.
Arguments:
- orbitals: float32 [64, 64, 64, 128], P('band', 'gx', 'gyz'), may hold values from -14 to 14
- local_potential: float32 [64, 64, 128], P('gx', 'gyz'), may hold values from -2 to 0
- occupations: float32 [64], P('band'), may hold values from 0 to 2
- proj_values: float32 [64, 4, 512], replicated, may hold values from -0.25 to 0.25
- proj_strength: float32 [64, 4], replicated, may hold values from 0.5 to 3
- atom_block: int32 [64], replicated, may hold values from 0 to 63
- atom_offset: int32 [64, 3], replicated, may hold values from 0 to 120, as said below
Outputs:
- filtered: float32 [64, 64, 64, 128], P('band', 'gx', 'gyz')
- hartree: float32 [64, 64, 128], P('gx', 'gyz')
Inputs may be any that keep to these rules, and one draw needn't show every extreme that they name: `atom_offset`: column 0 lies in 0 to 0, column 1 in 0 to 0, column 2 in 0 to 120.
All inputs are finite; a program needn't handle non-finite values.
Results may differ from a plain program's by a relative error of at most 0.0001.
Values sent between devices are 32-bit elements; how exact they have to be, the bound alone decides.
No kernel may reach another device: no remote copies, remote signals or barrier semaphores. Data moves between devices by JAX's collectives and lax.ppermute only.
A program may use at most 64 MiB of HBM per device.

v0:
```python
import jax
import jax.numpy as jnp
from jax import lax
from jax.sharding import PartitionSpec as P

PB = 8
DEGREE = 8
LEVELS = 4
PRE = 2
POST = 2
COARSE = 4


STENCIL = (
    -5369.0 / 1800.0,
    12.0 / 7.0,
    -15.0 / 56.0,
    10.0 / 189.0,
    -1.0 / 112.0,
    2.0 / 1925.0,
    -1.0 / 16632.0,
)
stencil_reach = 6
center = 12.0
half_width = 8.0
spectrum_low = 0.0
damping = 0.8


def extended(value, sides, width):
    for axis, dim in sides:
        size, length = (lax.axis_size(axis), value.shape[dim])
        up = [(i, (i + 1) % size) for i in range(size - 1)]
        down = [(j, i) for i, j in up]
        last = lax.slice_in_dim(value, length - width, length, axis=dim)
        initial = lax.slice_in_dim(value, 0, width, axis=dim)
        before = lax.ppermute(last, axis, up)
        after = lax.ppermute(initial, axis, down)
        value = jnp.concatenate([before, value, after], axis=dim)
    return value


def axis_second(padded, along, length):
    summed = STENCIL[1] * (
        lax.slice_in_dim(padded, stencil_reach + 1, stencil_reach + 1 + length, axis=along)
        + lax.slice_in_dim(padded, stencil_reach - 1, stencil_reach - 1 + length, axis=along)
    )
    for offset in range(2, stencil_reach + 1):
        summed = summed + STENCIL[offset] * (
            lax.slice_in_dim(
                padded, stencil_reach + offset, stencil_reach + offset + length, axis=along
            )
            + lax.slice_in_dim(
                padded, stencil_reach - offset, stencil_reach - offset + length, axis=along
            )
        )
    return summed


def laplacian(samples, padded_list, axes_list):
    summed = 3.0 * STENCIL[0] * samples
    for padded, along in zip(padded_list, axes_list):
        summed = summed + axis_second(padded, along, samples.shape[along])
    return summed


def chebyshev(orbital, apply_ham):
    sigma_now = half_width / (spectrum_low - center)
    tau_value = 2.0 / sigma_now
    previous = orbital
    current = (apply_ham(orbital) - center * orbital) * (sigma_now / half_width)
    for _ in range(DEGREE - 1):
        sigma_next = 1.0 / (tau_value - sigma_now)
        upcoming = (apply_ham(current) - center * current) * (
            2.0 * sigma_next / half_width
        ) - sigma_now * sigma_next * previous
        previous = current
        current = upcoming
        sigma_now = sigma_next
    return current


def restrict_mean(residual):
    sx, sy, sz = residual.shape
    return residual.reshape(sx // 2, 2, sy // 2, 2, sz // 2, 2).mean(axis=(1, 3, 5))


def prolong_copy(coarse):
    sx, sy, sz = coarse.shape
    wide = jnp.broadcast_to(coarse[:, None, :, None, :, None], (sx, 2, sy, 2, sz, 2))
    return wide.reshape(2 * sx, 2 * sy, 2 * sz)


def cycle_level(grid_level, source, pad_cells):
    level_scale = 4.0**grid_level
    diagonal = 6.0 / level_scale

    def operate(iterate):
        padded = pad_cells(iterate)
        neighbours = padded[2:, 1:-1, 1:-1] + padded[:-2, 1:-1, 1:-1]
        neighbours = neighbours + padded[1:-1, 2:, 1:-1] + padded[1:-1, :-2, 1:-1]
        neighbours = neighbours + padded[1:-1, 1:-1, 2:] + padded[1:-1, 1:-1, :-2]
        return (6.0 * iterate - neighbours) / level_scale

    sweeps = COARSE if grid_level == LEVELS - 1 else PRE
    iterate = damping * source / diagonal
    for _ in range(sweeps - 1):
        iterate = iterate + damping * (source - operate(iterate)) / diagonal
    if grid_level < LEVELS - 1:
        residual = source - operate(iterate)
        correction = cycle_level(grid_level + 1, restrict_mean(residual), pad_cells)
        iterate = iterate + prolong_copy(correction)
        for _ in range(POST):
            iterate = iterate + damping * (source - operate(iterate)) / diagonal
    return iterate


def local(
    orbitals, local_potential, occupations, proj_values, proj_strength, atom_block, atom_offset
):
    band_count, width_x, width_y, depth_cells = orbitals.shape
    box_cells = proj_values.shape[2]
    my_block = lax.axis_index("gx") * lax.axis_size("gyz") + lax.axis_index("gyz")
    anchor = jnp.zeros((), jnp.int32)

    def nonlocal_term(orbital):

        def visit_atom(atom_index, accumulated):

            def include(partial_sum):
                corner = (
                    anchor,
                    atom_offset[atom_index, 0],
                    atom_offset[atom_index, 1],
                    atom_offset[atom_index, 2],
                )
                window = lax.dynamic_slice(orbital, corner, (band_count, PB, PB, PB)).reshape(
                    band_count, box_cells
                )
                shapes = proj_values[atom_index]
                weights = (
                    lax.dot_general(
                        window, shapes, (((1,), (1,)), ((), ())), precision=lax.Precision.HIGHEST
                    )
                    * proj_strength[atom_index]
                )
                added_term = jnp.dot(weights, shapes, precision=lax.Precision.HIGHEST).reshape(
                    band_count, PB, PB, PB
                )
                current = lax.dynamic_slice(partial_sum, corner, (band_count, PB, PB, PB))
                return lax.dynamic_update_slice(partial_sum, current + added_term, corner)

            def keep_sum(partial_sum):
                return partial_sum

            return lax.cond(atom_block[atom_index] == my_block, include, keep_sum, accumulated)

        return lax.fori_loop(0, proj_values.shape[0], visit_atom, jnp.zeros_like(orbital))

    def hamiltonian(orbital):
        padded = extended(orbital, (("gx", 1), ("gyz", 2)), stencil_reach)
        x_padded = padded[:, :, stencil_reach : stencil_reach + width_y, :]
        y_padded = padded[:, stencil_reach : stencil_reach + width_x, :, :]
        z_padded = jnp.pad(orbital, ((0, 0), (0, 0), (0, 0), (stencil_reach, stencil_reach)))
        kinetic = laplacian(orbital, (x_padded, y_padded, z_padded), (1, 2, 3))
        return -0.5 * kinetic + local_potential * orbital + nonlocal_term(orbital)

    filtered = chebyshev(orbitals, hamiltonian)
    density_part = jnp.sum(occupations[:, None, None, None] * filtered * filtered, axis=0)
    total_bands = band_count * lax.axis_size("band")
    density = lax.psum(density_part, "band")

    def pad_cells(iterate):
        padded = extended(iterate, (("gx", 0), ("gyz", 1)), 1)
        return jnp.pad(padded, ((0, 0), (0, 0), (1, 1)))

    hartree = cycle_level(0, density / total_bands, pad_cells)
    return (filtered, hartree)


def solution(mesh):
    placed = (P("band", "gx", "gyz", None), P("gx", "gyz", None), P("band"), P(), P(), P(), P())
    return jax.shard_map(
        local,
        mesh=mesh,
        in_specs=placed,
        out_specs=(P("band", "gx", "gyz", None), P("gx", "gyz", None)),
        check_vma=False,
    )
```

profile of v0, /device:TPU:6, one launch (start us, length us, event | category | flops | bytes accessed | tf_op | source)
XLA Modules:
  0.0 1598.9 jit_solution(14164408754262733109)
XLA Ops:
  17.2 87.4 %while.128 = (s32[]{:T(128)}, f32[8,8,8,128]{3,0,2,1:T(8,128)S(1)}, s32[64]{0:T(128)S(1)}, s32[]{:T(128)}, s32[64,3]{0,1:T(4,128)S(1)}, /*index=5*/f32[8,8,8,128...) while((s32[]{:T(128)}, f32[8,8,8,128]{3,0,2,1:T(8,128)S(1)}, s32[64]{0:T(128)S(1)}, ...), condition=%wide.region_3.4_spmd, body=%wide.region_0.3_spmd.sunk | while | flops 397354 | bytes 197191 | solution.py:158
  108.5 23.8 %collective-permute-start.5 = (f32[8,6,8,128]{3,0,2,1:T(8,128)S(1)}, f32[8,6,8,128]{3,0,2,1:T(8,128)S(1)}, u32[]{:S(2)}, u32[]{:S(2)}) collective-permute-start(f32[8,6,8,128]{3,0,2,1:T(8,128)S(1)} %get-tuple-element.1699), channel_id=1, source_target_pairs={{0,8},{8,16},{16,24},{24,32},{32,40},{40,48},{48,56},{1,9},{9,17},... | collective-permute-start | bytes 589832 | tf_op jit(solution)/shard_map/ppermute | solution.py:37
  166.6 74.9 %while.129 = (s32[]{:T(128)}, f32[8,8,8,128]{3,0,2,1:T(8,128)S(1)}, s32[64]{0:T(128)S(1)}, s32[]{:T(128)}, s32[64,3]{0,1:T(4,128)S(1)}, /*index=5*/f32[8,8,8,128...) while((s32[]{:T(128)}, f32[8,8,8,128]{3,0,2,1:T(8,128)S(1)}, s32[64]{0:T(128)S(1)}, ...), condition=%wide.region_7.8_spmd, body=%wide.region_4.7_spmd.sunk | while | flops 397354 | bytes 197191 | solution.py:158
  244.0 20.5 %collective-permute-start.9 = (f32[8,6,8,128]{3,0,2,1:T(8,128)S(1)}, f32[8,6,8,128]{3,0,2,1:T(8,128)S(1)}, u32[]{:S(2)}, u32[]{:S(2)}) collective-permute-start(f32[8,6,8,128]{3,0,2,1:T(8,128)S(1)} %get-tuple-element.1697), channel_id=1, source_target_pairs={{0,8},{8,16},{16,24},{24,32},{32,40},{40,48},{48,56},{1,9},{9,17},... | collective-permute-start | bytes 589832 | tf_op jit(solution)/shard_map/ppermute | solution.py:37
  268.5 29.0 %collective-permute-start.11 = (f32[8,20,6,128]{3,0,2,1:T(8,128)}, f32[8,20,6,128]{3,0,2,1:T(8,128)S(1)}, u32[]{:S(2)}, u32[]{:S(2)}) collective-permute-start(f32[8,20,6,128]{3,0,2,1:T(8,128)} %get-tuple-element.1679), channel_id=1, source_target_pairs={{0,1},{1,2},{2,3},{3,4},{4,5},{5,6},{6,7},{8,9},{9,10},{10,11},{11... | collective-permute-start | bytes 1474568 | tf_op jit(solution)/shard_map/ppermute | solution.py:37
  297.6 74.9 %while.130 = (s32[]{:T(128)}, f32[8,8,8,128]{3,0,2,1:T(8,128)S(1)}, s32[64]{0:T(128)S(1)}, s32[]{:T(128)}, s32[64,3]{0,1:T(4,128)S(1)}, /*index=5*/f32[8,8,8,128...) while((s32[]{:T(128)}, f32[8,8,8,128]{3,0,2,1:T(8,128)S(1)}, s32[64]{0:T(128)S(1)}, ...), condition=%wide.region_11.12_spmd, body=%wide.region_8.11_spmd.sunk | while | flops 397354 | bytes 197191 | solution.py:158
  375.0 20.5 %collective-permute-start.13 = (f32[8,6,8,128]{3,0,2,1:T(8,128)S(1)}, f32[8,6,8,128]{3,0,2,1:T(8,128)S(1)}, u32[]{:S(2)}, u32[]{:S(2)}) collective-permute-start(f32[8,6,8,128]{3,0,2,1:T(8,128)S(1)} %get-tuple-element.1695), channel_id=1, source_target_pairs={{0,8},{8,16},{16,24},{24,32},{32,40},{40,48},{48,56},{1,9},{9,17},... | collective-permute-start | bytes 589832 | tf_op jit(solution)/shard_map/ppermute | solution.py:37
  399.5 29.5 %collective-permute-start.15 = (f32[8,20,6,128]{3,0,2,1:T(8,128)}, f32[8,20,6,128]{3,0,2,1:T(8,128)S(1)}, u32[]{:S(2)}, u32[]{:S(2)}) collective-permute-start(f32[8,20,6,128]{3,0,2,1:T(8,128)} %get-tuple-element.1675), channel_id=1, source_target_pairs={{0,1},{1,2},{2,3},{3,4},{4,5},{5,6},{6,7},{8,9},{9,10},{10,11},{11... | collective-permute-start | bytes 1474568 | tf_op jit(solution)/shard_map/ppermute | solution.py:37
  429.1 74.9 %while.131 = (s32[]{:T(128)}, f32[8,8,8,128]{3,0,2,1:T(8,128)S(1)}, s32[64]{0:T(128)S(1)}, s32[]{:T(128)}, s32[64,3]{0,1:T(4,128)S(1)}, /*index=5*/f32[8,8,8,128...) while((s32[]{:T(128)}, f32[8,8,8,128]{3,0,2,1:T(8,128)S(1)}, s32[64]{0:T(128)S(1)}, ...), condition=%wide.region_15.16_spmd, body=%wide.region_12.15_spmd.sunk | while | flops 397354 | bytes 197191 | solution.py:158
  506.5 20.5 %collective-permute-start.17 = (f32[8,6,8,128]{3,0,2,1:T(8,128)S(1)}, f32[8,6,8,128]{3,0,2,1:T(8,128)S(1)}, u32[]{:S(2)}, u32[]{:S(2)}) collective-permute-start(f32[8,6,8,128]{3,0,2,1:T(8,128)S(1)} %get-tuple-element.1693), channel_id=1, source_target_pairs={{0,8},{8,16},{16,24},{24,32},{32,40},{40,48},{48,56},{1,9},{9,17},... | collective-permute-start | bytes 589832 | tf_op jit(solution)/shard_map/ppermute | solution.py:37
  560.1 74.9 %while.132 = (s32[]{:T(128)}, f32[8,8,8,128]{3,0,2,1:T(8,128)S(1)}, s32[64]{0:T(128)S(1)}, s32[]{:T(128)}, s32[64,3]{0,1:T(4,128)S(1)}, /*index=5*/f32[8,8,8,128...) while((s32[]{:T(128)}, f32[8,8,8,128]{3,0,2,1:T(8,128)S(1)}, s32[64]{0:T(128)S(1)}, ...), condition=%wide.region_19.20_spmd, body=%wide.region_16.19_spmd.sunk | while | flops 397354 | bytes 197191 | solution.py:158
  637.5 20.5 %collective-permute-start.21 = (f32[8,6,8,128]{3,0,2,1:T(8,128)S(1)}, f32[8,6,8,128]{3,0,2,1:T(8,128)S(1)}, u32[]{:S(2)}, u32[]{:S(2)}) collective-permute-start(f32[8,6,8,128]{3,0,2,1:T(8,128)S(1)} %get-tuple-element.1691), channel_id=1, source_target_pairs={{0,8},{8,16},{16,24},{24,32},{32,40},{40,48},{48,56},{1,9},{9,17},... | collective-permute-start | bytes 589832 | tf_op jit(solution)/shard_map/ppermute | solution.py:37
  660.1 38.9 %collective-permute-start.22 = (f32[8,20,6,128]{3,0,2,1:T(8,128)}, f32[8,20,6,128]{3,0,2,1:T(8,128)S(1)}, u32[]{:S(2)}, u32[]{:S(2)}) collective-permute-start(f32[8,20,6,128]{3,0,2,1:T(8,128)} %get-tuple-element.1666), channel_id=1, source_target_pairs={{1,0},{2,1},{3,2},{4,3},{5,4},{6,5},{7,6},{9,8},{10,9},{11,10},{12... | collective-permute-start | bytes 1474568 | tf_op jit(solution)/shard_map/ppermute | solution.py:38
  701.0 74.9 %while.133 = (s32[]{:T(128)}, f32[8,8,8,128]{3,0,2,1:T(8,128)S(1)}, s32[64]{0:T(128)S(1)}, s32[]{:T(128)}, s32[64,3]{0,1:T(4,128)S(1)}, /*index=5*/f32[8,8,8,128...) while((s32[]{:T(128)}, f32[8,8,8,128]{3,0,2,1:T(8,128)S(1)}, s32[64]{0:T(128)S(1)}, ...), condition=%wide.region_23.24_spmd, body=%wide.region_20.23_spmd.sunk | while | flops 397354 | bytes 197191 | solution.py:158
  798.2 50.5 %collective-permute-start.26 = (f32[8,20,6,128]{3,0,2,1:T(8,128)}, f32[8,20,6,128]{3,0,2,1:T(8,128)S(1)}, u32[]{:S(2)}, u32[]{:S(2)}) collective-permute-start(f32[8,20,6,128]{3,0,2,1:T(8,128)} %get-tuple-element.1662), channel_id=1, source_target_pairs={{1,0},{2,1},{3,2},{4,3},{5,4},{6,5},{7,6},{9,8},{10,9},{11,10},{12... | collective-permute-start | bytes 1474568 | tf_op jit(solution)/shard_map/ppermute | solution.py:38
  850.9 89.6 %while.134 = (s32[]{:T(128)}, f32[8,8,8,128]{3,0,2,1:T(8,128)S(1)}, s32[64]{0:T(128)S(1)}, s32[]{:T(128)}, s32[64,3]{0,1:T(4,128)S(1)}, /*index=5*/f32[8,8,8,128...) while((s32[]{:T(128)}, f32[8,8,8,128]{3,0,2,1:T(8,128)S(1)}, s32[64]{0:T(128)S(1)}, ...), condition=%wide.region_27.28_spmd, body=%wide.region_24.27_spmd.sunk | while | flops 397354 | bytes 197191 | solution.py:158
  962.9 50.6 %collective-permute-start.30 = (f32[8,20,6,128]{3,0,2,1:T(8,128)}, f32[8,20,6,128]{3,0,2,1:T(8,128)S(1)}, u32[]{:S(2)}, u32[]{:S(2)}) collective-permute-start(f32[8,20,6,128]{3,0,2,1:T(8,128)} %get-tuple-element.1658), channel_id=1, source_target_pairs={{1,0},{2,1},{3,2},{4,3},{5,4},{6,5},{7,6},{9,8},{10,9},{11,10},{12... | collective-permute-start | bytes 1474568 | tf_op jit(solution)/shard_map/ppermute | solution.py:38
  1015.6 81.7 %while.135 = (s32[]{:T(128)}, f32[8,8,8,128]{3,0,2,1:T(8,128)S(1)}, s32[64]{0:T(128)S(1)}, s32[]{:T(128)}, s32[64,3]{0,1:T(4,128)S(1)}, /*index=5*/f32[8,8,8,128...) while((s32[]{:T(128)}, f32[8,8,8,128]{3,0,2,1:T(8,128)S(1)}, s32[64]{0:T(128)S(1)}, ...), condition=%wide.region_31.32_spmd, body=%wide.region_28.31_spmd.sunk | while | flops 397354 | bytes 197191 | solution.py:158
  1098.9 36.0 %psum.7 = f32[8,8,128]{2,1,0:T(8,128)S(1)} all-reduce(f32[8,8,128]{2,1,0:T(8,128)S(1)} %get-tuple-element.1652), channel_id=1, replica_groups=mesh['band'=8,'gx'=8,'gyz'=8] {'band'}, use_global_device_ids=true, to_apply=%region_33.34 | all-reduce | flops 8192 | bytes 65536 | tf_op jit(solution)/shard_map/psum | solution.py:171
  1148.1 58.2 %collective-permute-start.34 = (f32[10,1,128]{2,1,0:T(1,128)S(1)}, f32[10,1,128]{2,1,0:T(1,128)S(1)}, u32[]{:S(2)}, u32[]{:S(2)}) collective-permute-start(f32[10,1,128]{2,1,0:T(1,128)S(1)} %get-tuple-element.1716), channel_id=1, source_target_pairs={{1,0},{2,1},{3,2},{4,3},{5,4},{6,5},{7,6},{9,8},{10,9},{11,10},{12... | collective-permute-start | bytes 15368 | tf_op jit(solution)/shard_map/ppermute | solution.py:38
  1208.3 29.5 %collective-permute-done.35 = f32[10,1,128]{2,1,0:T(1,128)S(1)} collective-permute-done((f32[10,1,128]{2,1,0:T(1,128)S(1)}, f32[10,1,128]{2,1,0:T(1,128)S(1)}, u32[]{:S(2)}, u32[]{:S(2)}) %collective-permute-start.35) | collective-permute-done | bytes 5152 | tf_op jit(solution)/shard_map/ppermute | solution.py:37
  1252.4 48.5 %collective-permute-start.38 = (f32[10,1,128]{2,1,0:T(1,128)S(1)}, f32[10,1,128]{2,1,0:T(1,128)S(1)}, u32[]{:S(2)}, u32[]{:S(2)}) collective-permute-start(f32[10,1,128]{2,1,0:T(1,128)S(1)} %get-tuple-element.1714), channel_id=1, source_target_pairs={{1,0},{2,1},{3,2},{4,3},{5,4},{6,5},{7,6},{9,8},{10,9},{11,10},{12... | collective-permute-start | bytes 15368 | tf_op jit(solution)/shard_map/ppermute | solution.py:38
  1329.2 33.1 %collective-permute-start.45 = (f32[1,4,64]{2,1,0:T(4,128)S(1)}, f32[1,4,64]{2,1,0:T(4,128)S(1)}, u32[]{:S(2)}, u32[]{:S(2)}) collective-permute-start(f32[1,4,64]{2,1,0:T(4,128)S(1)} %get-tuple-element.1737), channel_id=1, source_target_pairs={{0,8},{8,16},{16,24},{24,32},{32,40},{40,48},{48,56},{1,9},{9,17},... | collective-permute-start | bytes 3080 | tf_op jit(solution)/shard_map/ppermute | solution.py:37
  1373.4 38.7 %collective-permute-start.49 = (f32[1,2,32]{2,1,0:T(2,128)S(1)}, f32[1,2,32]{2,1,0:T(2,128)S(1)}, u32[]{:S(2)}, u32[]{:S(2)}) collective-permute-start(f32[1,2,32]{2,1,0:T(2,128)S(1)} %get-tuple-element.1755), channel_id=1, source_target_pairs={{0,8},{8,16},{16,24},{24,32},{32,40},{40,48},{48,56},{1,9},{9,17},... | collective-permute-start | bytes 776 | tf_op jit(solution)/shard_map/ppermute | solution.py:37
  (1345 shorter events, 722.0 us)
Async XLA Ops:
  10.4 94.2 %collective-permute-start.2 = (f32[8,20,6,128]{3,0,2,1:T(8,128)}, f32[8,20,6,128]{3,0,2,1:T(8,128)}, u32[]{:S(2)}, u32[]{:S(2)}) collective-permute-start(f32[8,20,6,128]{3,0,2,1:T(8,128)} %get-tuple-element.1684), channel_id=1, source_target_pairs={{1,0},{2,1},{3,2},{4,3},{5,4},{6,5},{7,6},{9,8},{10,9},{11,10},{12... | collective-permute-start | bytes 1474568 | tf_op jit(solution)/shard_map/ppermute | solution.py:38
  14.2 90.4 %collective-permute-start.3 = (f32[8,20,6,128]{3,0,2,1:T(8,128)}, f32[8,20,6,128]{3,0,2,1:T(8,128)}, u32[]{:S(2)}, u32[]{:S(2)}) collective-permute-start(f32[8,20,6,128]{3,0,2,1:T(8,128)} %get-tuple-element.1685), channel_id=1, source_target_pairs={{0,1},{1,2},{2,3},{3,4},{4,5},{5,6},{6,7},{8,9},{9,10},{10,11},{11... | collective-permute-start | bytes 1474568 | tf_op jit(solution)/shard_map/ppermute | solution.py:37
  107.2 25.1 %collective-permute-start.4 = (f32[8,6,8,128]{3,0,2,1:T(8,128)S(1)}, f32[8,6,8,128]{3,0,2,1:T(8,128)S(1)}, u32[]{:S(2)}, u32[]{:S(2)}) collective-permute-start(f32[8,6,8,128]{3,0,2,1:T(8,128)S(1)} %get-tuple-element.1698), channel_id=1, source_target_pairs={{8,0},{16,8},{24,16},{32,24},{40,32},{48,40},{56,48},{9,1},{17,9},... | collective-permute-start | bytes 589832 | tf_op jit(solution)/shard_map/ppermute | solution.py:38
  134.4 107.1 %collective-permute-start.6 = (f32[8,20,6,128]{3,0,2,1:T(8,128)}, f32[8,20,6,128]{3,0,2,1:T(8,128)S(1)}, u32[]{:S(2)}, u32[]{:S(2)}) collective-permute-start(f32[8,20,6,128]{3,0,2,1:T(8,128)} %get-tuple-element.1682), channel_id=1, source_target_pairs={{1,0},{2,1},{3,2},{4,3},{5,4},{6,5},{7,6},{9,8},{10,9},{11,10},{12... | collective-permute-start | bytes 1474568 | tf_op jit(solution)/shard_map/ppermute | solution.py:38
  146.7 94.8 %collective-permute-start.7 = (f32[8,20,6,128]{3,0,2,1:T(8,128)}, f32[8,20,6,128]{3,0,2,1:T(8,128)S(1)}, u32[]{:S(2)}, u32[]{:S(2)}) collective-permute-start(f32[8,20,6,128]{3,0,2,1:T(8,128)} %get-tuple-element.1683), channel_id=1, source_target_pairs={{0,1},{1,2},{2,3},{3,4},{4,5},{5,6},{6,7},{8,9},{9,10},{10,11},{11... | collective-permute-start | bytes 1474568 | tf_op jit(solution)/shard_map/ppermute | solution.py:37
  266.6 106.0 %collective-permute-start.10 = (f32[8,20,6,128]{3,0,2,1:T(8,128)}, f32[8,20,6,128]{3,0,2,1:T(8,128)S(1)}, u32[]{:S(2)}, u32[]{:S(2)}) collective-permute-start(f32[8,20,6,128]{3,0,2,1:T(8,128)} %get-tuple-element.1678), channel_id=1, source_target_pairs={{1,0},{2,1},{3,2},{4,3},{5,4},{6,5},{7,6},{9,8},{10,9},{11,10},{12... | collective-permute-start | bytes 1474568 | tf_op jit(solution)/shard_map/ppermute | solution.py:38
  268.5 104.1 %collective-permute-start.11 = (f32[8,20,6,128]{3,0,2,1:T(8,128)}, f32[8,20,6,128]{3,0,2,1:T(8,128)S(1)}, u32[]{:S(2)}, u32[]{:S(2)}) collective-permute-start(f32[8,20,6,128]{3,0,2,1:T(8,128)} %get-tuple-element.1679), channel_id=1, source_target_pairs={{0,1},{1,2},{2,3},{3,4},{4,5},{5,6},{6,7},{8,9},{9,10},{10,11},{11... | collective-permute-start | bytes 1474568 | tf_op jit(solution)/shard_map/ppermute | solution.py:37
  397.6 106.4 %collective-permute-start.14 = (f32[8,20,6,128]{3,0,2,1:T(8,128)}, f32[8,20,6,128]{3,0,2,1:T(8,128)S(1)}, u32[]{:S(2)}, u32[]{:S(2)}) collective-permute-start(f32[8,20,6,128]{3,0,2,1:T(8,128)} %get-tuple-element.1674), channel_id=1, source_target_pairs={{1,0},{2,1},{3,2},{4,3},{5,4},{6,5},{7,6},{9,8},{10,9},{11,10},{12... | collective-permute-start | bytes 1474568 | tf_op jit(solution)/shard_map/ppermute | solution.py:38
  399.5 104.5 %collective-permute-start.15 = (f32[8,20,6,128]{3,0,2,1:T(8,128)}, f32[8,20,6,128]{3,0,2,1:T(8,128)S(1)}, u32[]{:S(2)}, u32[]{:S(2)}) collective-permute-start(f32[8,20,6,128]{3,0,2,1:T(8,128)} %get-tuple-element.1675), channel_id=1, source_target_pairs={{0,1},{1,2},{2,3},{3,4},{4,5},{5,6},{6,7},{8,9},{9,10},{10,11},{11... | collective-permute-start | bytes 1474568 | tf_op jit(solution)/shard_map/ppermute | solution.py:37
  529.1 106.0 %collective-permute-start.18 = (f32[8,20,6,128]{3,0,2,1:T(8,128)}, f32[8,20,6,128]{3,0,2,1:T(8,128)S(1)}, u32[]{:S(2)}, u32[]{:S(2)}) collective-permute-start(f32[8,20,6,128]{3,0,2,1:T(8,128)} %get-tuple-element.1670), channel_id=1, source_target_pairs={{1,0},{2,1},{3,2},{4,3},{5,4},{6,5},{7,6},{9,8},{10,9},{11,10},{12... | collective-permute-start | bytes 1474568 | tf_op jit(solution)/shard_map/ppermute | solution.py:38
  549.1 86.0 %collective-permute-start.19 = (f32[8,20,6,128]{3,0,2,1:T(8,128)}, f32[8,20,6,128]{3,0,2,1:T(8,128)S(1)}, u32[]{:S(2)}, u32[]{:S(2)}) collective-permute-start(f32[8,20,6,128]{3,0,2,1:T(8,128)} %get-tuple-element.1671), channel_id=1, source_target_pairs={{0,1},{1,2},{2,3},{3,4},{4,5},{5,6},{6,7},{8,9},{9,10},{10,11},{11... | collective-permute-start | bytes 1474568 | tf_op jit(solution)/shard_map/ppermute | solution.py:37
  660.1 115.9 %collective-permute-start.22 = (f32[8,20,6,128]{3,0,2,1:T(8,128)}, f32[8,20,6,128]{3,0,2,1:T(8,128)S(1)}, u32[]{:S(2)}, u32[]{:S(2)}) collective-permute-start(f32[8,20,6,128]{3,0,2,1:T(8,128)} %get-tuple-element.1666), channel_id=1, source_target_pairs={{1,0},{2,1},{3,2},{4,3},{5,4},{6,5},{7,6},{9,8},{10,9},{11,10},{12... | collective-permute-start | bytes 1474568 | tf_op jit(solution)/shard_map/ppermute | solution.py:38
  699.0 77.0 %collective-permute-start.23 = (f32[8,20,6,128]{3,0,2,1:T(8,128)}, f32[8,20,6,128]{3,0,2,1:T(8,128)S(1)}, u32[]{:S(2)}, u32[]{:S(2)}) collective-permute-start(f32[8,20,6,128]{3,0,2,1:T(8,128)} %get-tuple-element.1667), channel_id=1, source_target_pairs={{0,1},{1,2},{2,3},{3,4},{4,5},{5,6},{6,7},{8,9},{9,10},{10,11},{11... | collective-permute-start | bytes 1474568 | tf_op jit(solution)/shard_map/ppermute | solution.py:37
  798.2 142.3 %collective-permute-start.26 = (f32[8,20,6,128]{3,0,2,1:T(8,128)}, f32[8,20,6,128]{3,0,2,1:T(8,128)S(1)}, u32[]{:S(2)}, u32[]{:S(2)}) collective-permute-start(f32[8,20,6,128]{3,0,2,1:T(8,128)} %get-tuple-element.1662), channel_id=1, source_target_pairs={{1,0},{2,1},{3,2},{4,3},{5,4},{6,5},{7,6},{9,8},{10,9},{11,10},{12... | collective-permute-start | bytes 1474568 | tf_op jit(solution)/shard_map/ppermute | solution.py:38
  848.8 91.8 %collective-permute-start.27 = (f32[8,20,6,128]{3,0,2,1:T(8,128)S(1)}, f32[8,20,6,128]{3,0,2,1:T(8,128)S(1)}, u32[]{:S(2)}, u32[]{:S(2)}) collective-permute-start(f32[8,20,6,128]{3,0,2,1:T(8,128)S(1)} %get-tuple-element.1663), channel_id=1, source_target_pairs={{0,1},{1,2},{2,3},{3,4},{4,5},{5,6},{6,7},{8,9},{9,10},{10,11},{11... | collective-permute-start | bytes 1474568 | tf_op jit(solution)/shard_map/ppermute | solution.py:37
  962.9 134.4 %collective-permute-start.30 = (f32[8,20,6,128]{3,0,2,1:T(8,128)}, f32[8,20,6,128]{3,0,2,1:T(8,128)S(1)}, u32[]{:S(2)}, u32[]{:S(2)}) collective-permute-start(f32[8,20,6,128]{3,0,2,1:T(8,128)} %get-tuple-element.1658), channel_id=1, source_target_pairs={{1,0},{2,1},{3,2},{4,3},{5,4},{6,5},{7,6},{9,8},{10,9},{11,10},{12... | collective-permute-start | bytes 1474568 | tf_op jit(solution)/shard_map/ppermute | solution.py:38
  1013.5 83.8 %collective-permute-start.31 = (f32[8,20,6,128]{3,0,2,1:T(8,128)S(1)}, f32[8,20,6,128]{3,0,2,1:T(8,128)S(1)}, u32[]{:S(2)}, u32[]{:S(2)}) collective-permute-start(f32[8,20,6,128]{3,0,2,1:T(8,128)S(1)} %get-tuple-element.1659), channel_id=1, source_target_pairs={{0,1},{1,2},{2,3},{3,4},{4,5},{5,6},{6,7},{8,9},{9,10},{10,11},{11... | collective-permute-start | bytes 1474568 | tf_op jit(solution)/shard_map/ppermute | solution.py:37
  1148.1 60.1 %collective-permute-start.34 = (f32[10,1,128]{2,1,0:T(1,128)S(1)}, f32[10,1,128]{2,1,0:T(1,128)S(1)}, u32[]{:S(2)}, u32[]{:S(2)}) collective-permute-start(f32[10,1,128]{2,1,0:T(1,128)S(1)} %get-tuple-element.1716), channel_id=1, source_target_pairs={{1,0},{2,1},{3,2},{4,3},{5,4},{6,5},{7,6},{9,8},{10,9},{11,10},{12... | collective-permute-start | bytes 15368 | tf_op jit(solution)/shard_map/ppermute | solution.py:38
  1206.3 31.5 %collective-permute-start.35 = (f32[10,1,128]{2,1,0:T(1,128)S(1)}, f32[10,1,128]{2,1,0:T(1,128)S(1)}, u32[]{:S(2)}, u32[]{:S(2)}) collective-permute-start(f32[10,1,128]{2,1,0:T(1,128)S(1)} %get-tuple-element.1715), channel_id=1, source_target_pairs={{0,1},{1,2},{2,3},{3,4},{4,5},{5,6},{6,7},{8,9},{9,10},{10,11},{11... | collective-permute-start | bytes 15368 | tf_op jit(solution)/shard_map/ppermute | solution.py:37
  1252.4 50.5 %collective-permute-start.38 = (f32[10,1,128]{2,1,0:T(1,128)S(1)}, f32[10,1,128]{2,1,0:T(1,128)S(1)}, u32[]{:S(2)}, u32[]{:S(2)}) collective-permute-start(f32[10,1,128]{2,1,0:T(1,128)S(1)} %get-tuple-element.1714), channel_id=1, source_target_pairs={{1,0},{2,1},{3,2},{4,3},{5,4},{6,5},{7,6},{9,8},{10,9},{11,10},{12... | collective-permute-start | bytes 15368 | tf_op jit(solution)/shard_map/ppermute | solution.py:38
  1327.9 34.5 %collective-permute-start.44 = (f32[1,4,64]{2,1,0:T(4,128)S(1)}, f32[1,4,64]{2,1,0:T(4,128)S(1)}, u32[]{:S(2)}, u32[]{:S(2)}) collective-permute-start(f32[1,4,64]{2,1,0:T(4,128)S(1)} %get-tuple-element.1738), channel_id=1, source_target_pairs={{8,0},{16,8},{24,16},{32,24},{40,32},{48,40},{56,48},{9,1},{17,9},... | collective-permute-start | bytes 3080 | tf_op jit(solution)/shard_map/ppermute | solution.py:38
  1329.2 34.0 %collective-permute-start.45 = (f32[1,4,64]{2,1,0:T(4,128)S(1)}, f32[1,4,64]{2,1,0:T(4,128)S(1)}, u32[]{:S(2)}, u32[]{:S(2)}) collective-permute-start(f32[1,4,64]{2,1,0:T(4,128)S(1)} %get-tuple-element.1737), channel_id=1, source_target_pairs={{0,8},{8,16},{16,24},{24,32},{32,40},{40,48},{48,56},{1,9},{9,17},... | collective-permute-start | bytes 3080 | tf_op jit(solution)/shard_map/ppermute | solution.py:37
  1372.1 40.0 %collective-permute-start.48 = (f32[1,2,32]{2,1,0:T(2,128)S(1)}, f32[1,2,32]{2,1,0:T(2,128)S(1)}, u32[]{:S(2)}, u32[]{:S(2)}) collective-permute-start(f32[1,2,32]{2,1,0:T(2,128)S(1)} %get-tuple-element.1756), channel_id=1, source_target_pairs={{8,0},{16,8},{24,16},{32,24},{40,32},{48,40},{56,48},{9,1},{17,9},... | collective-permute-start | bytes 776 | tf_op jit(solution)/shard_map/ppermute | solution.py:38
  1373.4 39.5 %collective-permute-start.49 = (f32[1,2,32]{2,1,0:T(2,128)S(1)}, f32[1,2,32]{2,1,0:T(2,128)S(1)}, u32[]{:S(2)}, u32[]{:S(2)}) collective-permute-start(f32[1,2,32]{2,1,0:T(2,128)S(1)} %get-tuple-element.1755), channel_id=1, source_target_pairs={{0,8},{8,16},{16,24},{24,32},{32,40},{40,48},{48,56},{1,9},{9,17},... | collective-permute-start | bytes 776 | tf_op jit(solution)/shard_map/ppermute | solution.py:37
  (74 other events, 786.4 us)
where the time goes:
time: 1630 us; the launch traced here: 1600 us
  starting transfers between devices  806 us (49%)
  loops' own time  332 us (20%)
  local copies, waits for them, and re-layouts  317 us (19%)
  waiting for transfers between devices  90.4 us (6%)
  blocking collectives  36 us (2%)
    ppermute x46, starting transfers between devices, extended(): before = lax.ppermute(last, axis, up)  463 us
    ppermute x46, starting transfers between devices, extended(): after = lax.ppermute(initial, axis, down)  343 us
    another operation x8, loops' own time, nonlocal_term(): lax.fori_loop(0, proj_values.shape[0], visit_atom, jnp.zeros_like(orbital))  326 us
    dynamic_slice x512, local copies, waits for them, and re-layouts, visit_atom(): atom_block[atom_index] == my_block  301 us
    ppermute x46, waiting for transfers between devices, extended(): before = lax.ppermute(last, axis, up)  86.1 us
    psum x1, blocking collectives, local(): density = lax.psum(density_part, 'band')  36 us
  transfers between devices with their start and end apart: 92, of which 38 were waited for; matrix products, arithmetic and copies ran while one was open for 19% of the time, Pallas kernels for 0%

commit v1 on v0

v1 whole, which is shorter than its diff:
```python
import functools

import jax
import jax.numpy as jnp
import numpy as np
from jax import lax
from jax.experimental import pallas as pl
from jax.experimental.pallas import tpu as pltpu
from jax.sharding import Mesh
from jax.sharding import PartitionSpec as P

DEGREE = 8
LEVELS = 4
PRE = 2
POST = 2
COARSE = 4
STENCIL = (
    -5369.0 / 1800.0,
    12.0 / 7.0,
    -15.0 / 56.0,
    10.0 / 189.0,
    -1.0 / 112.0,
    2.0 / 1925.0,
    -1.0 / 16632.0,
)
HALF = tuple(-0.5 * c for c in STENCIL)
REACH = 6
CENTER = 12.0
HALF_WIDTH = 8.0
DAMPING = 0.8
BAND = "z"
GX = ("yhi", "core")
GYZ = ("xhi", "xlo", "ylo")
PLANE = GX + GYZ
GROUP = ("core", "xlo", "ylo")
CHIPS = ((0, 0), (0, 1), (1, 1), (1, 0))
SLAB_DEVICE = [c * 4 + xl * 2 + yl for xl, yl in CHIPS for c in (0, 1)]
VMEM = pltpu.CompilerParams(vmem_limit_bytes=40 * 1024 * 1024)
F32 = jnp.float32
BF16 = jnp.bfloat16


def plane_index(band, slab):
    yhi, xhi = band // 2, band % 2
    xlo, ylo = CHIPS[slab // 2]
    return yhi * 16 + (slab % 2) * 8 + xhi * 4 + xlo * 2 + ylo


def coupling():
    own, xu, xd, yu, yd = (np.zeros((128, 128)) for _ in range(5))
    for zh in range(2):
        for xi in range(8):
            for yi in range(8):
                i = zh * 64 + xi * 8 + yi
                for o in range(8):
                    for m, k in ((own, abs(o - xi)), (xu, o + 8 - xi), (xd, xi + 8 - o)):
                        if 1 <= k <= REACH:
                            m[i, zh * 64 + o * 8 + yi] += HALF[k]
                    for m, k in ((own, abs(o - yi)), (yu, o + 8 - yi), (yd, yi + 8 - o)):
                        if 1 <= k <= REACH:
                            m[i, zh * 64 + xi * 8 + o] += HALF[k]
    whole = np.concatenate([own, xu, xd, yu, yd], axis=1).astype(np.float32)
    high = whole.astype(jnp.bfloat16)
    low = (whole - high.astype(np.float32)).astype(jnp.bfloat16)
    return np.concatenate([high, high], axis=0), low


def lanes_low(shape):
    return lax.broadcasted_iota(jnp.int32, shape, len(shape) - 1) < 64


def swap(x):
    return pltpu.roll(x, 64, x.ndim - 1)


def split3(x):
    a = x.astype(BF16)
    r = x - a.astype(F32)
    b = r.astype(BF16)
    c = (r - b.astype(F32)).astype(BF16)
    return a, b, c


def pack_kernel(orb_ref, pot_ref, proj_ref, pick_ref, out_ref, tiles_ref):
    low = lanes_low((8, 128))
    for q in range(4):
        turned = orb_ref[q * 128 : (q + 1) * 128, :].T
        for s in range(8):
            a = turned[s * 16 : s * 16 + 8, :]
            b = turned[s * 16 + 8 : s * 16 + 16, :]
            out_ref[plane_index(2 * q, s), 0:8, :] = jnp.where(low, a, swap(b))
            out_ref[plane_index(2 * q + 1, s), 0:8, :] = jnp.where(low, swap(a), b)
    pot = pot_ref[...]
    turned = jnp.concatenate([pot, pot], axis=0).T
    for s in range(8):
        piece = jnp.where(low, turned[s * 16 : s * 16 + 8, :], turned[s * 16 + 8 : s * 16 + 16, :])
        for b in range(8):
            out_ref[plane_index(b, s), 8:16, :] = piece

    keep = lax.broadcasted_iota(jnp.int32, (32, 8, 512), 2) % 8 == lax.broadcasted_iota(
        jnp.int32, (32, 8, 512), 1
    )

    def body(i, carry):
        rows = proj_ref[pl.ds(pl.multiple_of(i * 32, 32), 32), :]
        spread = jnp.where(keep, rows[:, None, :], 0.0).reshape(256, 512)
        pick = pick_ref[...]
        total = sum(jnp.dot(part, pick, preferred_element_type=F32) for part in split3(spread))
        tiles_ref[pl.ds(i * 8, 8), :, :, :] = total.reshape(8, 4, 8, 128)
        return carry

    lax.fori_loop(0, 8, body, 0)


def pack(orbitals, potential, proj):
    pick = (np.arange(512)[:, None] // 8 == np.arange(128)[None, :] % 64).astype(jnp.bfloat16)
    return pl.pallas_call(
        pack_kernel,
        out_shape=(
            jax.ShapeDtypeStruct((64, 16, 128), F32),
            jax.ShapeDtypeStruct((64, 4, 8, 128), F32),
        ),
        compiler_params=VMEM,
    )(orbitals.reshape(512, 128), potential.reshape(64, 128), proj.reshape(256, 512), pick)


ID, SRC, ROW, UPPER, ROW_L, ON_L, ROW_U, ON_U, META = range(9)


def double_kernel(
    first, last, coef1, coef2, lists, strength, prev_ref, own_ref, next_ref, *refs
):
    refs = list(refs)
    if first:
        older_ref = pot_ref = None
    else:
        older_ref, pot_ref = refs.pop(0), refs.pop(0)
    tiles_ref, mat_ref, mat_low_ref, ones_ref = refs[:4]
    refs = refs[4:]
    out_ref = refs.pop(0)
    if first:
        pot_ref = refs.pop(0)
    mid_ref = None if last else refs.pop(0)
    ext, mid, new, c_own, c_xu, c_xd, c_yu, c_yd, weights = refs
    low = lanes_low((8, 128))
    count = lists[META, 0]
    below = lists[META, 1] > 0
    above = lists[META, 2] > 0
    zero8 = jnp.zeros((8, 128), F32)

    def fill(i, carry):
        for u in range(4):
            src = i * 4 + u
            p, o, n = prev_ref[src, 0:8, :], own_ref[src, 0:8, :], next_ref[src, 0:8, :]
            ext[src, 0:8, :] = p
            ext[src, 8:16, :] = swap(jnp.where(low, o, p))
            ext[src, 16:24, :] = o
            ext[src, 24:32, :] = swap(jnp.where(low, n, o))
            ext[src, 32:40, :] = n
            if first:
                p, o, n = prev_ref[src, 8:16, :], own_ref[src, 8:16, :], next_ref[src, 8:16, :]
                shift = 3.0 * HALF[0] - CENTER
                pot_ref[src, 0:8, :] = swap(jnp.where(low, o, p)) + shift
                pot_ref[src, 8:16, :] = o + shift
                pot_ref[src, 16:24, :] = swap(jnp.where(low, n, o)) + shift
        return carry

    lax.fori_loop(0, 16, fill, 0)
    for t in range(3):
        for e in range(8):
            c_xu[t, e, :, :] = zero8
            c_xd[t, 64 + e, :, :] = zero8

    def products(f_ref, first_tile, n_tiles):
        def body(i, carry):
            t = first_tile + i // 2
            base = pl.multiple_of((i % 2) * 32, 32)
            rows = pl.multiple_of(t * 8 + 8, 8)
            x = f_ref[pl.ds(base, 32), pl.ds(rows, 8), :].reshape(256, 128)
            high = x.astype(BF16)
            rest = (x - high.astype(F32)).astype(BF16)
            y = jnp.dot(
                jnp.concatenate([high, rest], axis=1), mat_ref[...], preferred_element_type=F32
            ) + jnp.dot(high, mat_low_ref[...], preferred_element_type=F32)
            y = y.reshape(32, 8, 640)
            c_own[t, pl.ds(base, 32), :, :] = y[:, :, 0:128]
            c_xu[t, pl.ds(base + 8, 32), :, :] = y[:, :, 128:256]
            c_xd[t, pl.ds(base, 32), :, :] = y[:, :, 256:384]
            c_yu[t, pl.ds(base, 32), :, :] = y[:, :, 384:512]
            c_yd[t, pl.ds(base, 32), :, :] = y[:, :, 512:640]
            return carry

        lax.fori_loop(0, 2 * n_tiles, body, 0)

    def project(f_ref):
        def body(i, carry):
            found = []
            for u in range(8):
                ii = i * 8 + u
                w = f_ref[lists[SRC, ii], pl.ds(lists[ROW, ii], 8), :]
                w = jnp.where(low == (lists[UPPER, ii] == 0), w, 0.0)
                found.append(jnp.sum(tiles_ref[lists[ID, ii]] * w[None], axis=1))
            q = jnp.concatenate(found, axis=0)
            high = q.astype(BF16)
            rest = (q - high.astype(F32)).astype(BF16)
            weights[pl.ds(pl.multiple_of(i * 32, 32), 32), :] = jnp.dot(
                jnp.concatenate([high, rest], axis=1), ones_ref[...], preferred_element_type=F32
            )
            return carry

        lax.fori_loop(0, (count + 7) // 8, body, 0)

    def combine(f_ref, y_ref, older, t, coef):
        a, b = coef
        r = t * 8 + 8

        def body(xb, carry):
            for yb in range(8):
                src = xb * 8 + yb
                total = c_own[t, src] + c_xu[t, src] + c_xd[t, src + 8]
                if yb > 0:
                    total = total + c_yu[t, src - 1]
                if yb < 7:
                    total = total + c_yd[t, src + 1]
                for k in range(1, REACH + 1):
                    total = total + HALF[k] * (
                        f_ref[src, r + k : r + k + 8, :] + f_ref[src, r - k : r - k + 8, :]
                    )
                total = total + pot_ref[src, t * 8 : t * 8 + 8, :] * f_ref[src, r : r + 8, :]
                total = a * total
                if older is not None:
                    total = total - b * older(src)
                if t == 0:
                    total = jnp.where(jnp.logical_or(below, jnp.logical_not(low)), total, 0.0)
                if t == 2:
                    total = jnp.where(jnp.logical_or(above, low), total, 0.0)
                y_ref[src, r : r + 8, :] = total
            return carry

        lax.fori_loop(0, 8, body, 0)

    def spread(y_ref, a):
        def body(i, carry):
            w = weights[pl.ds(pl.multiple_of(i * 32, 32), 32), :]
            for u in range(8):
                ii = i * 8 + u
                atom, src = lists[ID, ii], lists[SRC, ii]
                t = zero8
                for p in range(4):
                    t = t + (strength[p, ii] * a) * w[u * 4 + p : u * 4 + p + 1, :] * tiles_ref[atom, p]
                rows = pl.ds(lists[ROW_L, ii], 8)
                on = jnp.logical_and(low, lists[ON_L, ii] > 0)
                y_ref[src, rows, :] = y_ref[src, rows, :] + jnp.where(on, t, 0.0)
                rows = pl.ds(lists[ROW_U, ii], 8)
                on = jnp.logical_and(jnp.logical_not(low), lists[ON_U, ii] > 0)
                y_ref[src, rows, :] = y_ref[src, rows, :] + jnp.where(on, t, 0.0)
            return carry

        lax.fori_loop(0, (count + 7) // 8, body, 0)

    products(ext, 0, 3)
    project(ext)
    for t in range(3):
        older = None if first else (lambda src, t=t: older_ref[src, t * 8 : t * 8 + 8, :])
        combine(ext, mid, older, t, coef1)
    spread(mid, coef1[0])
    products(mid, 1, 1)
    project(mid)
    combine(mid, new, lambda src: ext[src, 16:24, :], 1, coef2)
    spread(new, coef2[0])
    out_ref[...] = new[:, 16:24, :]
    if not last:
        mid_ref[...] = mid[:, 8:32, :]


def double_step(first, last, coef1, coef2, lists, strength, halo, own, older, pot, tiles, mats):
    smem = pl.BlockSpec(memory_space=pltpu.SMEM)
    vmem = pl.BlockSpec(memory_space=pltpu.VMEM)
    ins = [lists, strength, halo[0], own, halo[1]]
    if not first:
        ins += [older, pot]
    ins += [tiles, *mats]
    outs = [jax.ShapeDtypeStruct((64, 8, 128), F32)]
    if first:
        outs.append(jax.ShapeDtypeStruct((64, 24, 128), F32))
    if not last:
        outs.append(jax.ShapeDtypeStruct((64, 24, 128), F32))
    return pl.pallas_call(
        functools.partial(double_kernel, first, last, coef1, coef2),
        out_shape=tuple(outs),
        in_specs=[smem, smem] + [vmem] * (len(ins) - 2),
        out_specs=tuple([vmem] * len(outs)),
        scratch_shapes=[
            pltpu.VMEM((64, 40, 128), F32),
            pltpu.VMEM((64, 40, 128), F32),
            pltpu.VMEM((64, 40, 128), F32),
            pltpu.VMEM((3, 64, 8, 128), F32),
            pltpu.VMEM((3, 72, 8, 128), F32),
            pltpu.VMEM((3, 72, 8, 128), F32),
            pltpu.VMEM((3, 64, 8, 128), F32),
            pltpu.VMEM((3, 64, 8, 128), F32),
            pltpu.VMEM((256, 128), F32),
        ],
        compiler_params=VMEM,
    )(*ins)


def atom_lists(slab, proj_strength, atom_block, atom_offset):
    number = jnp.arange(64, dtype=jnp.int32)
    dz = atom_offset[:, 2] - 16 * slab
    near = jnp.logical_and(dz >= -15, dz <= 23)
    before = jnp.sum(
        jnp.logical_and(near[None, :], number[None, :] < number[:, None]).astype(jnp.int32), axis=1
    )
    pick = jnp.logical_and(near[None, :], before[None, :] == number[:, None])

    def listed(values, empty):
        return jnp.sum(jnp.where(pick, values[None, :], 0), axis=1) + jnp.where(
            jnp.any(pick, axis=1), 0, empty
        )

    at = listed(dz, 0)
    valid = jnp.any(pick, axis=1)
    source = listed(jnp.clip(atom_block, 0, 63), 0)
    upper = at > 8
    meta = jnp.zeros((64,), jnp.int32).at[0].set(jnp.sum(near.astype(jnp.int32)))
    meta = meta.at[1].set(slab).at[2].set(7 - slab)
    lists = jnp.stack(
        [
            listed(number, 0),
            source,
            jnp.where(upper, at - 8, at) + 16,
            upper.astype(jnp.int32),
            jnp.clip(at, -16, 16) + 16,
            jnp.logical_and(valid, at <= 15).astype(jnp.int32),
            jnp.clip(at - 8, -16, 16) + 16,
            jnp.logical_and(valid, at >= -7).astype(jnp.int32),
            meta,
        ]
    )
    strength = jnp.sum(jnp.where(pick[None], proj_strength.T[:, None, :], 0.0), axis=2)
    return lists, strength


def unpack_kernel(occ, in_ref, out_ref, density_ref):
    low = lanes_low((8, 128))
    density = jnp.zeros((64, 128), F32)
    for q in range(4):
        rows = []
        for s in range(8):
            a = in_ref[plane_index(2 * q, s)]
            b = in_ref[plane_index(2 * q + 1, s)]
            rows += [jnp.where(low, a, swap(b)), jnp.where(low, swap(a), b)]
        block = jnp.concatenate(rows, axis=0).T
        out_ref[q * 128 : (q + 1) * 128, :] = block
        for e in range(2):
            part = block[e * 64 : (e + 1) * 64, :]
            density = density + occ[2 * q + e] * part * part
    density_ref[...] = density


def unpack(occupations, slabs):
    smem = pl.BlockSpec(memory_space=pltpu.SMEM)
    vmem = pl.BlockSpec(memory_space=pltpu.VMEM)
    return pl.pallas_call(
        unpack_kernel,
        out_shape=(jax.ShapeDtypeStruct((512, 128), F32), jax.ShapeDtypeStruct((64, 128), F32)),
        in_specs=[smem, vmem],
        out_specs=(vmem, vmem),
        compiler_params=VMEM,
    )(occupations, slabs)


def neighbours_sum(v):
    z = jnp.pad(v[1:-1, 1:-1], ((0, 0), (0, 0), (1, 1)))
    total = v[2:, 1:-1] + v[:-2, 1:-1] + v[1:-1, 2:] + v[1:-1, :-2]
    return total + z[:, :, 2:] + z[:, :, :-2]


def restrict_mean(r):
    sx, sy, sz = r.shape
    r = r.reshape(sx // 2, 2, sy, sz).sum(axis=1)
    r = r.reshape(sx // 2, sy // 2, 2, sz).sum(axis=2)
    halve = np.zeros((sz, sz // 2), np.float32)
    halve[np.arange(sz), np.arange(sz) // 2] = 0.125
    return jnp.einsum("xyz,zw->xyw", r, halve, precision=lax.Precision.HIGHEST)


def prolong_copy(e):
    sx, sy, sz = e.shape
    double = np.zeros((sz, 2 * sz), np.float32)
    double[np.arange(2 * sz) // 2, np.arange(2 * sz)] = 1.0
    e = jnp.einsum("xyz,zw->xyw", e, double, precision=lax.Precision.HIGHEST)
    e = jnp.broadcast_to(e[:, None, :, None, :], (sx, 2, sy, 2, 2 * sz))
    return e.reshape(2 * sx, 2 * sy, 2 * sz)


def coarse_cycle(level, source):
    scale = 4.0**level
    diagonal = 6.0 / scale

    def operate(v):
        padded = jnp.pad(v, ((1, 1), (1, 1), (0, 0)))
        return (6.0 * v - neighbours_sum(padded)) / scale

    v = DAMPING * source / diagonal
    for _ in range((COARSE if level == LEVELS - 1 else PRE) - 1):
        v = v + DAMPING * (source - operate(v)) / diagonal
    if level < LEVELS - 1:
        v = v + prolong_copy(coarse_cycle(level + 1, restrict_mean(source - operate(v))))
        for _ in range(POST):
            v = v + DAMPING * (source - operate(v)) / diagonal
    return v


def exchange(value, axes, dim, width, order=None):
    order = order or list(range(8))
    up = [(order[i], order[i + 1]) for i in range(7)]
    down = [(j, i) for i, j in up]
    length = value.shape[dim]
    before = lax.ppermute(lax.slice_in_dim(value, length - width, length, axis=dim), axes, up)
    after = lax.ppermute(lax.slice_in_dim(value, 0, width, axis=dim), axes, down)
    return before, after


def hartree_of(density):
    gx, gyz = lax.axis_index(GX), lax.axis_index(GYZ)
    before, after = exchange(density, GX, 0, 3)
    f = jnp.concatenate([before, density, after], axis=0)
    before, after = exchange(f, GYZ, 1, 3)
    f = jnp.concatenate([before, f, after], axis=1)

    def inside(width):
        def along(index):
            cell = jnp.arange(8 + 2 * width) - width + 8 * index
            return jnp.logical_and(cell >= 0, cell < 64)

        return jnp.logical_and(along(gx)[:, None, None], along(gyz)[None, :, None])

    def sweep(v, source):
        centre = v[1:-1, 1:-1]
        return centre + (DAMPING / 6.0) * (source - (6.0 * centre - neighbours_sum(v)))

    v = (DAMPING / 6.0) * f
    v = jnp.where(inside(2), sweep(v, f[1:-1, 1:-1]), 0.0)
    inner = v[1:-1, 1:-1]
    residual = f[2:-2, 2:-2] - (6.0 * inner - neighbours_sum(v))
    coarse = restrict_mean(residual[1:-1, 1:-1])
    sent = jnp.broadcast_to(coarse.reshape(1, 8, 128), (64, 8, 128))
    got = lax.all_to_all(sent, PLANE, 0, 0, tiled=True)
    whole = got.reshape(8, 8, 4, 4, 64).transpose(0, 2, 1, 3, 4).reshape(32, 32, 64)
    error = jnp.pad(coarse_cycle(1, whole), ((1, 1), (1, 1), (0, 0)))
    error = lax.dynamic_slice(error, (4 * gx, 4 * gyz, 0), (6, 6, 64))
    v = v + prolong_copy(error)
    v = jnp.where(inside(1), sweep(v, f[2:-2, 2:-2]), 0.0)
    return sweep(v, f[3:-3, 3:-3])


def local(
    orbitals, local_potential, occupations, proj_values, proj_strength, atom_block, atom_offset
):
    core, xlo, ylo = (lax.axis_index(a) for a in GROUP)
    slab = 2 * (xlo * (3 - ylo) + (1 - xlo) * ylo) + core
    lists, strength = atom_lists(slab, proj_strength, atom_block, atom_offset)
    high, low = coupling()
    mats = (jnp.asarray(high), jnp.asarray(low), jnp.ones((256, 128), BF16))

    packed, tiles = pack(orbitals, local_potential, proj_values)
    own = lax.all_to_all(packed, PLANE, 0, 0, tiled=True)

    sigma = HALF_WIDTH / (0.0 - CENTER)
    tau = 2.0 / sigma
    coefs = [(sigma / HALF_WIDTH, 0.0)]
    for _ in range(DEGREE - 1):
        following = 1.0 / (tau - sigma)
        coefs.append((2.0 * following / HALF_WIDTH, sigma * following))
        sigma = following
    older = pot = None
    for k in range(0, DEGREE, 2):
        first, last = k == 0, k == DEGREE - 2
        halo = exchange(own, GROUP, 1, own.shape[1], SLAB_DEVICE)
        outs = list(
            double_step(
                first, last, coefs[k], coefs[k + 1], lists, strength, halo, own, older, pot, tiles, mats
            )
        )
        own = outs.pop(0)
        if first:
            pot = outs.pop(0)
        if not last:
            older = outs.pop(0)

    back = lax.all_to_all(own, PLANE, 0, 0, tiled=True)
    filtered, density = unpack(occupations, back)
    sent = jnp.broadcast_to(density[None], (8, 64, 128))
    density = jnp.sum(lax.all_to_all(sent, BAND, 0, 0, tiled=True), axis=0) / 64.0
    hartree = hartree_of(density.reshape(8, 8, 128))
    return filtered.reshape(8, 8, 8, 128), hartree


def solution(mesh):
    fine = Mesh(
        mesh.devices.reshape(8, 4, 2, 2, 2, 2), (BAND, "yhi", "core", "xhi", "xlo", "ylo")
    )
    bands, grid = P(BAND, GX, GYZ, None), P(GX, GYZ, None)
    return jax.shard_map(
        local,
        mesh=fine,
        in_specs=(bands, grid, P(BAND), P(), P(), P(), P()),
        out_specs=(bands, grid),
        check_vma=False,
    )
```

time: 1630 us -> 199 us (0.12); the launches traced: 1600 us -> 197 us
  starting transfers between devices: 806 us -> 64.1 us
  loops' own time: 332 us -> 0 us
  local copies, waits for them, and re-layouts: 317 us -> 7.76 us
  Pallas kernels: 0 us -> 36.9 us
  waiting for transfers between devices: 90.4 us -> 60.7 us
  blocking collectives: 36 us -> 18.3 us
    ppermute x92 -> x12, starting transfers between devices: 806 us -> 32.7 us  [the longest x6 20.2 us: exchange(): lax.ppermute(lax.slice_in_dim(value, 0, width, axis=dim), axes, down)]
    another operation x520 -> x0, loops' own time: 332 us -> none  [the longest x8 326 us: nonlocal_term(): lax.fori_loop(0, proj_values.shape[0], visit_atom, jnp.zeros_like(orbital))]
    dynamic_slice x512 -> x0, local copies, waits for them, and re-layouts: 301 us -> none  [visit_atom(): atom_block[atom_index] == my_block]
    ppermute x92 -> x12, waiting for transfers between devices: 90.4 us -> 21.5 us  [the longest x6 11.1 us: exchange(): lax.ppermute(lax.slice_in_dim(value, length - width, length, axis=dim), a...]
    all_to_all x0 -> x3, waiting for transfers between devices: none -> 39.3 us  [the longest x1 14.9 us: local(): own = lax.all_to_all(packed, PLANE, 0, 0, tiled=True)]
    pallas_call x0 -> x6, Pallas kernels: none -> 36.9 us  [the longest x4 31.6 us: double_step(): pl.pallas_call(functools.partial(double_kernel, first, last, coef1, coef2...]
    psum x1 -> x0, blocking collectives: 36 us -> none  [local(): density = lax.psum(density_part, 'band')]
    all_to_all x0 -> x3, starting transfers between devices: none -> 31.4 us  [the longest x1 10.7 us: local(): own = lax.all_to_all(packed, PLANE, 0, 0, tiled=True)]
  transfers between devices with their start and end apart: 92 -> 15, of which waited for: 38 -> 13; matrix products, arithmetic and copies ran while one was open for 19% -> 2% of each run, Pallas kernels for 0% -> 0%
where the time goes in v1:
time: 199 us; the launch traced here: 197 us
  starting transfers between devices  64.1 us (32%)
  waiting for transfers between devices  60.7 us (31%)
  Pallas kernels  36.9 us (19%)
  blocking collectives  18.3 us (9%)
  local copies, waits for them, and re-layouts  7.76 us (4%)
  other arithmetic  6.21 us (3%)
    pallas_call x4, Pallas kernels, double_step(): pl.pallas_call(functools.partial(double_kernel, first, last, coef1, coef2...  31.6 us
    ppermute x6, starting transfers between devices, exchange(): lax.ppermute(lax.slice_in_dim(value, 0, width, axis=dim), axes, down)  20.2 us
    all_to_all x1, blocking collectives, local(): back = lax.all_to_all(own, PLANE, 0, 0, tiled=True)  18.3 us
    all_to_all x1, waiting for transfers between devices, local(): own = lax.all_to_all(packed, PLANE, 0, 0, tiled=True)  14.9 us
    all_to_all x1, waiting for transfers between devices, local(): lax.all_to_all(sent, BAND, 0, 0, tiled=True)  12.5 us
    ppermute x6, starting transfers between devices, exchange(): lax.ppermute(lax.slice_in_dim(value, length - width, length, axis=dim), a...  12.5 us
    all_to_all x1, waiting for transfers between devices, hartree_of(): got = lax.all_to_all(sent, PLANE, 0, 0, tiled=True)  11.8 us
    ppermute x6, waiting for transfers between devices, exchange(): lax.ppermute(lax.slice_in_dim(value, length - width, length, axis=dim), a...  11.1 us
  transfers between devices with their start and end apart: 15, of which 13 were waited for; matrix products, arithmetic and copies ran while one was open for 2% of the time, Pallas kernels for 0%

profile of v1, /device:TPU:6, one launch (start us, length us, event | category | flops | bytes accessed | tf_op | source)
XLA Modules:
  0.0 196.5 jit_solution(16902606163933886602)
XLA Ops:
  2.0 3.8 %shard_map.167 = (f32[64,16,128]{2,1,0:T(8,128)}, f32[64,4,8,128]{3,2,1,0:T(8,128)S(1)}) custom-call(f32[512,128]{1,0:T(8,128)S(1)} %bitcast.65, f32[64,128]{1,0:T(8,128)S(1)} %bitcast.66, f32[256,512]{1,0:T(8,128)S(1)} %reshape.359.proj_ref, bf16[512,128]{1,0:T(8,128)(2,1)S(1)} %copy-done.3), custom_call_target="tpu_custom_call" | custom-call | tf_op jit(solution)/shard_map/pallas_call | solution.py:117
  5.8 10.7 %all-to-all-start = ((f32[64,16,128]{2,1,0:T(8,128)}), f32[64,16,128]{2,1,0:T(8,128)S(1)}, u32[]{:S(2)}, u32[]{:S(2)}) async-start(f32[64,16,128]{2,1,0:T(8,128)} %get-tuple-element.49), calls=%async_computation | async-start | bytes 1048576 | tf_op jit(solution)/shard_map/all_to_all | solution.py:469
  19.2 14.9 %all-to-all-done.own_ref = f32[64,16,128]{2,1,0:T(8,128)S(1)} async-done(((f32[64,16,128]{2,1,0:T(8,128)}), f32[64,16,128]{2,1,0:T(8,128)S(1)}, u32[]{:S(2)}, u32[]{:S(2)}) %all-to-all-start) | async-done | bytes 524320 | tf_op jit(solution)/shard_map/all_to_all | solution.py:469
  34.1 2.1 %collective-permute-start = (f32[64,16,128]{2,1,0:T(8,128)S(1)}, f32[64,16,128]{2,1,0:T(8,128)S(1)}, u32[]{:S(2)}, u32[]{:S(2)}) collective-permute-start(f32[64,16,128]{2,1,0:T(8,128)S(1)} %all-to-all-done.own_ref), channel_id=1, source_target_pairs={{0,8},{8,1},{1,9},{9,3},{3,11},{11,2},{2,10},{4,12},{12,5},{5,13},... | collective-permute-start | bytes 1572872 | tf_op jit(solution)/shard_map/ppermute | solution.py:421
  36.2 3.5 %collective-permute-start.1 = (f32[64,16,128]{2,1,0:T(8,128)S(1)}, f32[64,16,128]{2,1,0:T(8,128)S(1)}, u32[]{:S(2)}, u32[]{:S(2)}) collective-permute-start(f32[64,16,128]{2,1,0:T(8,128)S(1)} %all-to-all-done.own_ref), channel_id=1, source_target_pairs={{8,0},{1,8},{9,1},{3,9},{11,3},{2,11},{10,2},{12,4},{5,12},{13,5},... | collective-permute-start | bytes 1572872 | tf_op jit(solution)/shard_map/ppermute | solution.py:422
  39.9 4.7 %collective-permute-done.prev_ref = f32[64,16,128]{2,1,0:T(8,128)S(1)} collective-permute-done((f32[64,16,128]{2,1,0:T(8,128)S(1)}, f32[64,16,128]{2,1,0:T(8,128)S(1)}, u32[]{:S(2)}, u32[]{:S(2)}) %collective-permute-start) | collective-permute-done | bytes 524320 | tf_op jit(solution)/shard_map/ppermute | solution.py:421
  46.4 7.9 %shard_map.168 = (f32[64,8,128]{2,1,0:T(8,128)S(1)}, f32[64,24,128]{2,1,0:T(8,128)S(1)}, f32[64,24,128]{2,1,0:T(8,128)S(1)}) custom-call(s32[9,64]{1,0:T(8,128)S(1)} %stack.27.lists, f32[4,64]{1,0:T(4,128)S(1)} %select_reduce_fusion.strength, f32[64,16,128]{2,1,0:T(8,128)S(1)} %collective-permute-done.prev_ref, f32[64,16,128]{2,1,0:T(8,128)S(1)} %all-to-all-done.own_ref, ...), custom_call_target="tpu_custom_call" | custom-call | tf_op jit(solution)/shard_map/pallas_call | solution.py:288
  56.2 3.8 %collective-permute-start.3 = (f32[64,8,128]{2,1,0:T(8,128)S(1)}, f32[64,8,128]{2,1,0:T(8,128)S(1)}, u32[]{:S(2)}, u32[]{:S(2)}) collective-permute-start(f32[64,8,128]{2,1,0:T(8,128)S(1)} %get-tuple-element.51.own_ref), channel_id=1, source_target_pairs={{8,0},{1,8},{9,1},{3,9},{11,3},{2,11},{10,2},{12,4},{5,12},{13,5},... | collective-permute-start | bytes 786440 | tf_op jit(solution)/shard_map/ppermute | solution.py:422
  60.1 2.1 %collective-permute-done.2.prev_ref = f32[64,8,128]{2,1,0:T(8,128)S(1)} collective-permute-done((f32[64,8,128]{2,1,0:T(8,128)S(1)}, f32[64,8,128]{2,1,0:T(8,128)S(1)}, u32[]{:S(2)}, u32[]{:S(2)}) %collective-permute-start.2) | collective-permute-done | bytes 262176 | tf_op jit(solution)/shard_map/ppermute | solution.py:421
  63.9 7.9 %shard_map.169 = (f32[64,8,128]{2,1,0:T(8,128)S(1)}, f32[64,24,128]{2,1,0:T(8,128)S(1)}) custom-call(s32[9,64]{1,0:T(8,128)S(1)} %stack.27.lists, f32[4,64]{1,0:T(4,128)S(1)} %select_reduce_fusion.strength, f32[64,8,128]{2,1,0:T(8,128)S(1)} %collective-permute-done.2.prev_ref, f32[64,8,128]{2,1,0:T(8,128)S(1)} %get-tuple-element.51.own_ref, ...), custom_call_target="tpu_custom_call" | custom-call | tf_op jit(solution)/shard_map/pallas_call | solution.py:288
  73.8 3.8 %collective-permute-start.5 = (f32[64,8,128]{2,1,0:T(8,128)S(1)}, f32[64,8,128]{2,1,0:T(8,128)S(1)}, u32[]{:S(2)}, u32[]{:S(2)}) collective-permute-start(f32[64,8,128]{2,1,0:T(8,128)S(1)} %get-tuple-element.54.own_ref), channel_id=1, source_target_pairs={{8,0},{1,8},{9,1},{3,9},{11,3},{2,11},{10,2},{12,4},{5,12},{13,5},... | collective-permute-start | bytes 786440 | tf_op jit(solution)/shard_map/ppermute | solution.py:422
  77.6 2.1 %collective-permute-done.4.prev_ref = f32[64,8,128]{2,1,0:T(8,128)S(1)} collective-permute-done((f32[64,8,128]{2,1,0:T(8,128)S(1)}, f32[64,8,128]{2,1,0:T(8,128)S(1)}, u32[]{:S(2)}, u32[]{:S(2)}) %collective-permute-start.4) | collective-permute-done | bytes 262176 | tf_op jit(solution)/shard_map/ppermute | solution.py:421
  81.5 7.9 %shard_map.170 = (f32[64,8,128]{2,1,0:T(8,128)S(1)}, f32[64,24,128]{2,1,0:T(8,128)S(1)}) custom-call(s32[9,64]{1,0:T(8,128)S(1)} %stack.27.lists, f32[4,64]{1,0:T(4,128)S(1)} %select_reduce_fusion.strength, f32[64,8,128]{2,1,0:T(8,128)S(1)} %collective-permute-done.4.prev_ref, f32[64,8,128]{2,1,0:T(8,128)S(1)} %get-tuple-element.54.own_ref, ...), custom_call_target="tpu_custom_call" | custom-call | tf_op jit(solution)/shard_map/pallas_call | solution.py:288
  91.3 3.8 %collective-permute-start.7 = (f32[64,8,128]{2,1,0:T(8,128)S(1)}, f32[64,8,128]{2,1,0:T(8,128)S(1)}, u32[]{:S(2)}, u32[]{:S(2)}) collective-permute-start(f32[64,8,128]{2,1,0:T(8,128)S(1)} %get-tuple-element.56.own_ref), channel_id=1, source_target_pairs={{8,0},{1,8},{9,1},{3,9},{11,3},{2,11},{10,2},{12,4},{5,12},{13,5},... | collective-permute-start | bytes 786440 | tf_op jit(solution)/shard_map/ppermute | solution.py:422
  95.1 2.1 %collective-permute-done.6.prev_ref = f32[64,8,128]{2,1,0:T(8,128)S(1)} collective-permute-done((f32[64,8,128]{2,1,0:T(8,128)S(1)}, f32[64,8,128]{2,1,0:T(8,128)S(1)}, u32[]{:S(2)}, u32[]{:S(2)}) %collective-permute-start.6) | collective-permute-done | bytes 262176 | tf_op jit(solution)/shard_map/ppermute | solution.py:421
  99.0 7.8 %shard_map.171 = f32[64,8,128]{2,1,0:T(8,128)S(1)} custom-call(s32[9,64]{1,0:T(8,128)S(1)} %stack.27.lists, f32[4,64]{1,0:T(4,128)S(1)} %select_reduce_fusion.strength, f32[64,8,128]{2,1,0:T(8,128)S(1)} %collective-permute-done.6.prev_ref, f32[64,8,128]{2,1,0:T(8,128)S(1)} %get-tuple-element.56.own_ref, f32[64,8,128]{2,1,0:T(8,128)S(1)} %collective-permute-done.7.next_ref, ...), custom_call_target="tpu_custom_call" | custom-call | tf_op jit(solution)/shard_map/pallas_call | solution.py:288
  106.8 18.3 %all_to_all.20.in_ref = f32[64,8,128]{2,1,0:T(8,128)S(1)} all-to-all(f32[64,8,128]{2,1,0:T(8,128)S(1)} %shard_map.171), channel_id=1, replica_groups=mesh['z'=8,'yhi'=4,'core'=2,'xhi'=2,'xlo'=2,'ylo'=2] {'yhi','core','xhi'..., dimensions={0} | all-to-all | bytes 524288 | tf_op jit(solution)/shard_map/all_to_all | solution.py:493
  127.3 10.3 %all-to-all-start.2 = ((f32[8,64,128]{2,1,0:T(8,128)}), f32[8,64,128]{2,1,0:T(8,128)S(1)}, u32[]{:S(2)}, u32[]{:S(2)}) async-start(f32[8,64,128]{2,1,0:T(8,128)} %broadcast_in_dim.136), calls=%async_computation.2 | async-start | bytes 524288 | tf_op jit(solution)/shard_map/all_to_all | solution.py:496
  137.7 12.5 %all-to-all-done.2 = f32[8,64,128]{2,1,0:T(8,128)S(1)} async-done(((f32[8,64,128]{2,1,0:T(8,128)}), f32[8,64,128]{2,1,0:T(8,128)S(1)}, u32[]{:S(2)}, u32[]{:S(2)}) %all-to-all-start.2) | async-done | bytes 262176 | tf_op jit(solution)/shard_map/all_to_all | solution.py:496
  150.2 1.9 collective-permute-start.8
  155.3 2.7 %collective-permute-start.10 = (f32[14,3,128]{2,1,0:T(4,128)S(1)}, f32[14,3,128]{2,1,0:T(4,128)S(1)}, u32[]{:S(2)}, u32[]{:S(2)}) collective-permute-start(f32[14,3,128]{2,1,0:T(4,128)S(1)} %get-tuple-element.73), channel_id=1, source_target_pairs={{0,1},{1,2},{2,3},{3,4},{4,5},{5,6},{6,7},{8,9},{9,10},{10,11},{11... | collective-permute-start | bytes 64520 | tf_op jit(solution)/shard_map/ppermute | solution.py:421
  158.0 4.1 %collective-permute-start.11 = (f32[14,3,128]{2,1,0:T(4,128)S(1)}, f32[14,3,128]{2,1,0:T(4,128)S(1)}, u32[]{:S(2)}, u32[]{:S(2)}) collective-permute-start(f32[14,3,128]{2,1,0:T(4,128)S(1)} %get-tuple-element.74), channel_id=1, source_target_pairs={{1,0},{2,1},{3,2},{4,3},{5,4},{6,5},{7,6},{9,8},{10,9},{11,10},{12... | collective-permute-start | bytes 64520 | tf_op jit(solution)/shard_map/ppermute | solution.py:422
  165.9 10.3 %all-to-all-start.3 = ((f32[64,8,128]{2,1,0:T(8,128)}), f32[64,8,128]{2,1,0:T(8,128)S(1)}, u32[]{:S(2)}, u32[]{:S(2)}) async-start(f32[64,8,128]{2,1,0:T(8,128)} %broadcast_in_dim.139), calls=%async_computation.3 | async-start | bytes 524288 | tf_op jit(solution)/shard_map/all_to_all | solution.py:450
  176.3 11.8 %all-to-all-done.3 = f32[64,8,128]{2,1,0:T(8,128)S(1)} async-done(((f32[64,8,128]{2,1,0:T(8,128)}), f32[64,8,128]{2,1,0:T(8,128)S(1)}, u32[]{:S(2)}, u32[]{:S(2)}) %all-to-all-start.3) | async-done | bytes 262176 | tf_op jit(solution)/shard_map/all_to_all | solution.py:450
  (106 shorter events, 34.2 us)
Async XLA Ops:
  0.6 1.3 copy-start.3
  0.6 1.3 copy-start.2
  0.7 1.3 copy-start.4
  5.8 10.8 %copy-start.11 = (s32[64]{0:T(128)S(1)}, s32[64]{0:T(128)}, u32[]{:S(2)}) copy-start(s32[64]{0:T(128)} %param.27) | copy-start | bytes 772
  5.8 34.0 %copy-start.10 = (f32[64,4]{0,1:T(4,128)S(1)}, f32[64,4]{0,1:T(4,128)}, u32[]{:S(2)}) copy-start(f32[64,4]{0,1:T(4,128)} %param.26) | copy-start | bytes 3076
  5.8 40.6 %copy-start = (bf16[256,640]{1,0:T(8,128)(2,1)S(1)}, bf16[256,640]{1,0:T(8,128)(2,1)}, u32[]{:S(2)}) copy-start(bf16[256,640]{1,0:T(8,128)(2,1)} %constant.228.clone.refs_1_.refs_3_) | copy-start | bytes 983044
  5.8 28.3 %all-to-all-start = ((f32[64,16,128]{2,1,0:T(8,128)}), f32[64,16,128]{2,1,0:T(8,128)S(1)}, u32[]{:S(2)}, u32[]{:S(2)}) async-start(f32[64,16,128]{2,1,0:T(8,128)} %get-tuple-element.49), calls=%async_computation | async-start | bytes 1048576 | tf_op jit(solution)/shard_map/all_to_all | solution.py:469
  16.5 29.9 %copy-start.1 = (bf16[128,640]{1,0:T(8,128)(2,1)S(1)}, bf16[128,640]{1,0:T(8,128)(2,1)}, u32[]{:S(2)}) copy-start(bf16[128,640]{1,0:T(8,128)(2,1)} %constant.229.clone.refs_2_.refs_4_) | copy-start | bytes 491524
  34.1 10.5 %collective-permute-start = (f32[64,16,128]{2,1,0:T(8,128)S(1)}, f32[64,16,128]{2,1,0:T(8,128)S(1)}, u32[]{:S(2)}, u32[]{:S(2)}) collective-permute-start(f32[64,16,128]{2,1,0:T(8,128)S(1)} %all-to-all-done.own_ref), channel_id=1, source_target_pairs={{0,8},{8,1},{1,9},{9,3},{3,11},{11,2},{2,10},{4,12},{12,5},{5,13},... | collective-permute-start | bytes 1572872 | tf_op jit(solution)/shard_map/ppermute | solution.py:421
  36.2 10.2 %collective-permute-start.1 = (f32[64,16,128]{2,1,0:T(8,128)S(1)}, f32[64,16,128]{2,1,0:T(8,128)S(1)}, u32[]{:S(2)}, u32[]{:S(2)}) collective-permute-start(f32[64,16,128]{2,1,0:T(8,128)S(1)} %all-to-all-done.own_ref), channel_id=1, source_target_pairs={{8,0},{1,8},{9,1},{3,9},{11,3},{2,11},{10,2},{12,4},{5,12},{13,5},... | collective-permute-start | bytes 1572872 | tf_op jit(solution)/shard_map/ppermute | solution.py:422
  54.3 7.9 %collective-permute-start.2 = (f32[64,8,128]{2,1,0:T(8,128)S(1)}, f32[64,8,128]{2,1,0:T(8,128)S(1)}, u32[]{:S(2)}, u32[]{:S(2)}) collective-permute-start(f32[64,8,128]{2,1,0:T(8,128)S(1)} %get-tuple-element.51.own_ref), channel_id=1, source_target_pairs={{0,8},{8,1},{1,9},{9,3},{3,11},{11,2},{2,10},{4,12},{12,5},{5,13},... | collective-permute-start | bytes 786440 | tf_op jit(solution)/shard_map/ppermute | solution.py:421
  56.2 7.7 %collective-permute-start.3 = (f32[64,8,128]{2,1,0:T(8,128)S(1)}, f32[64,8,128]{2,1,0:T(8,128)S(1)}, u32[]{:S(2)}, u32[]{:S(2)}) collective-permute-start(f32[64,8,128]{2,1,0:T(8,128)S(1)} %get-tuple-element.51.own_ref), channel_id=1, source_target_pairs={{8,0},{1,8},{9,1},{3,9},{11,3},{2,11},{10,2},{12,4},{5,12},{13,5},... | collective-permute-start | bytes 786440 | tf_op jit(solution)/shard_map/ppermute | solution.py:422
  71.8 7.9 %collective-permute-start.4 = (f32[64,8,128]{2,1,0:T(8,128)S(1)}, f32[64,8,128]{2,1,0:T(8,128)S(1)}, u32[]{:S(2)}, u32[]{:S(2)}) collective-permute-start(f32[64,8,128]{2,1,0:T(8,128)S(1)} %get-tuple-element.54.own_ref), channel_id=1, source_target_pairs={{0,8},{8,1},{1,9},{9,3},{3,11},{11,2},{2,10},{4,12},{12,5},{5,13},... | collective-permute-start | bytes 786440 | tf_op jit(solution)/shard_map/ppermute | solution.py:421
  73.8 7.7 %collective-permute-start.5 = (f32[64,8,128]{2,1,0:T(8,128)S(1)}, f32[64,8,128]{2,1,0:T(8,128)S(1)}, u32[]{:S(2)}, u32[]{:S(2)}) collective-permute-start(f32[64,8,128]{2,1,0:T(8,128)S(1)} %get-tuple-element.54.own_ref), channel_id=1, source_target_pairs={{8,0},{1,8},{9,1},{3,9},{11,3},{2,11},{10,2},{12,4},{5,12},{13,5},... | collective-permute-start | bytes 786440 | tf_op jit(solution)/shard_map/ppermute | solution.py:422
  89.4 7.9 %collective-permute-start.6 = (f32[64,8,128]{2,1,0:T(8,128)S(1)}, f32[64,8,128]{2,1,0:T(8,128)S(1)}, u32[]{:S(2)}, u32[]{:S(2)}) collective-permute-start(f32[64,8,128]{2,1,0:T(8,128)S(1)} %get-tuple-element.56.own_ref), channel_id=1, source_target_pairs={{0,8},{8,1},{1,9},{9,3},{3,11},{11,2},{2,10},{4,12},{12,5},{5,13},... | collective-permute-start | bytes 786440 | tf_op jit(solution)/shard_map/ppermute | solution.py:421
  91.3 7.7 %collective-permute-start.7 = (f32[64,8,128]{2,1,0:T(8,128)S(1)}, f32[64,8,128]{2,1,0:T(8,128)S(1)}, u32[]{:S(2)}, u32[]{:S(2)}) collective-permute-start(f32[64,8,128]{2,1,0:T(8,128)S(1)} %get-tuple-element.56.own_ref), channel_id=1, source_target_pairs={{8,0},{1,8},{9,1},{3,9},{11,3},{2,11},{10,2},{12,4},{5,12},{13,5},... | collective-permute-start | bytes 786440 | tf_op jit(solution)/shard_map/ppermute | solution.py:422
  106.8 18.3 %copy-start.5 = (f32[8]{0:T(128)S(1)}, f32[8]{0:T(128)}, u32[]{:S(2)}) copy-start(f32[8]{0:T(128)} %occ.1) | copy-start | bytes 100
  127.3 22.9 %all-to-all-start.2 = ((f32[8,64,128]{2,1,0:T(8,128)}), f32[8,64,128]{2,1,0:T(8,128)S(1)}, u32[]{:S(2)}, u32[]{:S(2)}) async-start(f32[8,64,128]{2,1,0:T(8,128)} %broadcast_in_dim.136), calls=%async_computation.2 | async-start | bytes 524288 | tf_op jit(solution)/shard_map/all_to_all | solution.py:496
  150.2 3.3 %collective-permute-start.8 = (f32[3,8,128]{2,1,0:T(8,128)S(1)}, f32[3,8,128]{2,1,0:T(8,128)S(1)}, u32[]{:S(2)}, u32[]{:S(2)}) collective-permute-start(f32[3,8,128]{2,1,0:T(8,128)S(1)} %get-tuple-element.75), channel_id=1, source_target_pairs={{0,8},{8,16},{16,24},{24,32},{32,40},{40,48},{48,56},{1,9},{9,17},... | collective-permute-start | bytes 36872 | tf_op jit(solution)/shard_map/ppermute | solution.py:421
  152.2 3.1 %collective-permute-start.9 = (f32[3,8,128]{2,1,0:T(8,128)S(1)}, f32[3,8,128]{2,1,0:T(8,128)S(1)}, u32[]{:S(2)}, u32[]{:S(2)}) collective-permute-start(f32[3,8,128]{2,1,0:T(8,128)S(1)} %get-tuple-element.76), channel_id=1, source_target_pairs={{8,0},{16,8},{24,16},{32,24},{40,32},{48,40},{56,48},{9,1},{17,9},... | collective-permute-start | bytes 36872 | tf_op jit(solution)/shard_map/ppermute | solution.py:422
  155.3 6.8 %collective-permute-start.10 = (f32[14,3,128]{2,1,0:T(4,128)S(1)}, f32[14,3,128]{2,1,0:T(4,128)S(1)}, u32[]{:S(2)}, u32[]{:S(2)}) collective-permute-start(f32[14,3,128]{2,1,0:T(4,128)S(1)} %get-tuple-element.73), channel_id=1, source_target_pairs={{0,1},{1,2},{2,3},{3,4},{4,5},{5,6},{6,7},{8,9},{9,10},{10,11},{11... | collective-permute-start | bytes 64520 | tf_op jit(solution)/shard_map/ppermute | solution.py:421
  158.0 5.8 %collective-permute-start.11 = (f32[14,3,128]{2,1,0:T(4,128)S(1)}, f32[14,3,128]{2,1,0:T(4,128)S(1)}, u32[]{:S(2)}, u32[]{:S(2)}) collective-permute-start(f32[14,3,128]{2,1,0:T(4,128)S(1)} %get-tuple-element.74), channel_id=1, source_target_pairs={{1,0},{2,1},{3,2},{4,3},{5,4},{6,5},{7,6},{9,8},{10,9},{11,10},{12... | collective-permute-start | bytes 64520 | tf_op jit(solution)/shard_map/ppermute | solution.py:422
  164.1 0.8 copy-start.7
  165.9 22.2 %all-to-all-start.3 = ((f32[64,8,128]{2,1,0:T(8,128)}), f32[64,8,128]{2,1,0:T(8,128)S(1)}, u32[]{:S(2)}, u32[]{:S(2)}) async-start(f32[64,8,128]{2,1,0:T(8,128)} %broadcast_in_dim.139), calls=%async_computation.3 | async-start | bytes 524288 | tf_op jit(solution)/shard_map/all_to_all | solution.py:450
  (5 other events, 3.6 us)

commit v2 on v1

--- a/solution.py
+++ b/solution.py
@@ -10,8 +10,6 @@
 from jax.sharding import PartitionSpec as P
 
 DEGREE = 8
-LEVELS = 4
-PRE = 2
 POST = 2
 COARSE = 4
 STENCIL = (
@@ -46,7 +44,7 @@
     return yhi * 16 + (slab % 2) * 8 + xhi * 4 + xlo * 2 + ylo
 
 
-def coupling():
+def coupling(weights):
     own, xu, xd, yu, yd = (np.zeros((128, 128)) for _ in range(5))
     for zh in range(2):
         for xi in range(8):
@@ -54,15 +52,20 @@
                 i = zh * 64 + xi * 8 + yi
                 for o in range(8):
                     for m, k in ((own, abs(o - xi)), (xu, o + 8 - xi), (xd, xi + 8 - o)):
-                        if 1 <= k <= REACH:
-                            m[i, zh * 64 + o * 8 + yi] += HALF[k]
+                        if 1 <= k < len(weights):
+                            m[i, zh * 64 + o * 8 + yi] += weights[k]
                     for m, k in ((own, abs(o - yi)), (yu, o + 8 - yi), (yd, yi + 8 - o)):
-                        if 1 <= k <= REACH:
-                            m[i, zh * 64 + xi * 8 + o] += HALF[k]
+                        if 1 <= k < len(weights):
+                            m[i, zh * 64 + xi * 8 + o] += weights[k]
     whole = np.concatenate([own, xu, xd, yu, yd], axis=1).astype(np.float32)
     high = whole.astype(jnp.bfloat16)
     low = (whole - high.astype(np.float32)).astype(jnp.bfloat16)
     return np.concatenate([high, high], axis=0), low
+
+
+def halves(x, axis):
+    high = x.astype(BF16)
+    return jnp.concatenate([high, (x - high.astype(F32)).astype(BF16)], axis=axis)
 
 
 def lanes_low(shape):
@@ -342,75 +345,394 @@
     return lists, strength
 
 
-def unpack_kernel(occ, in_ref, out_ref, density_ref):
+def unpack_kernel(in_ref, out_ref, hartree_ref):
     low = lanes_low((8, 128))
-    density = jnp.zeros((64, 128), F32)
+
+    def block(pairs):
+        rows = []
+        for a, b in pairs:
+            rows += [jnp.where(low, a, swap(b)), jnp.where(low, swap(a), b)]
+        return jnp.concatenate(rows, axis=0).T
+
     for q in range(4):
-        rows = []
-        for s in range(8):
-            a = in_ref[plane_index(2 * q, s)]
-            b = in_ref[plane_index(2 * q + 1, s)]
-            rows += [jnp.where(low, a, swap(b)), jnp.where(low, swap(a), b)]
-        block = jnp.concatenate(rows, axis=0).T
-        out_ref[q * 128 : (q + 1) * 128, :] = block
-        for e in range(2):
-            part = block[e * 64 : (e + 1) * 64, :]
-            density = density + occ[2 * q + e] * part * part
-    density_ref[...] = density
-
-
-def unpack(occupations, slabs):
+        out_ref[q * 128 : (q + 1) * 128, :] = block(
+            [
+                (in_ref[plane_index(2 * q, s), 0:8, :], in_ref[plane_index(2 * q + 1, s), 0:8, :])
+                for s in range(8)
+            ]
+        )
+    pairs = []
+    for s in range(8):
+        total = in_ref[plane_index(0, s), 8:16, :]
+        for b in range(1, 8):
+            total = total + in_ref[plane_index(b, s), 8:16, :]
+        pairs.append((total, total))
+    part = block(pairs)[0:64, :]
+    for e in range(8):
+        hartree_ref[e] = part
+
+
+def unpack(slabs):
+    return pl.pallas_call(
+        unpack_kernel,
+        out_shape=(
+            jax.ShapeDtypeStruct((512, 128), F32),
+            jax.ShapeDtypeStruct((8, 64, 128), F32),
+        ),
+        compiler_params=VMEM,
+    )(slabs)
+
+
+OMEGA = DAMPING / 6.0
+
+
+def cell_index(shape):
+    return np.indices(shape).reshape(len(shape), -1)
+
+
+def placing(rows, columns, weight):
+    same = np.all(rows[:, :, None] == columns[:, None, :], axis=0)
+    return (weight * same).astype(jnp.bfloat16)
+
+
+def level_matrices():
+    yb, zh, x, y = cell_index((8, 2, 8, 8))
+    fine = np.stack([zh, x // 2, yb * 4 + y // 2])
+    coarse = np.stack(cell_index((2, 4, 32)))
+    down0 = placing(fine, coarse, 0.5)
+    up0 = placing(np.stack(cell_index((4, 32))), np.stack([x // 2, yb * 4 + y // 2]), 1.0)
+    x, y = cell_index((16, 32))
+    fine, coarse = np.stack([x // 2, y // 2]), np.stack(cell_index((8, 16)))
+    down1, up1 = placing(fine, coarse, 0.5), placing(coarse, fine, 1.0)
+    x, y = cell_index((16, 16))
+    fine, coarse = np.stack([x // 2, y // 2]), np.stack(cell_index((16, 8)))
+    down2, up2 = placing(fine, coarse, 0.5), placing(coarse, fine, 1.0)
+
+    def beside(nx, ny, used):
+        x, y = cell_index((nx, ny))
+        dx, dy = x[None, :] - x[:, None], y[None, :] - y[:, None]
+        live = np.logical_and(x[None, :] < used, x[:, None] < used)
+        own = np.logical_and(np.abs(dx) + np.abs(dy) == 1, live)
+        to_next = np.logical_and(dx == 1 - nx, dy == 0)
+        to_last = np.logical_and(dx == nx - 1, dy == 0)
+        return [m.astype(jnp.bfloat16) for m in (own, to_next, to_last)]
+
+    def twice(m):
+        return np.concatenate([m, m], axis=0)
+
+    near1 = twice(np.concatenate(beside(4, 32, 4), axis=1))
+    near2 = twice(np.concatenate(beside(8, 16, 8), axis=1))
+    near3 = twice(beside(16, 8, 8)[0])
+    return down0, twice(up0), down1, twice(up1), down2, twice(up2), near1, near2, near3
+
+
+def xy_products(ref, r, mat_ref, couplings, t):
+    c_own, c_xu, c_xd, c_yu, c_yd = couplings
+    for base in (0, 32):
+        x = ref[base : base + 32, r : r + 8, :].reshape(256, 128)
+        y = jnp.dot(halves(x, 1), mat_ref[...], preferred_element_type=F32).reshape(32, 8, 640)
+        c_own[t, base : base + 32, :, :] = y[:, :, 0:128]
+        c_xu[t, base + 8 : base + 40, :, :] = y[:, :, 128:256]
+        c_xd[t, base : base + 32, :, :] = y[:, :, 256:384]
+        c_yu[t, base : base + 32, :, :] = y[:, :, 384:512]
+        c_yd[t, base : base + 32, :, :] = y[:, :, 512:640]
+
+
+def xy_sum(couplings, t, xb, yb):
+    c_own, c_xu, c_xd, c_yu, c_yd = couplings
+    src = xb * 8 + yb
+    total = c_own[t, src] + c_xu[t, src] + c_xd[t, src + 8]
+    if yb > 0:
+        total = total + c_yu[t, src - 1]
+    if yb < 7:
+        total = total + c_yd[t, src + 1]
+    return total
+
+
+def clear_borders(couplings, tiles):
+    zero = jnp.zeros((8, 8, 128), F32)
+    for t in range(tiles):
+        couplings[1][t, 0:8] = zero
+        couplings[2][t, 64:72] = zero
+
+
+COUPLINGS = [
+    pltpu.VMEM((2, n, 8, 128), F32) for n in (64, 72, 72, 64, 64)
+]
+
+
+def inside_slab_range(slab, r):
+    z = (
+        lax.broadcasted_iota(jnp.int32, (8, 128), 0)
+        + jnp.where(lanes_low((8, 128)), 0, 8)
+        + (16 * slab + (r - 16))
+    )
+    return jnp.logical_and(z >= 0, z < 128)
+
+
+def relax(ref, out_ref, rows, mat_ref, couplings, update):
+    for t, r in enumerate(rows):
+        xy_products(ref, r, mat_ref, couplings, t)
+    for t, r in enumerate(rows):
+
+        def body(xb, carry, t=t, r=r):
+            for yb in range(8):
+                src = xb * 8 + yb
+                near = xy_sum(couplings, t, xb, yb)
+                near = near + ref[src, r - 1 : r + 7, :] + ref[src, r + 1 : r + 9, :]
+                out_ref[src, r : r + 8, :] = update(src, r, ref[src, r : r + 8, :], near)
+            return carry
+
+        lax.fori_loop(0, 8, body, 0)
+
+
+def source_kernel(scalars, occ, own_ref, mat_ref, down_ref, f_ref, sent_ref, v, w, r0, *couplings):
+    low = lanes_low((8, 128))
+    slab, occupation = scalars[0], occ[scalars[1]] / 64.0
+    zero = jnp.zeros((8, 128), F32)
+
+    def fill(i, carry):
+        for u in range(16):
+            src = i * 16 + u
+            y = own_ref[src]
+            o = occupation * y * y
+            f_ref[src] = o
+            o = OMEGA * o
+            v[src, 0:8, :] = zero
+            v[src, 8:16, :] = swap(jnp.where(low, o, 0.0))
+            v[src, 16:24, :] = o
+            v[src, 24:32, :] = swap(jnp.where(low, 0.0, o))
+            v[src, 32:40, :] = zero
+            w[src, 8:16, :] = zero
+            w[src, 24:32, :] = zero
+        return carry
+
+    lax.fori_loop(0, 4, fill, 0)
+    clear_borders(couplings, 2)
+    keep = {r: inside_slab_range(slab, r) for r in (13, 19)}
+    relax(
+        v,
+        w,
+        (13, 19),
+        mat_ref,
+        couplings,
+        lambda src, r, c, near: jnp.where(keep[r], 1.2 * c + OMEGA * near, 0.0),
+    )
+    relax(
+        w,
+        r0,
+        (14, 18),
+        mat_ref,
+        couplings,
+        lambda src, r, c, near: v[src, r : r + 8, :] * (1.0 / OMEGA) - 6.0 * c + near,
+    )
+    rows = []
+    for xb in range(8):
+        parts = []
+        for yb in range(8):
+            src = xb * 8 + yb
+            parts.append(r0[src, pl.ds(14, 8, stride=2), :] + r0[src, pl.ds(15, 8, stride=2), :])
+        rows.append(jnp.concatenate(parts, axis=1))
+    summed = jnp.concatenate(rows, axis=0)
+    coarse = jnp.dot(halves(summed, 0), down_ref[...], preferred_element_type=F32)
+    coarse = coarse[0:64] + coarse[64:128]
+    below, above = [], []
+    own = []
+    for xb in range(8):
+        part = coarse[xb * 8 : xb * 8 + 8]
+        own.append(part[1:5, 0:128])
+        own.append(part[1:5, 128:256])
+        below.append(part[0:1, 0:128])
+        above.append(part[5:6, 128:256])
+    sent = jnp.concatenate(own + below + above, axis=0)
+    for e in range(8):
+        sent_ref[e] = sent
+
+
+def source_step(scalars, occupations, own, mat, down):
     smem = pl.BlockSpec(memory_space=pltpu.SMEM)
     vmem = pl.BlockSpec(memory_space=pltpu.VMEM)
     return pl.pallas_call(
-        unpack_kernel,
-        out_shape=(jax.ShapeDtypeStruct((512, 128), F32), jax.ShapeDtypeStruct((64, 128), F32)),
-        in_specs=[smem, vmem],
+        source_kernel,
+        out_shape=(
+            jax.ShapeDtypeStruct((64, 8, 128), F32),
+            jax.ShapeDtypeStruct((8, 80, 128), F32),
+        ),
+        in_specs=[smem, smem, vmem, vmem, vmem],
         out_specs=(vmem, vmem),
+        scratch_shapes=[pltpu.VMEM((64, 40, 128), F32)] * 3 + COUPLINGS,
         compiler_params=VMEM,
-    )(occupations, slabs)
-
-
-def neighbours_sum(v):
-    z = jnp.pad(v[1:-1, 1:-1], ((0, 0), (0, 0), (1, 1)))
-    total = v[2:, 1:-1] + v[:-2, 1:-1] + v[1:-1, 2:] + v[1:-1, :-2]
-    return total + z[:, :, 2:] + z[:, :, :-2]
-
-
-def restrict_mean(r):
-    sx, sy, sz = r.shape
-    r = r.reshape(sx // 2, 2, sy, sz).sum(axis=1)
-    r = r.reshape(sx // 2, sy // 2, 2, sz).sum(axis=2)
-    halve = np.zeros((sz, sz // 2), np.float32)
-    halve[np.arange(sz), np.arange(sz) // 2] = 0.125
-    return jnp.einsum("xyz,zw->xyw", r, halve, precision=lax.Precision.HIGHEST)
-
-
-def prolong_copy(e):
-    sx, sy, sz = e.shape
-    double = np.zeros((sz, 2 * sz), np.float32)
-    double[np.arange(2 * sz) // 2, np.arange(2 * sz)] = 1.0
-    e = jnp.einsum("xyz,zw->xyw", e, double, precision=lax.Precision.HIGHEST)
-    e = jnp.broadcast_to(e[:, None, :, None, :], (sx, 2, sy, 2, 2 * sz))
-    return e.reshape(2 * sx, 2 * sy, 2 * sz)
-
-
-def coarse_cycle(level, source):
-    scale = 4.0**level
-    diagonal = 6.0 / scale
-
-    def operate(v):
-        padded = jnp.pad(v, ((1, 1), (1, 1), (0, 0)))
-        return (6.0 * v - neighbours_sum(padded)) / scale
-
-    v = DAMPING * source / diagonal
-    for _ in range((COARSE if level == LEVELS - 1 else PRE) - 1):
-        v = v + DAMPING * (source - operate(v)) / diagonal
-    if level < LEVELS - 1:
-        v = v + prolong_copy(coarse_cycle(level + 1, restrict_mean(source - operate(v))))
-        for _ in range(POST):
-            v = v + DAMPING * (source - operate(v)) / diagonal
-    return v
+    )(scalars, occupations, own, mat, down)
+
+
+def double_rows(scratch, value, n):
+    scratch[:, pl.ds(0, n, stride=2), :] = value
+    scratch[:, pl.ds(1, n, stride=2), :] = value
+
+
+def coarse_solve(g, v, r1, v2, r2, v3, r3, mats):
+    down1, up1, down2, up2, near1, near2, near3 = mats
+
+    def near(ref, blocks, planes, mat):
+        rows = ref[:, 8 : 8 + planes, :]
+        y = jnp.dot(
+            halves(rows.reshape(blocks * planes, 128), 1), mat[...], preferred_element_type=F32
+        )
+        y = y.reshape(blocks, planes, -1)
+        total = y[:, :, 0:128] + ref[:, 7 : 7 + planes, :] + ref[:, 9 : 9 + planes, :]
+        if blocks > 1:
+            none = jnp.zeros((1, planes, 128), F32)
+            total = total + jnp.concatenate([none, y[:-1, :, 128:256]], axis=0)
+            total = total + jnp.concatenate([y[1:, :, 256:384], none], axis=0)
+        return rows, total
+
+    def sweep(ref, source, blocks, planes, mat):
+        rows, total = near(ref, blocks, planes, mat)
+        ref[:, 8 : 8 + planes, :] = rows + OMEGA * (source() - 6.0 * rows + total)
+
+    def residual(ref, source, blocks, planes, mat):
+        rows, total = near(ref, blocks, planes, mat)
+        return source() - 6.0 * rows + total
+
+    for ref, planes in ((v, 64), (v2, 32), (v3, 16)):
+        border = jnp.zeros((ref.shape[0], 8, 128), F32)
+        ref[:, 0:8, :] = border
+        ref[:, 8 + planes : 16 + planes, :] = border
+    g1 = lambda: g[:, 8:72, :]
+    v[:, 8:72, :] = OMEGA * g1()
+    sweep(v, g1, 8, 64, near1)
+    r1[...] = residual(v, g1, 8, 64, near1)
+    pair = r1[:, pl.ds(0, 32, stride=2), :] + r1[:, pl.ds(1, 32, stride=2), :]
+    rows = [jnp.concatenate([pair[4 * b + e] for e in range(4)], axis=1) for b in range(2)]
+    d = jnp.dot(halves(jnp.concatenate(rows, axis=0), 0), down1[...], preferred_element_type=F32)
+    s2 = (d[0:64] + d[64:128]).reshape(2, 32, 128)
+    g2 = lambda: s2
+    v2[:, 8:40, :] = OMEGA * s2
+    sweep(v2, g2, 2, 32, near2)
+    r2[...] = residual(v2, g2, 2, 32, near2)
+    pair = r2[:, pl.ds(0, 16, stride=2), :] + r2[:, pl.ds(1, 16, stride=2), :]
+    both = jnp.concatenate([pair[0], pair[1]], axis=1)
+    d = jnp.dot(halves(both, 0), down2[...], preferred_element_type=F32)
+    s3 = (d[0:16] + d[16:32]).reshape(1, 16, 128)
+    g3 = lambda: s3
+    v3[:, 8:24, :] = OMEGA * s3
+    for _ in range(COARSE - 1):
+        sweep(v3, g3, 1, 16, near3)
+    double_rows(r3, v3[:, 8:24, :], 16)
+    up = jnp.dot(halves(r3[0], 1), up2[...], preferred_element_type=F32)
+    for b in range(2):
+        v2[b, 8:40, :] = v2[b, 8:40, :] + up[:, b * 128 : b * 128 + 128]
+    for _ in range(POST):
+        sweep(v2, g2, 2, 32, near2)
+    double_rows(r1.at[0:2], v2[:, 8:40, :], 32)
+    up = jnp.dot(halves(r1[0:2].reshape(128, 128), 1), up1[...], preferred_element_type=F32)
+    for b in range(8):
+        part = up[(b // 4) * 64 : (b // 4) * 64 + 64, (b % 4) * 128 : (b % 4) * 128 + 128]
+        v[b, 8:72, :] = v[b, 8:72, :] + part
+    for _ in range(POST):
+        sweep(v, g1, 8, 64, near1)
+
+
+def finish_kernel(scalars, got_ref, prev_ref, f_ref, next_ref, y_ref, mat_ref, up_ref, *refs):
+    refs = list(refs)
+    mats, out_ref, refs = refs[:7], refs[7], refs[8:]
+    fx, va, vb, up, g, v, r1, v2, r2, v3, r3, wide = refs[:12]
+    couplings = refs[12:]
+    low = lanes_low((8, 128))
+    slab = scalars[0]
+
+    for s in range(8):
+        g[:, 8 + 8 * s : 16 + 8 * s, :] = got_ref[SLAB_DEVICE[s], 0:64, :].reshape(8, 8, 128)
+    for s in range(8):
+        for xb in range(8):
+            if s > 0:
+                row = 8 + 8 * s - 1
+                g[xb, row : row + 1, :] = g[xb, row : row + 1, :] + got_ref[SLAB_DEVICE[s], 64 + xb : 65 + xb, :]
+            if s < 7:
+                row = 8 + 8 * s + 8
+                g[xb, row : row + 1, :] = g[xb, row : row + 1, :] + got_ref[SLAB_DEVICE[s], 72 + xb : 73 + xb, :]
+    coarse_solve(g, v, r1, v2, r2, v3, r3, mats)
+    double_rows(wide, v[:, pl.ds(8 * slab + 4, 16), :], 16)
+    up[...] = jnp.dot(
+        halves(wide[...].reshape(256, 128), 1), up_ref[...], preferred_element_type=F32
+    ).reshape(8, 32, 1024)
+
+    def fill(i, carry):
+        for u in range(16):
+            src = i * 16 + u
+            p, o, n = prev_ref[src], f_ref[src], next_ref[src]
+            fx[src, 8:16, :] = OMEGA * swap(jnp.where(low, o, p))
+            fx[src, 16:24, :] = OMEGA * o
+            fx[src, 24:32, :] = OMEGA * swap(jnp.where(low, n, o))
+        return carry
+
+    lax.fori_loop(0, 4, fill, 0)
+    clear_borders(couplings, 2)
+    keep = {r: inside_slab_range(slab, r) for r in (14, 18, 15, 17)}
+
+    def to_third(src, r, c, near):
+        return jnp.where(keep[r], 1.2 * c + OMEGA * near, 0.0)
+
+    relax(fx, va, (14, 18), mat_ref, couplings, to_third)
+
+    def add_up(xb, carry):
+        for yb in range(8):
+            src = xb * 8 + yb
+            for r in (14, 22):
+                n = 8 if r == 14 else 4
+                e = jnp.where(
+                    lanes_low((n, 128)),
+                    up[xb, r - 8 : r - 8 + n, yb * 128 : yb * 128 + 128],
+                    up[xb, r : r + n, yb * 128 : yb * 128 + 128],
+                )
+                va[src, r : r + n, :] = va[src, r : r + n, :] + e
+        return carry
+
+    lax.fori_loop(0, 8, add_up, 0)
+
+    def swept(src, r, c, near):
+        return c + (fx[src, r : r + 8, :] - DAMPING * c + OMEGA * near)
+
+    relax(
+        va,
+        vb,
+        (15, 17),
+        mat_ref,
+        couplings,
+        lambda src, r, c, near: jnp.where(keep[r], swept(src, r, c, near), 0.0),
+    )
+    relax(vb, va, (16,), mat_ref, couplings, swept)
+    out_ref[:, 0:8, :] = y_ref[...]
+    out_ref[:, 8:16, :] = va[:, 16:24, :]
+
+
+def finish_step(scalars, got, halo, f, own, mat, levels):
+    smem = pl.BlockSpec(memory_space=pltpu.SMEM)
+    vmem = pl.BlockSpec(memory_space=pltpu.VMEM)
+    ins = [scalars, got, halo[0], f, halo[1], own, mat, levels[1], *levels[2:]]
+    big = pltpu.VMEM((64, 40, 128), F32)
+    return pl.pallas_call(
+        finish_kernel,
+        out_shape=jax.ShapeDtypeStruct((64, 16, 128), F32),
+        in_specs=[smem] + [vmem] * (len(ins) - 1),
+        out_specs=vmem,
+        scratch_shapes=[
+            big,
+            big,
+            big,
+            pltpu.VMEM((8, 32, 1024), F32),
+            pltpu.VMEM((8, 80, 128), F32),
+            pltpu.VMEM((8, 80, 128), F32),
+            pltpu.VMEM((8, 64, 128), F32),
+            pltpu.VMEM((2, 48, 128), F32),
+            pltpu.VMEM((2, 32, 128), F32),
+            pltpu.VMEM((1, 32, 128), F32),
+            pltpu.VMEM((1, 32, 128), F32),
+            pltpu.VMEM((8, 32, 128), F32),
+        ]
+        + COUPLINGS,
+        compiler_params=VMEM,
+    )(*ins)
 
 
 def exchange(value, axes, dim, width, order=None):
@@ -423,46 +745,13 @@
     return before, after
 
 
-def hartree_of(density):
-    gx, gyz = lax.axis_index(GX), lax.axis_index(GYZ)
-    before, after = exchange(density, GX, 0, 3)
-    f = jnp.concatenate([before, density, after], axis=0)
-    before, after = exchange(f, GYZ, 1, 3)
-    f = jnp.concatenate([before, f, after], axis=1)
-
-    def inside(width):
-        def along(index):
-            cell = jnp.arange(8 + 2 * width) - width + 8 * index
-            return jnp.logical_and(cell >= 0, cell < 64)
-
-        return jnp.logical_and(along(gx)[:, None, None], along(gyz)[None, :, None])
-
-    def sweep(v, source):
-        centre = v[1:-1, 1:-1]
-        return centre + (DAMPING / 6.0) * (source - (6.0 * centre - neighbours_sum(v)))
-
-    v = (DAMPING / 6.0) * f
-    v = jnp.where(inside(2), sweep(v, f[1:-1, 1:-1]), 0.0)
-    inner = v[1:-1, 1:-1]
-    residual = f[2:-2, 2:-2] - (6.0 * inner - neighbours_sum(v))
-    coarse = restrict_mean(residual[1:-1, 1:-1])
-    sent = jnp.broadcast_to(coarse.reshape(1, 8, 128), (64, 8, 128))
-    got = lax.all_to_all(sent, PLANE, 0, 0, tiled=True)
-    whole = got.reshape(8, 8, 4, 4, 64).transpose(0, 2, 1, 3, 4).reshape(32, 32, 64)
-    error = jnp.pad(coarse_cycle(1, whole), ((1, 1), (1, 1), (0, 0)))
-    error = lax.dynamic_slice(error, (4 * gx, 4 * gyz, 0), (6, 6, 64))
-    v = v + prolong_copy(error)
-    v = jnp.where(inside(1), sweep(v, f[2:-2, 2:-2]), 0.0)
-    return sweep(v, f[3:-3, 3:-3])
-
-
 def local(
     orbitals, local_potential, occupations, proj_values, proj_strength, atom_block, atom_offset
 ):
     core, xlo, ylo = (lax.axis_index(a) for a in GROUP)
     slab = 2 * (xlo * (3 - ylo) + (1 - xlo) * ylo) + core
     lists, strength = atom_lists(slab, proj_strength, atom_block, atom_offset)
-    high, low = coupling()
+    high, low = coupling(HALF)
     mats = (jnp.asarray(high), jnp.asarray(low), jnp.ones((256, 128), BF16))
 
     packed, tiles = pack(orbitals, local_potential, proj_values)
@@ -490,12 +779,18 @@
         if not last:
             older = outs.pop(0)
 
-    back = lax.all_to_all(own, PLANE, 0, 0, tiled=True)
-    filtered, density = unpack(occupations, back)
-    sent = jnp.broadcast_to(density[None], (8, 64, 128))
-    density = jnp.sum(lax.all_to_all(sent, BAND, 0, 0, tiled=True), axis=0) / 64.0
-    hartree = hartree_of(density.reshape(8, 8, 128))
-    return filtered.reshape(8, 8, 8, 128), hartree
+    scalars = jnp.stack([slab, 2 * lax.axis_index("yhi") + lax.axis_index("xhi")]).astype(jnp.int32)
+    near, _ = coupling((0.0, 1.0))
+    near = jnp.asarray(near)
+    levels = [jnp.asarray(m) for m in level_matrices()]
+    f, sent = source_step(scalars, occupations, own, near, levels[0])
+    halo = exchange(f, GROUP, 1, 8, SLAB_DEVICE)
+    got = lax.all_to_all(sent, GROUP, 0, 0, tiled=True)
+    packed = finish_step(scalars, got, halo, f, own, near, levels)
+    back = lax.all_to_all(packed, PLANE, 0, 0, tiled=True)
+    filtered, part = unpack(back)
+    hartree = jnp.sum(lax.all_to_all(part, BAND, 0, 0, tiled=True), axis=0)
+    return filtered.reshape(8, 8, 8, 128), hartree.reshape(8, 8, 128)
 
 
 def solution(mesh):

time: 199 us -> 188 us (0.945)
  blocking collectives: 18.3 us -> 46.3 us
  starting transfers between devices: 64.1 us -> 38.5 us
  waiting for transfers between devices: 60.7 us -> 44.7 us
  Pallas kernels: 36.9 us -> 46.2 us
  other arithmetic: 6.21 us -> 2.59 us
    all_to_all x1 -> x2, blocking collectives: 18.3 us -> 46.3 us  [the longest x1 24 us: local(): back = lax.all_to_all(packed, PLANE, 0, 0, tiled=True)]
    all_to_all x2 -> x1, waiting for transfers between devices: 24.3 us -> 0.01 us  [local(): got = lax.all_to_all(sent, GROUP, 0, 0, tiled=True)]
    all_to_all x2 -> x1, starting transfers between devices: 20.7 us -> 5.06 us  [local(): got = lax.all_to_all(sent, GROUP, 0, 0, tiled=True)]
    pallas_call x0 -> x2, Pallas kernels: none -> 9.93 us  [the longest x1 6.17 us: finish_step(): pl.pallas_call(finish_kernel, out_shape=jax.ShapeDtypeStruct((64, 16, 128...]
    ppermute x6 -> x5, starting transfers between devices: 20.2 us -> 11.5 us  [exchange(): lax.ppermute(lax.slice_in_dim(value, 0, width, axis=dim), axes, down)]
    ppermute x6 -> x5, waiting for transfers between devices: 11.1 us -> 19.2 us  [exchange(): lax.ppermute(lax.slice_in_dim(value, length - width, length, axis=dim), a...]
    add x12 -> x0, other arithmetic: 2.72 us -> none  [the longest x7 1.88 us: coarse_cycle(): v = v + DAMPING * (source - operate(v)) / diagonal]
    unnamed x28 -> x48, local copies, waits for them, and re-layouts: 3.17 us -> 5.58 us
  transfers between devices with their start and end apart: 15 -> 12, of which waited for: 13 -> 11; matrix products, arithmetic and copies ran while one was open for 2% -> 2% of each run, Pallas kernels for 0% -> 0%
where the time goes in v2:
time: 188 us; the launch traced here: 187 us
  blocking collectives  46.3 us (25%)
  Pallas kernels  46.2 us (25%)
  waiting for transfers between devices  44.7 us (24%)
  starting transfers between devices  38.5 us (20%)
  local copies, waits for them, and re-layouts  7.76 us (4%)
  other arithmetic  2.59 us (1%)
    pallas_call x4, Pallas kernels, double_step(): pl.pallas_call(functools.partial(double_kernel, first, last, coef1, coef2...  31.5 us
    all_to_all x1, blocking collectives, local(): back = lax.all_to_all(packed, PLANE, 0, 0, tiled=True)  24 us
    all_to_all x1, blocking collectives, local(): hartree = jnp.sum(lax.all_to_all(part, BAND, 0, 0, tiled=True), axis=0)  22.3 us
    ppermute x5, waiting for transfers between devices, exchange(): lax.ppermute(lax.slice_in_dim(value, length - width, length, axis=dim), a...  19.2 us
    all_to_all x1, waiting for transfers between devices, local(): own = lax.all_to_all(packed, PLANE, 0, 0, tiled=True)  14.9 us
    ppermute x5, starting transfers between devices, exchange(): lax.ppermute(lax.slice_in_dim(value, 0, width, axis=dim), axes, down)  11.5 us
    ppermute x5, starting transfers between devices, exchange(): lax.ppermute(lax.slice_in_dim(value, length - width, length, axis=dim), a...  11.3 us
    all_to_all x1, starting transfers between devices, local(): own = lax.all_to_all(packed, PLANE, 0, 0, tiled=True)  10.7 us
  transfers between devices with their start and end apart: 12, of which 11 were waited for; matrix products, arithmetic and copies ran while one was open for 2% of the time, Pallas kernels for 0%

profile of v2, /device:TPU:6, one launch (start us, length us, event | category | flops | bytes accessed | tf_op | source)
XLA Modules:
  0.0 187.1 jit_solution(953030696167320384)
XLA Ops:
  2.0 3.8 %shard_map.203 = (f32[64,16,128]{2,1,0:T(8,128)}, f32[64,4,8,128]{3,2,1,0:T(8,128)S(1)}) custom-call(f32[512,128]{1,0:T(8,128)S(1)} %bitcast.33, f32[64,128]{1,0:T(8,128)S(1)} %bitcast.34, f32[256,512]{1,0:T(8,128)S(1)} %reshape.221.proj_ref, bf16[512,128]{1,0:T(8,128)(2,1)S(1)} %copy-done.17), custom_call_target="tpu_custom_call" | custom-call | tf_op jit(solution)/shard_map/pallas_call | solution.py:120
  5.8 10.7 %all-to-all-start = ((f32[64,16,128]{2,1,0:T(8,128)}), f32[64,16,128]{2,1,0:T(8,128)S(1)}, u32[]{:S(2)}, u32[]{:S(2)}) async-start(f32[64,16,128]{2,1,0:T(8,128)} %get-tuple-element.51), calls=%async_computation | async-start | bytes 1048576 | tf_op jit(solution)/shard_map/all_to_all | solution.py:758
  19.2 14.9 %all-to-all-done.own_ref = f32[64,16,128]{2,1,0:T(8,128)S(1)} async-done(((f32[64,16,128]{2,1,0:T(8,128)}), f32[64,16,128]{2,1,0:T(8,128)S(1)}, u32[]{:S(2)}, u32[]{:S(2)}) %all-to-all-start) | async-done | bytes 524320 | tf_op jit(solution)/shard_map/all_to_all | solution.py:758
  34.1 2.6 %collective-permute-start.1 = (f32[64,16,128]{2,1,0:T(8,128)S(1)}, f32[64,16,128]{2,1,0:T(8,128)S(1)}, u32[]{:S(2)}, u32[]{:S(2)}) collective-permute-start(f32[64,16,128]{2,1,0:T(8,128)S(1)} %all-to-all-done.own_ref), channel_id=1, source_target_pairs={{8,0},{1,8},{9,1},{3,9},{11,3},{2,11},{10,2},{12,4},{5,12},{13,5},... | collective-permute-start | bytes 1572872 | tf_op jit(solution)/shard_map/ppermute | solution.py:744
  38.8 4.6 %collective-permute-done.1.next_ref = f32[64,16,128]{2,1,0:T(8,128)S(1)} collective-permute-done((f32[64,16,128]{2,1,0:T(8,128)S(1)}, f32[64,16,128]{2,1,0:T(8,128)S(1)}, u32[]{:S(2)}, u32[]{:S(2)}) %collective-permute-start.1) | collective-permute-done | bytes 524320 | tf_op jit(solution)/shard_map/ppermute | solution.py:744
  43.4 3.8 %collective-permute-done.prev_ref = f32[64,16,128]{2,1,0:T(8,128)S(1)} collective-permute-done((f32[64,16,128]{2,1,0:T(8,128)S(1)}, f32[64,16,128]{2,1,0:T(8,128)S(1)}, u32[]{:S(2)}, u32[]{:S(2)}) %collective-permute-start) | collective-permute-done | bytes 524320 | tf_op jit(solution)/shard_map/ppermute | solution.py:743
  49.1 7.9 %shard_map.204 = (f32[64,8,128]{2,1,0:T(8,128)S(1)}, f32[64,24,128]{2,1,0:T(8,128)S(1)}, f32[64,24,128]{2,1,0:T(8,128)S(1)}) custom-call(s32[9,64]{1,0:T(8,128)S(1)} %stack.39.lists, f32[4,64]{1,0:T(4,128)S(1)} %select_reduce_fusion.strength, f32[64,16,128]{2,1,0:T(8,128)S(1)} %copy-done.8, f32[64,16,128]{2,1,0:T(8,128)S(1)} %all-to-all-done.own_ref, ...), custom_call_target="tpu_custom_call" | custom-call | tf_op jit(solution)/shard_map/pallas_call | solution.py:291
  59.0 2.4 %collective-permute-start.2 = (f32[64,8,128]{2,1,0:T(8,128)S(1)}, f32[64,8,128]{2,1,0:T(8,128)S(1)}, u32[]{:S(2)}, u32[]{:S(2)}) collective-permute-start(f32[64,8,128]{2,1,0:T(8,128)S(1)} %get-tuple-element.53.own_ref), channel_id=1, source_target_pairs={{0,8},{8,1},{1,9},{9,3},{3,11},{11,2},{2,10},{4,12},{12,5},{5,13},... | collective-permute-start | bytes 786440 | tf_op jit(solution)/shard_map/ppermute | solution.py:743
  62.8 3.8 %collective-permute-done.2.prev_ref = f32[64,8,128]{2,1,0:T(8,128)S(1)} collective-permute-done((f32[64,8,128]{2,1,0:T(8,128)S(1)}, f32[64,8,128]{2,1,0:T(8,128)S(1)}, u32[]{:S(2)}, u32[]{:S(2)}) %collective-permute-start.2) | collective-permute-done | bytes 262176 | tf_op jit(solution)/shard_map/ppermute | solution.py:743
  66.7 7.8 %shard_map.205 = (f32[64,8,128]{2,1,0:T(8,128)S(1)}, f32[64,24,128]{2,1,0:T(8,128)S(1)}) custom-call(s32[9,64]{1,0:T(8,128)S(1)} %stack.39.lists, f32[4,64]{1,0:T(4,128)S(1)} %select_reduce_fusion.strength, f32[64,8,128]{2,1,0:T(8,128)S(1)} %collective-permute-done.2.prev_ref, f32[64,8,128]{2,1,0:T(8,128)S(1)} %get-tuple-element.53.own_ref, ...), custom_call_target="tpu_custom_call" | custom-call | tf_op jit(solution)/shard_map/pallas_call | solution.py:291
  76.4 2.4 %collective-permute-start.4 = (f32[64,8,128]{2,1,0:T(8,128)S(1)}, f32[64,8,128]{2,1,0:T(8,128)S(1)}, u32[]{:S(2)}, u32[]{:S(2)}) collective-permute-start(f32[64,8,128]{2,1,0:T(8,128)S(1)} %get-tuple-element.56.own_ref), channel_id=1, source_target_pairs={{0,8},{8,1},{1,9},{9,3},{3,11},{11,2},{2,10},{4,12},{12,5},{5,13},... | collective-permute-start | bytes 786440 | tf_op jit(solution)/shard_map/ppermute | solution.py:743
  80.3 3.8 %collective-permute-done.4.prev_ref = f32[64,8,128]{2,1,0:T(8,128)S(1)} collective-permute-done((f32[64,8,128]{2,1,0:T(8,128)S(1)}, f32[64,8,128]{2,1,0:T(8,128)S(1)}, u32[]{:S(2)}, u32[]{:S(2)}) %collective-permute-start.4) | collective-permute-done | bytes 262176 | tf_op jit(solution)/shard_map/ppermute | solution.py:743
  84.1 7.9 %shard_map.206 = (f32[64,8,128]{2,1,0:T(8,128)S(1)}, f32[64,24,128]{2,1,0:T(8,128)S(1)}) custom-call(s32[9,64]{1,0:T(8,128)S(1)} %stack.39.lists, f32[4,64]{1,0:T(4,128)S(1)} %select_reduce_fusion.strength, f32[64,8,128]{2,1,0:T(8,128)S(1)} %collective-permute-done.4.prev_ref, f32[64,8,128]{2,1,0:T(8,128)S(1)} %get-tuple-element.56.own_ref, ...), custom_call_target="tpu_custom_call" | custom-call | tf_op jit(solution)/shard_map/pallas_call | solution.py:291
  94.8 2.4 %collective-permute-start.6 = (f32[64,8,128]{2,1,0:T(8,128)S(1)}, f32[64,8,128]{2,1,0:T(8,128)S(1)}, u32[]{:S(2)}, u32[]{:S(2)}) collective-permute-start(f32[64,8,128]{2,1,0:T(8,128)S(1)} %get-tuple-element.58.own_ref), channel_id=1, source_target_pairs={{0,8},{8,1},{1,9},{9,3},{3,11},{11,2},{2,10},{4,12},{12,5},{5,13},... | collective-permute-start | bytes 786440 | tf_op jit(solution)/shard_map/ppermute | solution.py:743
  98.7 3.9 %collective-permute-done.6.prev_ref = f32[64,8,128]{2,1,0:T(8,128)S(1)} collective-permute-done((f32[64,8,128]{2,1,0:T(8,128)S(1)}, f32[64,8,128]{2,1,0:T(8,128)S(1)}, u32[]{:S(2)}, u32[]{:S(2)}) %collective-permute-start.6) | collective-permute-done | bytes 262176 | tf_op jit(solution)/shard_map/ppermute | solution.py:743
  105.4 7.9 %shard_map.207.own_ref.y_ref = f32[64,8,128]{2,1,0:T(8,128)S(1)} custom-call(s32[9,64]{1,0:T(8,128)S(1)} %stack.39.lists, f32[4,64]{1,0:T(4,128)S(1)} %select_reduce_fusion.strength, f32[64,8,128]{2,1,0:T(8,128)S(1)} %copy-done.12, f32[64,8,128]{2,1,0:T(8,128)S(1)} %get-tuple-element.58.own_ref, f32[64,8,128]{2,1,0:T(8,128)S(1)} %collective-permute-done.7.next_ref, ...), custom_call_target="tpu_custom_call" | custom-call | tf_op jit(solution)/shard_map/pallas_call | solution.py:291
  113.4 3.8 %shard_map.208 = (f32[64,8,128]{2,1,0:T(8,128)S(1)}, f32[8,80,128]{2,1,0:T(8,128)}) custom-call(s32[2]{0:T(128)S(1)} %pad_add_fusion.scalars, f32[8]{0:T(128)S(1)} %copy-done.21, f32[64,8,128]{2,1,0:T(8,128)S(1)} %shard_map.207.own_ref.y_ref, bf16[256,640]{1,0:T(8,128)(2,1)S(1)} %copy-done.2, bf16[1024,256]{1,0:T(8,128)(2,1)S(1)} %copy-done.5), custom_call_target="tpu_custom_call" | custom-call | tf_op jit(solution)/shard_map/pallas_call | solution.py:555
  117.1 5.1 %all-to-all-start.1 = ((f32[8,80,128]{2,1,0:T(8,128)}), f32[8,80,128]{2,1,0:T(8,128)S(1)}, u32[]{:S(2)}, u32[]{:S(2)}) async-start(f32[8,80,128]{2,1,0:T(8,128)} %get-tuple-element.60), calls=%async_computation.1 | async-start | bytes 655360 | tf_op jit(solution)/shard_map/all_to_all | solution.py:788
  122.2 3.1 %collective-permute-start.9 = (f32[64,8,128]{2,1,0:T(8,128)S(1)}, f32[64,8,128]{2,1,0:T(8,128)S(1)}, u32[]{:S(2)}, u32[]{:S(2)}) collective-permute-start(f32[64,8,128]{2,1,0:T(8,128)S(1)} %get-tuple-element.61.f_ref), channel_id=1, source_target_pairs={{8,0},{1,8},{9,1},{3,9},{11,3},{2,11},{10,2},{12,4},{5,12},{13,5},... | collective-permute-start | bytes 786440 | tf_op jit(solution)/shard_map/ppermute | solution.py:744
  125.3 2.1 %collective-permute-start.8 = (f32[64,8,128]{2,1,0:T(8,128)S(1)}, f32[64,8,128]{2,1,0:T(8,128)S(1)}, u32[]{:S(2)}, u32[]{:S(2)}) collective-permute-start(f32[64,8,128]{2,1,0:T(8,128)S(1)} %get-tuple-element.61.f_ref), channel_id=1, source_target_pairs={{0,8},{8,1},{1,9},{9,3},{3,11},{11,2},{2,10},{4,12},{12,5},{5,13},... | collective-permute-start | bytes 786440 | tf_op jit(solution)/shard_map/ppermute | solution.py:743
  129.3 3.7 %collective-permute-done.8.prev_ref = f32[64,8,128]{2,1,0:T(8,128)S(1)} collective-permute-done((f32[64,8,128]{2,1,0:T(8,128)S(1)}, f32[64,8,128]{2,1,0:T(8,128)S(1)}, u32[]{:S(2)}, u32[]{:S(2)}) %collective-permute-start.8) | collective-permute-done | bytes 262176 | tf_op jit(solution)/shard_map/ppermute | solution.py:743
  133.1 6.2 %shard_map.209 = f32[64,16,128]{2,1,0:T(8,128)S(1)} custom-call(s32[2]{0:T(128)S(1)} %pad_add_fusion.scalars, f32[8,80,128]{2,1,0:T(8,128)S(1)} %all-to-all-done.1.got_ref, f32[64,8,128]{2,1,0:T(8,128)S(1)} %collective-permute-done.8.prev_ref, f32[64,8,128]{2,1,0:T(8,128)S(1)} %get-tuple-element.61.f_ref, f32[64,8,128]{2,1,0:T(8,128)S(1)} %collective-permute-done.9.next_ref, ...), custom_call_target="tpu_custom_call" | custom-call | tf_op jit(solution)/shard_map/pallas_call | solution.py:714
  139.3 24.0 %all_to_all.20.in_ref = f32[64,16,128]{2,1,0:T(8,128)S(1)} all-to-all(f32[64,16,128]{2,1,0:T(8,128)S(1)} %shard_map.209), channel_id=1, replica_groups=mesh['z'=8,'yhi'=4,'core'=2,'xhi'=2,'xlo'=2,'ylo'=2] {'yhi','core','xhi'..., dimensions={0} | all-to-all | bytes 1048576 | tf_op jit(solution)/shard_map/all_to_all | solution.py:790
  164.2 22.3 %all_to_all.21 = f32[8,64,128]{2,1,0:T(8,128)S(1)} all-to-all(f32[8,64,128]{2,1,0:T(8,128)S(1)} %get-tuple-element.63), channel_id=1, replica_groups=mesh['z'=8,'yhi'=4,'core'=2,'xhi'=2,'xlo'=2,'ylo'=2] {'z'}, dimensions={0} | all-to-all | bytes 524288 | tf_op jit(solution)/shard_map/all_to_all | solution.py:792
  (74 shorter events, 25.1 us)
Async XLA Ops:
  5.8 10.8 %copy-start.23 = (s32[64]{0:T(128)S(1)}, s32[64]{0:T(128)}, u32[]{:S(2)}) copy-start(s32[64]{0:T(128)} %param.31) | copy-start | bytes 772
  5.8 32.9 %copy-start.22 = (f32[64,4]{0,1:T(4,128)S(1)}, f32[64,4]{0,1:T(4,128)}, u32[]{:S(2)}) copy-start(f32[64,4]{0,1:T(4,128)} %param.30) | copy-start | bytes 3076
  5.8 42.3 %copy-start = (bf16[256,640]{1,0:T(8,128)(2,1)S(1)}, bf16[256,640]{1,0:T(8,128)(2,1)}, u32[]{:S(2)}) copy-start(bf16[256,640]{1,0:T(8,128)(2,1)} %constant.149.clone.refs_1_.refs_3_) | copy-start | bytes 983044
  5.8 28.3 %all-to-all-start = ((f32[64,16,128]{2,1,0:T(8,128)}), f32[64,16,128]{2,1,0:T(8,128)S(1)}, u32[]{:S(2)}, u32[]{:S(2)}) async-start(f32[64,16,128]{2,1,0:T(8,128)} %get-tuple-element.51), calls=%async_computation | async-start | bytes 1048576 | tf_op jit(solution)/shard_map/all_to_all | solution.py:758
  16.5 31.5 %copy-start.1 = (bf16[128,640]{1,0:T(8,128)(2,1)S(1)}, bf16[128,640]{1,0:T(8,128)(2,1)}, u32[]{:S(2)}) copy-start(bf16[128,640]{1,0:T(8,128)(2,1)} %constant.150.clone.refs_2_.refs_4_) | copy-start | bytes 491524
  34.1 9.3 %collective-permute-start.1 = (f32[64,16,128]{2,1,0:T(8,128)S(1)}, f32[64,16,128]{2,1,0:T(8,128)S(1)}, u32[]{:S(2)}, u32[]{:S(2)}) collective-permute-start(f32[64,16,128]{2,1,0:T(8,128)S(1)} %all-to-all-done.own_ref), channel_id=1, source_target_pairs={{8,0},{1,8},{9,1},{3,9},{11,3},{2,11},{10,2},{12,4},{5,12},{13,5},... | collective-permute-start | bytes 1572872 | tf_op jit(solution)/shard_map/ppermute | solution.py:744
  36.7 10.5 %collective-permute-start = (f32[64,16,128]{2,1,0:T(8,128)S(1)}, f32[64,16,128]{2,1,0:T(8,128)S(1)}, u32[]{:S(2)}, u32[]{:S(2)}) collective-permute-start(f32[64,16,128]{2,1,0:T(8,128)S(1)} %all-to-all-done.own_ref), channel_id=1, source_target_pairs={{0,8},{8,1},{1,9},{9,3},{3,11},{11,2},{2,10},{4,12},{12,5},{5,13},... | collective-permute-start | bytes 1572872 | tf_op jit(solution)/shard_map/ppermute | solution.py:743
  57.0 5.8 %collective-permute-start.3 = (f32[64,8,128]{2,1,0:T(8,128)S(1)}, f32[64,8,128]{2,1,0:T(8,128)S(1)}, u32[]{:S(2)}, u32[]{:S(2)}) collective-permute-start(f32[64,8,128]{2,1,0:T(8,128)S(1)} %get-tuple-element.53.own_ref), channel_id=1, source_target_pairs={{8,0},{1,8},{9,1},{3,9},{11,3},{2,11},{10,2},{12,4},{5,12},{13,5},... | collective-permute-start | bytes 786440 | tf_op jit(solution)/shard_map/ppermute | solution.py:744
  59.0 7.7 %collective-permute-start.2 = (f32[64,8,128]{2,1,0:T(8,128)S(1)}, f32[64,8,128]{2,1,0:T(8,128)S(1)}, u32[]{:S(2)}, u32[]{:S(2)}) collective-permute-start(f32[64,8,128]{2,1,0:T(8,128)S(1)} %get-tuple-element.53.own_ref), channel_id=1, source_target_pairs={{0,8},{8,1},{1,9},{9,3},{3,11},{11,2},{2,10},{4,12},{12,5},{5,13},... | collective-permute-start | bytes 786440 | tf_op jit(solution)/shard_map/ppermute | solution.py:743
  74.5 5.8 %collective-permute-start.5 = (f32[64,8,128]{2,1,0:T(8,128)S(1)}, f32[64,8,128]{2,1,0:T(8,128)S(1)}, u32[]{:S(2)}, u32[]{:S(2)}) collective-permute-start(f32[64,8,128]{2,1,0:T(8,128)S(1)} %get-tuple-element.56.own_ref), channel_id=1, source_target_pairs={{8,0},{1,8},{9,1},{3,9},{11,3},{2,11},{10,2},{12,4},{5,12},{13,5},... | collective-permute-start | bytes 786440 | tf_op jit(solution)/shard_map/ppermute | solution.py:744
  76.4 7.7 %collective-permute-start.4 = (f32[64,8,128]{2,1,0:T(8,128)S(1)}, f32[64,8,128]{2,1,0:T(8,128)S(1)}, u32[]{:S(2)}, u32[]{:S(2)}) collective-permute-start(f32[64,8,128]{2,1,0:T(8,128)S(1)} %get-tuple-element.56.own_ref), channel_id=1, source_target_pairs={{0,8},{8,1},{1,9},{9,3},{3,11},{11,2},{2,10},{4,12},{12,5},{5,13},... | collective-permute-start | bytes 786440 | tf_op jit(solution)/shard_map/ppermute | solution.py:743
  92.9 5.8 %collective-permute-start.7 = (f32[64,8,128]{2,1,0:T(8,128)S(1)}, f32[64,8,128]{2,1,0:T(8,128)S(1)}, u32[]{:S(2)}, u32[]{:S(2)}) collective-permute-start(f32[64,8,128]{2,1,0:T(8,128)S(1)} %get-tuple-element.58.own_ref), channel_id=1, source_target_pairs={{8,0},{1,8},{9,1},{3,9},{11,3},{2,11},{10,2},{12,4},{5,12},{13,5},... | collective-permute-start | bytes 786440 | tf_op jit(solution)/shard_map/ppermute | solution.py:744
  94.8 7.8 %collective-permute-start.6 = (f32[64,8,128]{2,1,0:T(8,128)S(1)}, f32[64,8,128]{2,1,0:T(8,128)S(1)}, u32[]{:S(2)}, u32[]{:S(2)}) collective-permute-start(f32[64,8,128]{2,1,0:T(8,128)S(1)} %get-tuple-element.58.own_ref), channel_id=1, source_target_pairs={{0,8},{8,1},{1,9},{9,3},{3,11},{11,2},{2,10},{4,12},{12,5},{5,13},... | collective-permute-start | bytes 786440 | tf_op jit(solution)/shard_map/ppermute | solution.py:743
  113.3 19.7 %copy-start.9 = (bf16[256,512]{1,0:T(8,128)(2,1)S(1)}, bf16[256,512]{1,0:T(8,128)(2,1)}, u32[]{:S(2)}) copy-start(bf16[256,512]{1,0:T(8,128)(2,1)} %constant.156.clone.refs_1_) | copy-start | bytes 786436
  113.3 19.7 %copy-start.13 = (bf16[256,384]{1,0:T(8,128)(2,1)S(1)}, bf16[256,384]{1,0:T(8,128)(2,1)}, u32[]{:S(2)}) copy-start(bf16[256,384]{1,0:T(8,128)(2,1)} %constant.160.clone.refs_5_) | copy-start | bytes 589828
  113.3 19.7 %copy-start.14 = (bf16[256,384]{1,0:T(8,128)(2,1)S(1)}, bf16[256,384]{1,0:T(8,128)(2,1)}, u32[]{:S(2)}) copy-start(bf16[256,384]{1,0:T(8,128)(2,1)} %constant.159.clone.refs_4_) | copy-start | bytes 589828
  113.3 19.7 %copy-start.16 = (bf16[512,128]{1,0:T(8,128)(2,1)S(1)}, bf16[512,128]{1,0:T(8,128)(2,1)}, u32[]{:S(2)}) copy-start(bf16[512,128]{1,0:T(8,128)(2,1)} %constant.155.clone.refs_0_) | copy-start | bytes 393220
  113.3 19.7 %copy-start.18 = (bf16[256,128]{1,0:T(8,128)(2,1)S(1)}, bf16[256,128]{1,0:T(8,128)(2,1)}, u32[]{:S(2)}) copy-start(bf16[256,128]{1,0:T(8,128)(2,1)} %constant.161.clone.refs_6_) | copy-start | bytes 196612
  113.4 19.7 %copy-start.19 = (bf16[256,128]{1,0:T(8,128)(2,1)S(1)}, bf16[256,128]{1,0:T(8,128)(2,1)}, u32[]{:S(2)}) copy-start(bf16[256,128]{1,0:T(8,128)(2,1)} %constant.157.clone.refs_2_) | copy-start | bytes 196612
  117.1 15.9 %copy-start.6 = (bf16[256,1024]{1,0:T(8,128)(2,1)S(1)}, bf16[256,1024]{1,0:T(8,128)(2,1)}, u32[]{:S(2)}) copy-start(bf16[256,1024]{1,0:T(8,128)(2,1)} %constant.154.clone.up_ref) | copy-start | bytes 1572868
  117.1 15.9 %copy-start.15 = (bf16[256,256]{1,0:T(8,128)(2,1)S(1)}, bf16[256,256]{1,0:T(8,128)(2,1)}, u32[]{:S(2)}) copy-start(bf16[256,256]{1,0:T(8,128)(2,1)} %constant.158.clone.refs_3_) | copy-start | bytes 393220
  117.1 15.9 %all-to-all-start.1 = ((f32[8,80,128]{2,1,0:T(8,128)}), f32[8,80,128]{2,1,0:T(8,128)S(1)}, u32[]{:S(2)}, u32[]{:S(2)}) async-start(f32[8,80,128]{2,1,0:T(8,128)} %get-tuple-element.60), calls=%async_computation.1 | async-start | bytes 655360 | tf_op jit(solution)/shard_map/all_to_all | solution.py:788
  122.2 7.1 %collective-permute-start.9 = (f32[64,8,128]{2,1,0:T(8,128)S(1)}, f32[64,8,128]{2,1,0:T(8,128)S(1)}, u32[]{:S(2)}, u32[]{:S(2)}) collective-permute-start(f32[64,8,128]{2,1,0:T(8,128)S(1)} %get-tuple-element.61.f_ref), channel_id=1, source_target_pairs={{8,0},{1,8},{9,1},{3,9},{11,3},{2,11},{10,2},{12,4},{5,12},{13,5},... | collective-permute-start | bytes 786440 | tf_op jit(solution)/shard_map/ppermute | solution.py:744
  125.3 7.7 %collective-permute-start.8 = (f32[64,8,128]{2,1,0:T(8,128)S(1)}, f32[64,8,128]{2,1,0:T(8,128)S(1)}, u32[]{:S(2)}, u32[]{:S(2)}) collective-permute-start(f32[64,8,128]{2,1,0:T(8,128)S(1)} %get-tuple-element.61.f_ref), channel_id=1, source_target_pairs={{0,8},{8,1},{1,9},{9,3},{3,11},{11,2},{2,10},{4,12},{12,5},{5,13},... | collective-permute-start | bytes 786440 | tf_op jit(solution)/shard_map/ppermute | solution.py:743
  (12 other events, 33.1 us)

commit v3 on v2

--- a/solution.py
+++ b/solution.py
@@ -33,7 +33,9 @@
 GROUP = ("core", "xlo", "ylo")
 CHIPS = ((0, 0), (0, 1), (1, 1), (1, 0))
 SLAB_DEVICE = [c * 4 + xl * 2 + yl for xl, yl in CHIPS for c in (0, 1)]
-VMEM = pltpu.CompilerParams(vmem_limit_bytes=40 * 1024 * 1024)
+VMEM = pltpu.CompilerParams(vmem_limit_bytes=12 * 1024 * 1024)
+FILL = 16
+HEAD = 3
 F32 = jnp.float32
 BF16 = jnp.bfloat16
 
@@ -60,7 +62,7 @@
     whole = np.concatenate([own, xu, xd, yu, yd], axis=1).astype(np.float32)
     high = whole.astype(jnp.bfloat16)
     low = (whole - high.astype(np.float32)).astype(jnp.bfloat16)
-    return np.concatenate([high, high], axis=0), low
+    return high, low
 
 
 def halves(x, axis):
@@ -70,6 +72,10 @@
 
 def lanes_low(shape):
     return lax.broadcasted_iota(jnp.int32, shape, len(shape) - 1) < 64
+
+
+def dot2(x, m):
+    return jnp.dot(halves(x, 1), jnp.concatenate([m, m], axis=0), preferred_element_type=F32)
 
 
 def swap(x):
@@ -84,7 +90,7 @@
     return a, b, c
 
 
-def pack_kernel(orb_ref, pot_ref, proj_ref, pick_ref, out_ref, tiles_ref):
+def pack_kernel(orb_ref, pot_ref, out_ref):
     low = lanes_low((8, 128))
     for q in range(4):
         turned = orb_ref[q * 128 : (q + 1) * 128, :].T
@@ -100,13 +106,26 @@
         for b in range(8):
             out_ref[plane_index(b, s), 8:16, :] = piece
 
-    keep = lax.broadcasted_iota(jnp.int32, (32, 8, 512), 2) % 8 == lax.broadcasted_iota(
-        jnp.int32, (32, 8, 512), 1
+
+def pack(orbitals, potential):
+    return pl.pallas_call(
+        pack_kernel,
+        out_shape=jax.ShapeDtypeStruct((64, 16, 128), F32),
+        compiler_params=VMEM,
+    )(orbitals.reshape(512, 128), potential.reshape(64, 128))
+
+
+def tiles_kernel(proj_ref, pick_ref, tiles_ref):
+    keep = lax.broadcasted_iota(jnp.int32, (4, 8, 512), 2) % 8 == lax.broadcasted_iota(
+        jnp.int32, (4, 8, 512), 1
     )
 
     def body(i, carry):
-        rows = proj_ref[pl.ds(pl.multiple_of(i * 32, 32), 32), :]
-        spread = jnp.where(keep, rows[:, None, :], 0.0).reshape(256, 512)
+        parts = [
+            jnp.where(keep, proj_ref[i * 8 + u][:, None, :], 0.0).reshape(32, 512)
+            for u in range(8)
+        ]
+        spread = jnp.concatenate(parts, axis=0)
         pick = pick_ref[...]
         total = sum(jnp.dot(part, pick, preferred_element_type=F32) for part in split3(spread))
         tiles_ref[pl.ds(i * 8, 8), :, :, :] = total.reshape(8, 4, 8, 128)
@@ -115,16 +134,13 @@
     lax.fori_loop(0, 8, body, 0)
 
 
-def pack(orbitals, potential, proj):
+def projector_tiles(proj):
     pick = (np.arange(512)[:, None] // 8 == np.arange(128)[None, :] % 64).astype(jnp.bfloat16)
     return pl.pallas_call(
-        pack_kernel,
-        out_shape=(
-            jax.ShapeDtypeStruct((64, 16, 128), F32),
-            jax.ShapeDtypeStruct((64, 4, 8, 128), F32),
-        ),
+        tiles_kernel,
+        out_shape=jax.ShapeDtypeStruct((64, 4, 8, 128), F32),
         compiler_params=VMEM,
-    )(orbitals.reshape(512, 128), potential.reshape(64, 128), proj.reshape(256, 512), pick)
+    )(proj, pick)
 
 
 ID, SRC, ROW, UPPER, ROW_L, ON_L, ROW_U, ON_U, META = range(9)
@@ -138,8 +154,8 @@
         older_ref = pot_ref = None
     else:
         older_ref, pot_ref = refs.pop(0), refs.pop(0)
-    tiles_ref, mat_ref, mat_low_ref, ones_ref = refs[:4]
-    refs = refs[4:]
+    tiles_ref, mat_ref, mat_low_ref = refs[:3]
+    refs = refs[3:]
     out_ref = refs.pop(0)
     if first:
         pot_ref = refs.pop(0)
@@ -152,8 +168,8 @@
     zero8 = jnp.zeros((8, 128), F32)
 
     def fill(i, carry):
-        for u in range(4):
-            src = i * 4 + u
+        for u in range(FILL):
+            src = i * FILL + u
             p, o, n = prev_ref[src, 0:8, :], own_ref[src, 0:8, :], next_ref[src, 0:8, :]
             ext[src, 0:8, :] = p
             ext[src, 8:16, :] = swap(jnp.where(low, o, p))
@@ -168,50 +184,47 @@
                 pot_ref[src, 16:24, :] = swap(jnp.where(low, n, o)) + shift
         return carry
 
-    lax.fori_loop(0, 16, fill, 0)
+    lax.fori_loop(0, 64 // FILL, fill, 0)
     for t in range(3):
         for e in range(8):
             c_xu[t, e, :, :] = zero8
             c_xd[t, 64 + e, :, :] = zero8
 
-    def products(f_ref, first_tile, n_tiles):
-        def body(i, carry):
-            t = first_tile + i // 2
-            base = pl.multiple_of((i % 2) * 32, 32)
-            rows = pl.multiple_of(t * 8 + 8, 8)
-            x = f_ref[pl.ds(base, 32), pl.ds(rows, 8), :].reshape(256, 128)
-            high = x.astype(BF16)
-            rest = (x - high.astype(F32)).astype(BF16)
-            y = jnp.dot(
-                jnp.concatenate([high, rest], axis=1), mat_ref[...], preferred_element_type=F32
-            ) + jnp.dot(high, mat_low_ref[...], preferred_element_type=F32)
-            y = y.reshape(32, 8, 640)
-            c_own[t, pl.ds(base, 32), :, :] = y[:, :, 0:128]
-            c_xu[t, pl.ds(base + 8, 32), :, :] = y[:, :, 128:256]
-            c_xd[t, pl.ds(base, 32), :, :] = y[:, :, 256:384]
-            c_yu[t, pl.ds(base, 32), :, :] = y[:, :, 384:512]
-            c_yd[t, pl.ds(base, 32), :, :] = y[:, :, 512:640]
-            return carry
-
-        lax.fori_loop(0, 2 * n_tiles, body, 0)
+    def products(f_ref, tiles):
+        for t in tiles:
+            x = f_ref[:, t * 8 + 8 : t * 8 + 16, :].reshape(512, 128)
+            both = halves(x, 1)
+            m = mat_ref[...]
+            y = jnp.dot(both, jnp.concatenate([m, m], axis=0), preferred_element_type=F32)
+            y = y + jnp.dot(both[:, 0:128], mat_low_ref[...], preferred_element_type=F32)
+            y = y.reshape(64, 8, 640)
+            c_own[t, :, :, :] = y[:, :, 0:128]
+            c_xu[t, 8:72, :, :] = y[:, :, 128:256]
+            c_xd[t, 0:64, :, :] = y[:, :, 256:384]
+            c_yu[t, :, :, :] = y[:, :, 384:512]
+            c_yd[t, :, :, :] = y[:, :, 512:640]
 
     def project(f_ref):
-        def body(i, carry):
+        def chunk(i):
             found = []
             for u in range(8):
                 ii = i * 8 + u
                 w = f_ref[lists[SRC, ii], pl.ds(lists[ROW, ii], 8), :]
                 w = jnp.where(low == (lists[UPPER, ii] == 0), w, 0.0)
                 found.append(jnp.sum(tiles_ref[lists[ID, ii]] * w[None], axis=1))
-            q = jnp.concatenate(found, axis=0)
-            high = q.astype(BF16)
-            rest = (q - high.astype(F32)).astype(BF16)
-            weights[pl.ds(pl.multiple_of(i * 32, 32), 32), :] = jnp.dot(
-                jnp.concatenate([high, rest], axis=1), ones_ref[...], preferred_element_type=F32
-            )
+            return jnp.concatenate(found, axis=0)
+
+        def summed(q):
+            return dot2(q, jnp.ones((128, 128), BF16))
+
+        head = jnp.concatenate([chunk(i) for i in range(HEAD)], axis=0)
+        weights[0 : HEAD * 32, :] = summed(head)
+
+        def body(i, carry):
+            weights[pl.ds(pl.multiple_of(i * 32, 32), 32), :] = summed(chunk(i))
             return carry
 
-        lax.fori_loop(0, (count + 7) // 8, body, 0)
+        lax.fori_loop(HEAD, (count + 7) // 8, body, 0)
 
     def combine(f_ref, y_ref, older, t, coef):
         a, b = coef
@@ -243,31 +256,46 @@
         lax.fori_loop(0, 8, body, 0)
 
     def spread(y_ref, a):
+        def term(i, u, w):
+            ii = i * 8 + u
+            atom = lists[ID, ii]
+            t = zero8
+            for p in range(4):
+                t = t + (strength[p, ii] * a) * w[u * 4 + p : u * 4 + p + 1, :] * tiles_ref[atom, p]
+            return t
+
+        def add(i, u, t):
+            ii = i * 8 + u
+            src = lists[SRC, ii]
+            rows = pl.ds(lists[ROW_L, ii], 8)
+            on = jnp.logical_and(low, lists[ON_L, ii] > 0)
+            y_ref[src, rows, :] = y_ref[src, rows, :] + jnp.where(on, t, 0.0)
+            rows = pl.ds(lists[ROW_U, ii], 8)
+            on = jnp.logical_and(jnp.logical_not(low), lists[ON_U, ii] > 0)
+            y_ref[src, rows, :] = y_ref[src, rows, :] + jnp.where(on, t, 0.0)
+
+        for i in range(HEAD):
+            w = weights[i * 32 : i * 32 + 32, :]
+            terms = [term(i, u, w) for u in range(8)]
+            for u in range(8):
+                add(i, u, terms[u])
+
         def body(i, carry):
             w = weights[pl.ds(pl.multiple_of(i * 32, 32), 32), :]
+            terms = [term(i, u, w) for u in range(8)]
             for u in range(8):
-                ii = i * 8 + u
-                atom, src = lists[ID, ii], lists[SRC, ii]
-                t = zero8
-                for p in range(4):
-                    t = t + (strength[p, ii] * a) * w[u * 4 + p : u * 4 + p + 1, :] * tiles_ref[atom, p]
-                rows = pl.ds(lists[ROW_L, ii], 8)
-                on = jnp.logical_and(low, lists[ON_L, ii] > 0)
-                y_ref[src, rows, :] = y_ref[src, rows, :] + jnp.where(on, t, 0.0)
-                rows = pl.ds(lists[ROW_U, ii], 8)
-                on = jnp.logical_and(jnp.logical_not(low), lists[ON_U, ii] > 0)
-                y_ref[src, rows, :] = y_ref[src, rows, :] + jnp.where(on, t, 0.0)
+                add(i, u, terms[u])
             return carry
 
-        lax.fori_loop(0, (count + 7) // 8, body, 0)
-
-    products(ext, 0, 3)
+        lax.fori_loop(HEAD, (count + 7) // 8, body, 0)
+
+    products(ext, range(3))
     project(ext)
     for t in range(3):
         older = None if first else (lambda src, t=t: older_ref[src, t * 8 : t * 8 + 8, :])
         combine(ext, mid, older, t, coef1)
     spread(mid, coef1[0])
-    products(mid, 1, 1)
+    products(mid, (1,))
     project(mid)
     combine(mid, new, lambda src: ext[src, 16:24, :], 1, coef2)
     spread(new, coef2[0])
@@ -396,11 +424,6 @@
 
 
 def level_matrices():
-    yb, zh, x, y = cell_index((8, 2, 8, 8))
-    fine = np.stack([zh, x // 2, yb * 4 + y // 2])
-    coarse = np.stack(cell_index((2, 4, 32)))
-    down0 = placing(fine, coarse, 0.5)
-    up0 = placing(np.stack(cell_index((4, 32))), np.stack([x // 2, yb * 4 + y // 2]), 1.0)
     x, y = cell_index((16, 32))
     fine, coarse = np.stack([x // 2, y // 2]), np.stack(cell_index((8, 16)))
     down1, up1 = placing(fine, coarse, 0.5), placing(coarse, fine, 1.0)
@@ -417,25 +440,21 @@
         to_last = np.logical_and(dx == nx - 1, dy == 0)
         return [m.astype(jnp.bfloat16) for m in (own, to_next, to_last)]
 
-    def twice(m):
-        return np.concatenate([m, m], axis=0)
-
-    near1 = twice(np.concatenate(beside(4, 32, 4), axis=1))
-    near2 = twice(np.concatenate(beside(8, 16, 8), axis=1))
-    near3 = twice(beside(16, 8, 8)[0])
-    return down0, twice(up0), down1, twice(up1), down2, twice(up2), near1, near2, near3
+    near1 = np.concatenate(beside(4, 32, 4), axis=1)
+    near2 = np.concatenate(beside(8, 16, 8), axis=1)
+    near3 = beside(16, 8, 8)[0]
+    return down1, up1, down2, up2, near1, near2, near3
 
 
 def xy_products(ref, r, mat_ref, couplings, t):
     c_own, c_xu, c_xd, c_yu, c_yd = couplings
-    for base in (0, 32):
-        x = ref[base : base + 32, r : r + 8, :].reshape(256, 128)
-        y = jnp.dot(halves(x, 1), mat_ref[...], preferred_element_type=F32).reshape(32, 8, 640)
-        c_own[t, base : base + 32, :, :] = y[:, :, 0:128]
-        c_xu[t, base + 8 : base + 40, :, :] = y[:, :, 128:256]
-        c_xd[t, base : base + 32, :, :] = y[:, :, 256:384]
-        c_yu[t, base : base + 32, :, :] = y[:, :, 384:512]
-        c_yd[t, base : base + 32, :, :] = y[:, :, 512:640]
+    x = ref[:, r : r + 8, :].reshape(512, 128)
+    y = dot2(x, mat_ref[...]).reshape(64, 8, 640)
+    c_own[t, :, :, :] = y[:, :, 0:128]
+    c_xu[t, 8:72, :, :] = y[:, :, 128:256]
+    c_xd[t, 0:64, :, :] = y[:, :, 256:384]
+    c_yu[t, :, :, :] = y[:, :, 384:512]
+    c_yd[t, :, :, :] = y[:, :, 512:640]
 
 
 def xy_sum(couplings, t, xb, yb):
@@ -470,7 +489,7 @@
     return jnp.logical_and(z >= 0, z < 128)
 
 
-def relax(ref, out_ref, rows, mat_ref, couplings, update):
+def relax(ref, rows, mat_ref, couplings, update):
     for t, r in enumerate(rows):
         xy_products(ref, r, mat_ref, couplings, t)
     for t, r in enumerate(rows):
@@ -480,13 +499,13 @@
                 src = xb * 8 + yb
                 near = xy_sum(couplings, t, xb, yb)
                 near = near + ref[src, r - 1 : r + 7, :] + ref[src, r + 1 : r + 9, :]
-                out_ref[src, r : r + 8, :] = update(src, r, ref[src, r : r + 8, :], near)
+                update(src, r, ref[src, r : r + 8, :], near)
             return carry
 
         lax.fori_loop(0, 8, body, 0)
 
 
-def source_kernel(scalars, occ, own_ref, mat_ref, down_ref, f_ref, sent_ref, v, w, r0, *couplings):
+def source_kernel(scalars, occ, own_ref, mat_ref, sent_ref, v, w, r0, *couplings):
     low = lanes_low((8, 128))
     slab, occupation = scalars[0], occ[scalars[1]] / 64.0
     zero = jnp.zeros((8, 128), F32)
@@ -495,9 +514,7 @@
         for u in range(16):
             src = i * 16 + u
             y = own_ref[src]
-            o = occupation * y * y
-            f_ref[src] = o
-            o = OMEGA * o
+            o = OMEGA * (occupation * y * y)
             v[src, 0:8, :] = zero
             v[src, 8:16, :] = swap(jnp.where(low, o, 0.0))
             v[src, 16:24, :] = o
@@ -510,22 +527,15 @@
     lax.fori_loop(0, 4, fill, 0)
     clear_borders(couplings, 2)
     keep = {r: inside_slab_range(slab, r) for r in (13, 19)}
-    relax(
-        v,
-        w,
-        (13, 19),
-        mat_ref,
-        couplings,
-        lambda src, r, c, near: jnp.where(keep[r], 1.2 * c + OMEGA * near, 0.0),
-    )
-    relax(
-        w,
-        r0,
-        (14, 18),
-        mat_ref,
-        couplings,
-        lambda src, r, c, near: v[src, r : r + 8, :] * (1.0 / OMEGA) - 6.0 * c + near,
-    )
+
+    def second(src, r, c, near):
+        w[src, r : r + 8, :] = jnp.where(keep[r], 1.2 * c + OMEGA * near, 0.0)
+
+    def residual(src, r, c, near):
+        r0[src, r : r + 8, :] = v[src, r : r + 8, :] * (1.0 / OMEGA) - 6.0 * c + near
+
+    relax(v, (13, 19), mat_ref, couplings, second)
+    relax(w, (14, 18), mat_ref, couplings, residual)
     rows = []
     for xb in range(8):
         parts = []
@@ -534,7 +544,14 @@
             parts.append(r0[src, pl.ds(14, 8, stride=2), :] + r0[src, pl.ds(15, 8, stride=2), :])
         rows.append(jnp.concatenate(parts, axis=1))
     summed = jnp.concatenate(rows, axis=0)
-    coarse = jnp.dot(halves(summed, 0), down_ref[...], preferred_element_type=F32)
+
+    i = lax.broadcasted_iota(jnp.int32, (128, 256), 0)
+    o = lax.broadcasted_iota(jnp.int32, (128, 256), 1)
+    apart = (o // 128) * 1000 + o % 128 - (i // 64) * 1000 - ((i // 16) % 4) * 32 - (i % 8) // 2
+    down = [jnp.where(apart == 4 * yb, 0.5, 0.0).astype(BF16) for yb in range(8)]
+    coarse = jnp.dot(
+        halves(summed, 0), jnp.concatenate(down, axis=0), preferred_element_type=F32
+    )
     coarse = coarse[0:64] + coarse[64:128]
     below, above = [], []
     own = []
@@ -549,20 +566,17 @@
         sent_ref[e] = sent
 
 
-def source_step(scalars, occupations, own, mat, down):
+def source_step(scalars, occupations, own, near):
     smem = pl.BlockSpec(memory_space=pltpu.SMEM)
     vmem = pl.BlockSpec(memory_space=pltpu.VMEM)
     return pl.pallas_call(
         source_kernel,
-        out_shape=(
-            jax.ShapeDtypeStruct((64, 8, 128), F32),
-            jax.ShapeDtypeStruct((8, 80, 128), F32),
-        ),
-        in_specs=[smem, smem, vmem, vmem, vmem],
-        out_specs=(vmem, vmem),
+        out_shape=jax.ShapeDtypeStruct((8, 80, 128), F32),
+        in_specs=[smem, smem, vmem, vmem],
+        out_specs=vmem,
         scratch_shapes=[pltpu.VMEM((64, 40, 128), F32)] * 3 + COUPLINGS,
         compiler_params=VMEM,
-    )(scalars, occupations, own, mat, down)
+    )(scalars, occupations, own, near)
 
 
 def double_rows(scratch, value, n):
@@ -575,9 +589,7 @@
 
     def near(ref, blocks, planes, mat):
         rows = ref[:, 8 : 8 + planes, :]
-        y = jnp.dot(
-            halves(rows.reshape(blocks * planes, 128), 1), mat[...], preferred_element_type=F32
-        )
+        y = dot2(rows.reshape(blocks * planes, 128), mat[...])
         y = y.reshape(blocks, planes, -1)
         total = y[:, :, 0:128] + ref[:, 7 : 7 + planes, :] + ref[:, 9 : 9 + planes, :]
         if blocks > 1:
@@ -619,13 +631,13 @@
     for _ in range(COARSE - 1):
         sweep(v3, g3, 1, 16, near3)
     double_rows(r3, v3[:, 8:24, :], 16)
-    up = jnp.dot(halves(r3[0], 1), up2[...], preferred_element_type=F32)
+    up = dot2(r3[0], up2[...])
     for b in range(2):
         v2[b, 8:40, :] = v2[b, 8:40, :] + up[:, b * 128 : b * 128 + 128]
     for _ in range(POST):
         sweep(v2, g2, 2, 32, near2)
     double_rows(r1.at[0:2], v2[:, 8:40, :], 32)
-    up = jnp.dot(halves(r1[0:2].reshape(128, 128), 1), up1[...], preferred_element_type=F32)
+    up = dot2(r1[0:2].reshape(128, 128), up1[...])
     for b in range(8):
         part = up[(b // 4) * 64 : (b // 4) * 64 + 64, (b % 4) * 128 : (b % 4) * 128 + 128]
         v[b, 8:72, :] = v[b, 8:72, :] + part
@@ -633,13 +645,12 @@
         sweep(v, g1, 8, 64, near1)
 
 
-def finish_kernel(scalars, got_ref, prev_ref, f_ref, next_ref, y_ref, mat_ref, up_ref, *refs):
-    refs = list(refs)
-    mats, out_ref, refs = refs[:7], refs[7], refs[8:]
-    fx, va, vb, up, g, v, r1, v2, r2, v3, r3, wide = refs[:12]
-    couplings = refs[12:]
+def finish_kernel(scalars, occ, got_ref, prev_ref, y_ref, next_ref, mat_ref, *refs):
+    mats, out_ref = refs[:7], refs[7]
+    fx, va, vb, up, g, v, r1, v2, r2, v3, r3, wide = refs[8:20]
+    couplings = refs[20:]
     low = lanes_low((8, 128))
-    slab = scalars[0]
+    slab, factor = scalars[0], OMEGA * (occ[scalars[1]] / 64.0)
 
     for s in range(8):
         g[:, 8 + 8 * s : 16 + 8 * s, :] = got_ref[SLAB_DEVICE[s], 0:64, :].reshape(8, 8, 128)
@@ -653,33 +664,35 @@
                 g[xb, row : row + 1, :] = g[xb, row : row + 1, :] + got_ref[SLAB_DEVICE[s], 72 + xb : 73 + xb, :]
     coarse_solve(g, v, r1, v2, r2, v3, r3, mats)
     double_rows(wide, v[:, pl.ds(8 * slab + 4, 16), :], 16)
-    up[...] = jnp.dot(
-        halves(wide[...].reshape(256, 128), 1), up_ref[...], preferred_element_type=F32
-    ).reshape(8, 32, 1024)
+    i = lax.broadcasted_iota(jnp.int32, (128, 128), 0)
+    o = lax.broadcasted_iota(jnp.int32, (128, 128), 1)
+    apart = i - ((o // 16) % 4) * 32 - (o % 8) // 2
+    spread = jnp.concatenate(
+        [jnp.where(apart == 4 * yb, 1.0, 0.0).astype(BF16) for yb in range(8)], axis=1
+    )
+    up[...] = dot2(wide[...].reshape(256, 128), spread).reshape(8, 32, 1024)
 
     def fill(i, carry):
         for u in range(16):
             src = i * 16 + u
-            p, o, n = prev_ref[src], f_ref[src], next_ref[src]
-            fx[src, 8:16, :] = OMEGA * swap(jnp.where(low, o, p))
-            fx[src, 16:24, :] = OMEGA * o
-            fx[src, 24:32, :] = OMEGA * swap(jnp.where(low, n, o))
+            p, o, n = (factor * jnp.square(ref[src]) for ref in (prev_ref, y_ref, next_ref))
+            fx[src, 8:16, :] = swap(jnp.where(low, o, p))
+            fx[src, 16:24, :] = o
+            fx[src, 24:32, :] = swap(jnp.where(low, n, o))
+            out_ref[src, 0:8, :] = y_ref[src]
         return carry
 
     lax.fori_loop(0, 4, fill, 0)
     clear_borders(couplings, 2)
     keep = {r: inside_slab_range(slab, r) for r in (14, 18, 15, 17)}
 
-    def to_third(src, r, c, near):
-        return jnp.where(keep[r], 1.2 * c + OMEGA * near, 0.0)
-
-    relax(fx, va, (14, 18), mat_ref, couplings, to_third)
+    def second(src, r, c, near):
+        va[src, r : r + 8, :] = jnp.where(keep[r], 1.2 * c + OMEGA * near, 0.0)
 
     def add_up(xb, carry):
         for yb in range(8):
             src = xb * 8 + yb
-            for r in (14, 22):
-                n = 8 if r == 14 else 4
+            for r, n in ((14, 8), (22, 4)):
                 e = jnp.where(
                     lanes_low((n, 128)),
                     up[xb, r - 8 : r - 8 + n, yb * 128 : yb * 128 + 128],
@@ -688,38 +701,34 @@
                 va[src, r : r + n, :] = va[src, r : r + n, :] + e
         return carry
 
-    lax.fori_loop(0, 8, add_up, 0)
-
     def swept(src, r, c, near):
         return c + (fx[src, r : r + 8, :] - DAMPING * c + OMEGA * near)
 
-    relax(
-        va,
-        vb,
-        (15, 17),
-        mat_ref,
-        couplings,
-        lambda src, r, c, near: jnp.where(keep[r], swept(src, r, c, near), 0.0),
-    )
-    relax(vb, va, (16,), mat_ref, couplings, swept)
-    out_ref[:, 0:8, :] = y_ref[...]
-    out_ref[:, 8:16, :] = va[:, 16:24, :]
-
-
-def finish_step(scalars, got, halo, f, own, mat, levels):
+    def fourth(src, r, c, near):
+        vb[src, r : r + 8, :] = jnp.where(keep[r], swept(src, r, c, near), 0.0)
+
+    def fifth(src, r, c, near):
+        out_ref[src, 8:16, :] = swept(src, r, c, near)
+
+    relax(fx, (14, 18), mat_ref, couplings, second)
+    lax.fori_loop(0, 8, add_up, 0)
+    relax(va, (15, 17), mat_ref, couplings, fourth)
+    relax(vb, (16,), mat_ref, couplings, fifth)
+
+
+def finish_step(scalars, occupations, got, halo, own, near, levels):
     smem = pl.BlockSpec(memory_space=pltpu.SMEM)
     vmem = pl.BlockSpec(memory_space=pltpu.VMEM)
-    ins = [scalars, got, halo[0], f, halo[1], own, mat, levels[1], *levels[2:]]
-    big = pltpu.VMEM((64, 40, 128), F32)
+    ins = [scalars, occupations, got, halo[0], own, halo[1], near, *levels]
     return pl.pallas_call(
         finish_kernel,
         out_shape=jax.ShapeDtypeStruct((64, 16, 128), F32),
-        in_specs=[smem] + [vmem] * (len(ins) - 1),
+        in_specs=[smem, smem] + [vmem] * (len(ins) - 2),
         out_specs=vmem,
         scratch_shapes=[
-            big,
-            big,
-            big,
+            pltpu.VMEM((64, 40, 128), F32),
+            pltpu.VMEM((64, 40, 128), F32),
+            pltpu.VMEM((64, 40, 128), F32),
             pltpu.VMEM((8, 32, 1024), F32),
             pltpu.VMEM((8, 80, 128), F32),
             pltpu.VMEM((8, 80, 128), F32),
@@ -752,9 +761,10 @@
     slab = 2 * (xlo * (3 - ylo) + (1 - xlo) * ylo) + core
     lists, strength = atom_lists(slab, proj_strength, atom_block, atom_offset)
     high, low = coupling(HALF)
-    mats = (jnp.asarray(high), jnp.asarray(low), jnp.ones((256, 128), BF16))
-
-    packed, tiles = pack(orbitals, local_potential, proj_values)
+    mats = (jnp.asarray(high), jnp.asarray(low))
+
+    packed = pack(orbitals, local_potential)
+    tiles = projector_tiles(proj_values)
     own = lax.all_to_all(packed, PLANE, 0, 0, tiled=True)
 
     sigma = HALF_WIDTH / (0.0 - CENTER)
@@ -780,13 +790,12 @@
             older = outs.pop(0)
 
     scalars = jnp.stack([slab, 2 * lax.axis_index("yhi") + lax.axis_index("xhi")]).astype(jnp.int32)
-    near, _ = coupling((0.0, 1.0))
-    near = jnp.asarray(near)
+    near = jnp.asarray(coupling((0.0, 1.0))[0])
     levels = [jnp.asarray(m) for m in level_matrices()]
-    f, sent = source_step(scalars, occupations, own, near, levels[0])
-    halo = exchange(f, GROUP, 1, 8, SLAB_DEVICE)
+    halo = exchange(own, GROUP, 1, 8, SLAB_DEVICE)
+    sent = source_step(scalars, occupations, own, near)
     got = lax.all_to_all(sent, GROUP, 0, 0, tiled=True)
-    packed = finish_step(scalars, got, halo, f, own, near, levels)
+    packed = finish_step(scalars, occupations, got, halo, own, near, levels)
     back = lax.all_to_all(packed, PLANE, 0, 0, tiled=True)
     filtered, part = unpack(back)
     hartree = jnp.sum(lax.all_to_all(part, BAND, 0, 0, tiled=True), axis=0)

time: 188 us -> 171 us (0.910)
  Pallas kernels: 46.2 us -> 35.4 us
  waiting for transfers between devices: 44.7 us -> 38.9 us
    pallas_call x4, Pallas kernels: 31.5 us -> 20 us  [double_step(): pl.pallas_call(functools.partial(double_kernel, first, last, coef1, coef2...]
    all_to_all x1, waiting for transfers between devices: 14.9 us -> 11.2 us  [local(): own = lax.all_to_all(packed, PLANE, 0, 0, tiled=True)]
    unnamed x48 -> x46, local copies, waits for them, and re-layouts: 5.58 us -> 8.24 us
    pallas_call x2 -> x3, Pallas kernels: 7.58 us -> 8.01 us  [the longest x1 3.82 us: source_step(): pl.pallas_call(source_kernel, out_shape=jax.ShapeDtypeStruct((8, 80, 128)...]
  transfers between devices with their start and end apart: 12 -> 12, of which waited for: 11 -> 11; matrix products, arithmetic and copies ran while one was open for 2% -> 2% of each run, Pallas kernels for 0% -> 2%
where the time goes in v3:
time: 171 us; the launch traced here: 170 us
  blocking collectives  45.8 us (27%)
  waiting for transfers between devices  38.9 us (23%)
  starting transfers between devices  36.9 us (22%)
  Pallas kernels  35.4 us (21%)
  local copies, waits for them, and re-layouts  9.14 us (5%)
  other arithmetic  2.54 us (1%)
    all_to_all x1, blocking collectives, local(): back = lax.all_to_all(packed, PLANE, 0, 0, tiled=True)  23.4 us
    all_to_all x1, blocking collectives, local(): hartree = jnp.sum(lax.all_to_all(part, BAND, 0, 0, tiled=True), axis=0)  22.3 us
    pallas_call x4, Pallas kernels, double_step(): pl.pallas_call(functools.partial(double_kernel, first, last, coef1, coef2...  20 us
    ppermute x5, waiting for transfers between devices, exchange(): lax.ppermute(lax.slice_in_dim(value, length - width, length, axis=dim), a...  18.4 us
    ppermute x5, starting transfers between devices, exchange(): lax.ppermute(lax.slice_in_dim(value, 0, width, axis=dim), axes, down)  11.4 us
    ppermute x5, starting transfers between devices, exchange(): lax.ppermute(lax.slice_in_dim(value, length - width, length, axis=dim), a...  11.3 us
    all_to_all x1, waiting for transfers between devices, local(): own = lax.all_to_all(packed, PLANE, 0, 0, tiled=True)  11.2 us
    all_to_all x1, starting transfers between devices, local(): own = lax.all_to_all(packed, PLANE, 0, 0, tiled=True)  10.7 us
  transfers between devices with their start and end apart: 12, of which 11 were waited for; matrix products, arithmetic and copies ran while one was open for 2% of the time, Pallas kernels for 2%

profile of v3, /device:TPU:6, one launch (start us, length us, event | category | flops | bytes accessed | tf_op | source)
XLA Modules:
  0.0 169.7 jit_solution(16018440853066801867)
XLA Ops:
  3.5 10.7 %all-to-all-start = ((f32[64,16,128]{2,1,0:T(8,128)}), f32[64,16,128]{2,1,0:T(8,128)S(1)}, u32[]{:S(2)}, u32[]{:S(2)}) async-start(f32[64,16,128]{2,1,0:T(8,128)} %shard_map.185), calls=%async_computation | async-start | bytes 1048576 | tf_op jit(solution)/shard_map/all_to_all | solution.py:768
  17.1 3.1 %shard_map.186.refs_0_.refs_2_ = f32[64,4,8,128]{3,2,1,0:T(8,128)S(1)} custom-call(f32[64,4,512]{2,1,0:T(4,128)S(1)} %copy-done.5, bf16[512,128]{1,0:T(8,128)(2,1)S(1)} %copy-done.13), custom_call_target="tpu_custom_call" | custom-call | tf_op jit(solution)/shard_map/pallas_call | solution.py:139
  20.6 11.2 %all-to-all-done.own_ref = f32[64,16,128]{2,1,0:T(8,128)S(1)} async-done(((f32[64,16,128]{2,1,0:T(8,128)}), f32[64,16,128]{2,1,0:T(8,128)S(1)}, u32[]{:S(2)}, u32[]{:S(2)}) %all-to-all-start) | async-done | bytes 524320 | tf_op jit(solution)/shard_map/all_to_all | solution.py:768
  31.8 2.6 %collective-permute-start.1 = (f32[64,16,128]{2,1,0:T(8,128)S(1)}, f32[64,16,128]{2,1,0:T(8,128)S(1)}, u32[]{:S(2)}, u32[]{:S(2)}) collective-permute-start(f32[64,16,128]{2,1,0:T(8,128)S(1)} %all-to-all-done.own_ref), channel_id=1, source_target_pairs={{8,0},{1,8},{9,1},{3,9},{11,3},{2,11},{10,2},{12,4},{5,12},{13,5},... | collective-permute-start | bytes 1572872 | tf_op jit(solution)/shard_map/ppermute | solution.py:753
  37.2 3.9 %collective-permute-done.1.next_ref = f32[64,16,128]{2,1,0:T(8,128)S(1)} collective-permute-done((f32[64,16,128]{2,1,0:T(8,128)S(1)}, f32[64,16,128]{2,1,0:T(8,128)S(1)}, u32[]{:S(2)}, u32[]{:S(2)}) %collective-permute-start.1) | collective-permute-done | bytes 524320 | tf_op jit(solution)/shard_map/ppermute | solution.py:753
  41.1 3.8 %collective-permute-done.prev_ref = f32[64,16,128]{2,1,0:T(8,128)S(1)} collective-permute-done((f32[64,16,128]{2,1,0:T(8,128)S(1)}, f32[64,16,128]{2,1,0:T(8,128)S(1)}, u32[]{:S(2)}, u32[]{:S(2)}) %collective-permute-start) | collective-permute-done | bytes 524320 | tf_op jit(solution)/shard_map/ppermute | solution.py:752
  46.8 5.0 %shard_map.187 = (f32[64,8,128]{2,1,0:T(8,128)S(1)}, f32[64,24,128]{2,1,0:T(8,128)S(1)}, f32[64,24,128]{2,1,0:T(8,128)S(1)}) custom-call(s32[9,64]{1,0:T(8,128)S(1)} %stack.39.lists, f32[4,64]{1,0:T(4,128)S(1)} %select_reduce_fusion.strength, f32[64,16,128]{2,1,0:T(8,128)S(1)} %copy-done.4, f32[64,16,128]{2,1,0:T(8,128)S(1)} %all-to-all-done.own_ref, ...), custom_call_target="tpu_custom_call" | custom-call | tf_op jit(solution)/shard_map/pallas_call | solution.py:319
  53.7 2.4 %collective-permute-start.2 = (f32[64,8,128]{2,1,0:T(8,128)S(1)}, f32[64,8,128]{2,1,0:T(8,128)S(1)}, u32[]{:S(2)}, u32[]{:S(2)}) collective-permute-start(f32[64,8,128]{2,1,0:T(8,128)S(1)} %get-tuple-element.47.own_ref), channel_id=1, source_target_pairs={{0,8},{8,1},{1,9},{9,3},{3,11},{11,2},{2,10},{4,12},{12,5},{5,13},... | collective-permute-start | bytes 786440 | tf_op jit(solution)/shard_map/ppermute | solution.py:752
  57.6 3.8 %collective-permute-done.2.prev_ref = f32[64,8,128]{2,1,0:T(8,128)S(1)} collective-permute-done((f32[64,8,128]{2,1,0:T(8,128)S(1)}, f32[64,8,128]{2,1,0:T(8,128)S(1)}, u32[]{:S(2)}, u32[]{:S(2)}) %collective-permute-start.2) | collective-permute-done | bytes 262176 | tf_op jit(solution)/shard_map/ppermute | solution.py:752
  61.4 4.9 %shard_map.188 = (f32[64,8,128]{2,1,0:T(8,128)S(1)}, f32[64,24,128]{2,1,0:T(8,128)S(1)}) custom-call(s32[9,64]{1,0:T(8,128)S(1)} %stack.39.lists, f32[4,64]{1,0:T(4,128)S(1)} %select_reduce_fusion.strength, f32[64,8,128]{2,1,0:T(8,128)S(1)} %collective-permute-done.2.prev_ref, f32[64,8,128]{2,1,0:T(8,128)S(1)} %get-tuple-element.47.own_ref, ...), custom_call_target="tpu_custom_call" | custom-call | tf_op jit(solution)/shard_map/pallas_call | solution.py:319
  68.2 2.4 %collective-permute-start.4 = (f32[64,8,128]{2,1,0:T(8,128)S(1)}, f32[64,8,128]{2,1,0:T(8,128)S(1)}, u32[]{:S(2)}, u32[]{:S(2)}) collective-permute-start(f32[64,8,128]{2,1,0:T(8,128)S(1)} %get-tuple-element.50.own_ref), channel_id=1, source_target_pairs={{0,8},{8,1},{1,9},{9,3},{3,11},{11,2},{2,10},{4,12},{12,5},{5,13},... | collective-permute-start | bytes 786440 | tf_op jit(solution)/shard_map/ppermute | solution.py:752
  72.1 3.8 %collective-permute-done.4.prev_ref = f32[64,8,128]{2,1,0:T(8,128)S(1)} collective-permute-done((f32[64,8,128]{2,1,0:T(8,128)S(1)}, f32[64,8,128]{2,1,0:T(8,128)S(1)}, u32[]{:S(2)}, u32[]{:S(2)}) %collective-permute-start.4) | collective-permute-done | bytes 262176 | tf_op jit(solution)/shard_map/ppermute | solution.py:752
  75.9 5.0 %shard_map.189 = (f32[64,8,128]{2,1,0:T(8,128)S(1)}, f32[64,24,128]{2,1,0:T(8,128)S(1)}) custom-call(s32[9,64]{1,0:T(8,128)S(1)} %stack.39.lists, f32[4,64]{1,0:T(4,128)S(1)} %select_reduce_fusion.strength, f32[64,8,128]{2,1,0:T(8,128)S(1)} %collective-permute-done.4.prev_ref, f32[64,8,128]{2,1,0:T(8,128)S(1)} %get-tuple-element.50.own_ref, ...), custom_call_target="tpu_custom_call" | custom-call | tf_op jit(solution)/shard_map/pallas_call | solution.py:319
  82.9 2.6 %collective-permute-start.6 = (f32[64,8,128]{2,1,0:T(8,128)S(1)}, f32[64,8,128]{2,1,0:T(8,128)}, u32[]{:S(2)}, u32[]{:S(2)}) collective-permute-start(f32[64,8,128]{2,1,0:T(8,128)S(1)} %get-tuple-element.52.own_ref), channel_id=1, source_target_pairs={{0,8},{8,1},{1,9},{9,3},{3,11},{11,2},{2,10},{4,12},{12,5},{5,13},... | collective-permute-start | bytes 786440 | tf_op jit(solution)/shard_map/ppermute | solution.py:752
  87.4 3.2 %collective-permute-done.6.prev_ref = f32[64,8,128]{2,1,0:T(8,128)} collective-permute-done((f32[64,8,128]{2,1,0:T(8,128)S(1)}, f32[64,8,128]{2,1,0:T(8,128)}, u32[]{:S(2)}, u32[]{:S(2)}) %collective-permute-start.6) | collective-permute-done | bytes 262176 | tf_op jit(solution)/shard_map/ppermute | solution.py:752
  92.6 5.2 %shard_map.190.own_ref.y_ref = f32[64,8,128]{2,1,0:T(8,128)S(1)} custom-call(s32[9,64]{1,0:T(8,128)S(1)} %stack.39.lists, f32[4,64]{1,0:T(4,128)S(1)} %select_reduce_fusion.strength, f32[64,8,128]{2,1,0:T(8,128)} %collective-permute-done.6.prev_ref, f32[64,8,128]{2,1,0:T(8,128)S(1)} %copy-done.8, f32[64,8,128]{2,1,0:T(8,128)S(1)} %copy-done.10, ...), custom_call_target="tpu_custom_call" | custom-call | tf_op jit(solution)/shard_map/pallas_call | solution.py:319
  97.7 3.8 %shard_map.191 = f32[8,80,128]{2,1,0:T(8,128)} custom-call(s32[2]{0:T(128)S(1)} %pad_add_fusion.scalars, f32[8]{0:T(128)S(1)} %copy-done.20, f32[64,8,128]{2,1,0:T(8,128)S(1)} %shard_map.190.own_ref.y_ref, bf16[128,640]{1,0:T(8,128)(2,1)S(1)} %copy-done.2), custom_call_target="tpu_custom_call" | custom-call | tf_op jit(solution)/shard_map/pallas_call | solution.py:572
  101.6 3.5 %all-to-all-start.1 = ((f32[8,80,128]{2,1,0:T(8,128)}), f32[8,80,128]{2,1,0:T(8,128)S(1)}, u32[]{:S(2)}, u32[]{:S(2)}) async-start(f32[8,80,128]{2,1,0:T(8,128)} %shard_map.191), calls=%async_computation.1 | async-start | bytes 655360 | tf_op jit(solution)/shard_map/all_to_all | solution.py:797
  105.1 3.0 %collective-permute-start.9 = (f32[64,8,128]{2,1,0:T(8,128)S(1)}, f32[64,8,128]{2,1,0:T(8,128)S(1)}, u32[]{:S(2)}, u32[]{:S(2)}) collective-permute-start(f32[64,8,128]{2,1,0:T(8,128)S(1)} %shard_map.190.own_ref.y_ref), channel_id=1, source_target_pairs={{8,0},{1,8},{9,1},{3,9},{11,3},{2,11},{10,2},{12,4},{5,12},{13,5},... | collective-permute-start | bytes 786440 | tf_op jit(solution)/shard_map/ppermute | solution.py:753
  110.1 2.0 %collective-permute-done.9.next_ref = f32[64,8,128]{2,1,0:T(8,128)S(1)} collective-permute-done((f32[64,8,128]{2,1,0:T(8,128)S(1)}, f32[64,8,128]{2,1,0:T(8,128)S(1)}, u32[]{:S(2)}, u32[]{:S(2)}) %collective-permute-start.9) | collective-permute-done | bytes 262176 | tf_op jit(solution)/shard_map/ppermute | solution.py:753
  112.1 3.7 %collective-permute-done.8.prev_ref = f32[64,8,128]{2,1,0:T(8,128)S(1)} collective-permute-done((f32[64,8,128]{2,1,0:T(8,128)S(1)}, f32[64,8,128]{2,1,0:T(8,128)S(1)}, u32[]{:S(2)}, u32[]{:S(2)}) %collective-permute-start.8) | collective-permute-done | bytes 262176 | tf_op jit(solution)/shard_map/ppermute | solution.py:752
  115.9 6.4 %shard_map.192 = f32[64,16,128]{2,1,0:T(8,128)S(1)} custom-call(s32[2]{0:T(128)S(1)} %pad_add_fusion.scalars, f32[8]{0:T(128)S(1)} %copy-done.20, f32[8,80,128]{2,1,0:T(8,128)S(1)} %all-to-all-done.1.got_ref, f32[64,8,128]{2,1,0:T(8,128)S(1)} %collective-permute-done.8.prev_ref, f32[64,8,128]{2,1,0:T(8,128)S(1)} %shard_map.190.own_ref.y_ref, ...), custom_call_target="tpu_custom_call" | custom-call | tf_op jit(solution)/shard_map/pallas_call | solution.py:723
  122.3 23.4 %all_to_all.20.in_ref = f32[64,16,128]{2,1,0:T(8,128)S(1)} all-to-all(f32[64,16,128]{2,1,0:T(8,128)S(1)} %shard_map.192), channel_id=1, replica_groups=mesh['z'=8,'yhi'=4,'core'=2,'xhi'=2,'xlo'=2,'ylo'=2] {'yhi','core','xhi'..., dimensions={0} | all-to-all | bytes 1048576 | tf_op jit(solution)/shard_map/all_to_all | solution.py:799
  146.7 22.3 %all_to_all.21 = f32[8,64,128]{2,1,0:T(8,128)S(1)} all-to-all(f32[8,64,128]{2,1,0:T(8,128)S(1)} %get-tuple-element.55), channel_id=1, replica_groups=mesh['z'=8,'yhi'=4,'core'=2,'xhi'=2,'xlo'=2,'ylo'=2] {'z'}, dimensions={0} | all-to-all | bytes 524288 | tf_op jit(solution)/shard_map/all_to_all | solution.py:801
  (71 shorter events, 26.8 us)
Async XLA Ops:
  3.5 13.6 %copy-start.5 = (f32[64,4,512]{2,1,0:T(4,128)S(1)}, f32[64,4,512]{2,1,0:T(4,128)}, u32[]{:S(2)}) copy-start(f32[64,4,512]{2,1,0:T(4,128)} %proj_ref.1) | copy-start | bytes 1572868
  3.5 13.6 %copy-start.13 = (bf16[512,128]{1,0:T(8,128)(2,1)S(1)}, bf16[512,128]{1,0:T(8,128)(2,1)}, u32[]{:S(2)}) copy-start(bf16[512,128]{1,0:T(8,128)(2,1)} %constant.145.clone.pick_ref) | copy-start | bytes 393220
  3.5 28.3 %all-to-all-start = ((f32[64,16,128]{2,1,0:T(8,128)}), f32[64,16,128]{2,1,0:T(8,128)S(1)}, u32[]{:S(2)}, u32[]{:S(2)}) async-start(f32[64,16,128]{2,1,0:T(8,128)} %shard_map.185), calls=%async_computation | async-start | bytes 1048576 | tf_op jit(solution)/shard_map/all_to_all | solution.py:768
  17.1 28.6 %copy-start = (bf16[128,640]{1,0:T(8,128)(2,1)S(1)}, bf16[128,640]{1,0:T(8,128)(2,1)}, u32[]{:S(2)}) copy-start(bf16[128,640]{1,0:T(8,128)(2,1)} %constant.144.clone.refs_2_.refs_4_) | copy-start | bytes 491524
  17.1 28.6 %copy-start.1 = (bf16[128,640]{1,0:T(8,128)(2,1)S(1)}, bf16[128,640]{1,0:T(8,128)(2,1)}, u32[]{:S(2)}) copy-start(bf16[128,640]{1,0:T(8,128)(2,1)} %constant.143.clone.refs_1_.refs_3_) | copy-start | bytes 491524
  31.8 9.3 %collective-permute-start.1 = (f32[64,16,128]{2,1,0:T(8,128)S(1)}, f32[64,16,128]{2,1,0:T(8,128)S(1)}, u32[]{:S(2)}, u32[]{:S(2)}) collective-permute-start(f32[64,16,128]{2,1,0:T(8,128)S(1)} %all-to-all-done.own_ref), channel_id=1, source_target_pairs={{8,0},{1,8},{9,1},{3,9},{11,3},{2,11},{10,2},{12,4},{5,12},{13,5},... | collective-permute-start | bytes 1572872 | tf_op jit(solution)/shard_map/ppermute | solution.py:753
  34.4 10.5 %collective-permute-start = (f32[64,16,128]{2,1,0:T(8,128)S(1)}, f32[64,16,128]{2,1,0:T(8,128)S(1)}, u32[]{:S(2)}, u32[]{:S(2)}) collective-permute-start(f32[64,16,128]{2,1,0:T(8,128)S(1)} %all-to-all-done.own_ref), channel_id=1, source_target_pairs={{0,8},{8,1},{1,9},{9,3},{3,11},{11,2},{2,10},{4,12},{12,5},{5,13},... | collective-permute-start | bytes 1572872 | tf_op jit(solution)/shard_map/ppermute | solution.py:752
  51.8 5.8 %collective-permute-start.3 = (f32[64,8,128]{2,1,0:T(8,128)S(1)}, f32[64,8,128]{2,1,0:T(8,128)S(1)}, u32[]{:S(2)}, u32[]{:S(2)}) collective-permute-start(f32[64,8,128]{2,1,0:T(8,128)S(1)} %get-tuple-element.47.own_ref), channel_id=1, source_target_pairs={{8,0},{1,8},{9,1},{3,9},{11,3},{2,11},{10,2},{12,4},{5,12},{13,5},... | collective-permute-start | bytes 786440 | tf_op jit(solution)/shard_map/ppermute | solution.py:753
  53.7 7.7 %collective-permute-start.2 = (f32[64,8,128]{2,1,0:T(8,128)S(1)}, f32[64,8,128]{2,1,0:T(8,128)S(1)}, u32[]{:S(2)}, u32[]{:S(2)}) collective-permute-start(f32[64,8,128]{2,1,0:T(8,128)S(1)} %get-tuple-element.47.own_ref), channel_id=1, source_target_pairs={{0,8},{8,1},{1,9},{9,3},{3,11},{11,2},{2,10},{4,12},{12,5},{5,13},... | collective-permute-start | bytes 786440 | tf_op jit(solution)/shard_map/ppermute | solution.py:752
  66.3 5.8 %collective-permute-start.5 = (f32[64,8,128]{2,1,0:T(8,128)S(1)}, f32[64,8,128]{2,1,0:T(8,128)S(1)}, u32[]{:S(2)}, u32[]{:S(2)}) collective-permute-start(f32[64,8,128]{2,1,0:T(8,128)S(1)} %get-tuple-element.50.own_ref), channel_id=1, source_target_pairs={{8,0},{1,8},{9,1},{3,9},{11,3},{2,11},{10,2},{12,4},{5,12},{13,5},... | collective-permute-start | bytes 786440 | tf_op jit(solution)/shard_map/ppermute | solution.py:753
  68.2 7.7 %collective-permute-start.4 = (f32[64,8,128]{2,1,0:T(8,128)S(1)}, f32[64,8,128]{2,1,0:T(8,128)S(1)}, u32[]{:S(2)}, u32[]{:S(2)}) collective-permute-start(f32[64,8,128]{2,1,0:T(8,128)S(1)} %get-tuple-element.50.own_ref), channel_id=1, source_target_pairs={{0,8},{8,1},{1,9},{9,3},{3,11},{11,2},{2,10},{4,12},{12,5},{5,13},... | collective-permute-start | bytes 786440 | tf_op jit(solution)/shard_map/ppermute | solution.py:752
  80.9 5.8 %collective-permute-start.7 = (f32[64,8,128]{2,1,0:T(8,128)S(1)}, f32[64,8,128]{2,1,0:T(8,128)S(1)}, u32[]{:S(2)}, u32[]{:S(2)}) collective-permute-start(f32[64,8,128]{2,1,0:T(8,128)S(1)} %get-tuple-element.52.own_ref), channel_id=1, source_target_pairs={{8,0},{1,8},{9,1},{3,9},{11,3},{2,11},{10,2},{12,4},{5,12},{13,5},... | collective-permute-start | bytes 786440 | tf_op jit(solution)/shard_map/ppermute | solution.py:753
  82.9 7.8 %collective-permute-start.6 = (f32[64,8,128]{2,1,0:T(8,128)S(1)}, f32[64,8,128]{2,1,0:T(8,128)}, u32[]{:S(2)}, u32[]{:S(2)}) collective-permute-start(f32[64,8,128]{2,1,0:T(8,128)S(1)} %get-tuple-element.52.own_ref), channel_id=1, source_target_pairs={{0,8},{8,1},{1,9},{9,3},{3,11},{11,2},{2,10},{4,12},{12,5},{5,13},... | collective-permute-start | bytes 786440 | tf_op jit(solution)/shard_map/ppermute | solution.py:752
  92.6 5.2 %copy-start.20 = (f32[8]{0:T(128)S(1)}, f32[8]{0:T(128)}, u32[]{:S(2)}) copy-start(f32[8]{0:T(128)} %occ.3) | copy-start | bytes 100
  101.6 14.3 %copy-start.11 = (bf16[128,512]{1,0:T(8,128)(2,1)S(1)}, bf16[128,512]{1,0:T(8,128)(2,1)}, u32[]{:S(2)}) copy-start(bf16[128,512]{1,0:T(8,128)(2,1)} %constant.148.clone.refs_1_) | copy-start | bytes 393220
  101.6 14.3 %copy-start.12 = (bf16[512,128]{1,0:T(8,128)(2,1)S(1)}, bf16[512,128]{1,0:T(8,128)(2,1)}, u32[]{:S(2)}) copy-start(bf16[512,128]{1,0:T(8,128)(2,1)} %constant.147.clone.refs_0_) | copy-start | bytes 393220
  101.6 14.3 %copy-start.14 = (bf16[128,384]{1,0:T(8,128)(2,1)S(1)}, bf16[128,384]{1,0:T(8,128)(2,1)}, u32[]{:S(2)}) copy-start(bf16[128,384]{1,0:T(8,128)(2,1)} %constant.152.clone.refs_5_) | copy-start | bytes 294916
  101.6 14.3 %copy-start.15 = (bf16[128,384]{1,0:T(8,128)(2,1)S(1)}, bf16[128,384]{1,0:T(8,128)(2,1)}, u32[]{:S(2)}) copy-start(bf16[128,384]{1,0:T(8,128)(2,1)} %constant.151.clone.refs_4_) | copy-start | bytes 294916
  101.6 14.3 %copy-start.16 = (bf16[128,256]{1,0:T(8,128)(2,1)S(1)}, bf16[128,256]{1,0:T(8,128)(2,1)}, u32[]{:S(2)}) copy-start(bf16[128,256]{1,0:T(8,128)(2,1)} %constant.150.clone.refs_3_) | copy-start | bytes 196612
  101.6 14.3 %copy-start.17 = (bf16[256,128]{1,0:T(8,128)(2,1)S(1)}, bf16[256,128]{1,0:T(8,128)(2,1)}, u32[]{:S(2)}) copy-start(bf16[256,128]{1,0:T(8,128)(2,1)} %constant.149.clone.refs_2_) | copy-start | bytes 196612
  101.6 14.3 %copy-start.18 = (bf16[128,128]{1,0:T(8,128)(2,1)S(1)}, bf16[128,128]{1,0:T(8,128)(2,1)}, u32[]{:S(2)}) copy-start(bf16[128,128]{1,0:T(8,128)(2,1)} %constant.153.clone.refs_6_) | copy-start | bytes 98308
  101.6 14.3 %all-to-all-start.1 = ((f32[8,80,128]{2,1,0:T(8,128)}), f32[8,80,128]{2,1,0:T(8,128)S(1)}, u32[]{:S(2)}, u32[]{:S(2)}) async-start(f32[8,80,128]{2,1,0:T(8,128)} %shard_map.191), calls=%async_computation.1 | async-start | bytes 655360 | tf_op jit(solution)/shard_map/all_to_all | solution.py:797
  105.1 7.0 %collective-permute-start.9 = (f32[64,8,128]{2,1,0:T(8,128)S(1)}, f32[64,8,128]{2,1,0:T(8,128)S(1)}, u32[]{:S(2)}, u32[]{:S(2)}) collective-permute-start(f32[64,8,128]{2,1,0:T(8,128)S(1)} %shard_map.190.own_ref.y_ref), channel_id=1, source_target_pairs={{8,0},{1,8},{9,1},{3,9},{11,3},{2,11},{10,2},{12,4},{5,12},{13,5},... | collective-permute-start | bytes 786440 | tf_op jit(solution)/shard_map/ppermute | solution.py:753
  108.2 7.7 %collective-permute-start.8 = (f32[64,8,128]{2,1,0:T(8,128)S(1)}, f32[64,8,128]{2,1,0:T(8,128)S(1)}, u32[]{:S(2)}, u32[]{:S(2)}) collective-permute-start(f32[64,8,128]{2,1,0:T(8,128)S(1)} %shard_map.190.own_ref.y_ref), channel_id=1, source_target_pairs={{0,8},{8,1},{1,9},{9,3},{3,11},{11,2},{2,10},{4,12},{12,5},{5,13},... | collective-permute-start | bytes 786440 | tf_op jit(solution)/shard_map/ppermute | solution.py:752
  (11 other events, 13.4 us)

commit v4 on v3

--- a/solution.py
+++ b/solution.py
@@ -34,7 +34,7 @@
 CHIPS = ((0, 0), (0, 1), (1, 1), (1, 0))
 SLAB_DEVICE = [c * 4 + xl * 2 + yl for xl, yl in CHIPS for c in (0, 1)]
 VMEM = pltpu.CompilerParams(vmem_limit_bytes=12 * 1024 * 1024)
-FILL = 16
+FILL = 64
 HEAD = 3
 F32 = jnp.float32
 BF16 = jnp.bfloat16
@@ -116,6 +116,7 @@
 
 
 def tiles_kernel(proj_ref, pick_ref, tiles_ref):
+    low = lanes_low((8, 2, 8, 128))
     keep = lax.broadcasted_iota(jnp.int32, (4, 8, 512), 2) % 8 == lax.broadcasted_iota(
         jnp.int32, (4, 8, 512), 1
     )
@@ -128,7 +129,8 @@
         spread = jnp.concatenate(parts, axis=0)
         pick = pick_ref[...]
         total = sum(jnp.dot(part, pick, preferred_element_type=F32) for part in split3(spread))
-        tiles_ref[pl.ds(i * 8, 8), :, :, :] = total.reshape(8, 4, 8, 128)
+        total = total.reshape(8, 2, 2, 8, 128)
+        tiles_ref[pl.ds(i * 8, 8), :, :, :] = jnp.where(low, total[:, :, 0], total[:, :, 1])
         return carry
 
     lax.fori_loop(0, 8, body, 0)
@@ -138,7 +140,7 @@
     pick = (np.arange(512)[:, None] // 8 == np.arange(128)[None, :] % 64).astype(jnp.bfloat16)
     return pl.pallas_call(
         tiles_kernel,
-        out_shape=jax.ShapeDtypeStruct((64, 4, 8, 128), F32),
+        out_shape=jax.ShapeDtypeStruct((64, 2, 8, 128), F32),
         compiler_params=VMEM,
     )(proj, pick)
 
@@ -167,6 +169,10 @@
     above = lists[META, 2] > 0
     zero8 = jnp.zeros((8, 128), F32)
 
+    for t in range(3):
+        for e in range(8):
+            c_xu[t, e, :, :] = zero8
+            c_xd[t, 64 + e, :, :] = zero8
     def fill(i, carry):
         for u in range(FILL):
             src = i * FILL + u
@@ -185,10 +191,6 @@
         return carry
 
     lax.fori_loop(0, 64 // FILL, fill, 0)
-    for t in range(3):
-        for e in range(8):
-            c_xu[t, e, :, :] = zero8
-            c_xd[t, 64 + e, :, :] = zero8
 
     def products(f_ref, tiles):
         for t in tiles:
@@ -211,58 +213,67 @@
                 ii = i * 8 + u
                 w = f_ref[lists[SRC, ii], pl.ds(lists[ROW, ii], 8), :]
                 w = jnp.where(low == (lists[UPPER, ii] == 0), w, 0.0)
+                w = w + swap(w)
                 found.append(jnp.sum(tiles_ref[lists[ID, ii]] * w[None], axis=1))
             return jnp.concatenate(found, axis=0)
 
-        def summed(q):
-            return dot2(q, jnp.ones((128, 128), BF16))
-
+        i, o = lane_pairs(128, 128)
+        same_half = filled(i // 64 == o // 64, 1.0)
         head = jnp.concatenate([chunk(i) for i in range(HEAD)], axis=0)
-        weights[0 : HEAD * 32, :] = summed(head)
+        weights[0 : HEAD * 16, :] = dot2(head, same_half)
 
         def body(i, carry):
-            weights[pl.ds(pl.multiple_of(i * 32, 32), 32), :] = summed(chunk(i))
+            weights[pl.ds(pl.multiple_of(i * 16, 16), 16), :] = dot2(chunk(i), same_half)
             return carry
 
         lax.fori_loop(HEAD, (count + 7) // 8, body, 0)
 
-    def combine(f_ref, y_ref, older, t, coef):
+    def combine(f_ref, y_ref, older, tiles, coef):
         a, b = coef
-        r = t * 8 + 8
 
         def body(xb, carry):
             for yb in range(8):
                 src = xb * 8 + yb
-                total = c_own[t, src] + c_xu[t, src] + c_xd[t, src + 8]
-                if yb > 0:
-                    total = total + c_yu[t, src - 1]
-                if yb < 7:
-                    total = total + c_yd[t, src + 1]
-                for k in range(1, REACH + 1):
-                    total = total + HALF[k] * (
-                        f_ref[src, r + k : r + k + 8, :] + f_ref[src, r - k : r - k + 8, :]
-                    )
-                total = total + pot_ref[src, t * 8 : t * 8 + 8, :] * f_ref[src, r : r + 8, :]
-                total = a * total
-                if older is not None:
-                    total = total - b * older(src)
-                if t == 0:
-                    total = jnp.where(jnp.logical_or(below, jnp.logical_not(low)), total, 0.0)
-                if t == 2:
-                    total = jnp.where(jnp.logical_or(above, low), total, 0.0)
-                y_ref[src, r : r + 8, :] = total
+                rows = {}
+                for t in tiles:
+                    for o in range(t * 8 + 8 - REACH, t * 8 + 9 + REACH):
+                        if o not in rows:
+                            rows[o] = f_ref[src, o : o + 8, :]
+                done = []
+                for t in tiles:
+                    r = t * 8 + 8
+                    total = c_own[t, src] + c_xu[t, src] + c_xd[t, src + 8]
+                    if yb > 0:
+                        total = total + c_yu[t, src - 1]
+                    if yb < 7:
+                        total = total + c_yd[t, src + 1]
+                    for k in range(1, REACH + 1):
+                        total = total + HALF[k] * (rows[r + k] + rows[r - k])
+                    total = a * (total + pot_ref[src, t * 8 : t * 8 + 8, :] * rows[r])
+                    if older is not None:
+                        total = total - b * older(src, t)
+                    if t == 0:
+                        total = jnp.where(jnp.logical_or(below, jnp.logical_not(low)), total, 0.0)
+                    if t == 2:
+                        total = jnp.where(jnp.logical_or(above, low), total, 0.0)
+                    done.append(total)
+                for t, total in zip(tiles, done):
+                    y_ref[src, t * 8 + 8 : t * 8 + 16, :] = total
             return carry
 
         lax.fori_loop(0, 8, body, 0)
 
     def spread(y_ref, a):
+        low_row = lanes_low((1, 128))
+
         def term(i, u, w):
             ii = i * 8 + u
             atom = lists[ID, ii]
             t = zero8
-            for p in range(4):
-                t = t + (strength[p, ii] * a) * w[u * 4 + p : u * 4 + p + 1, :] * tiles_ref[atom, p]
-            return t
+            for q in range(2):
+                scale = jnp.where(low_row, strength[2 * q, ii] * a, strength[2 * q + 1, ii] * a)
+                t = t + (scale * w[u * 2 + q : u * 2 + q + 1, :]) * tiles_ref[atom, q]
+            return t + swap(t)
 
         def add(i, u, t):
             ii = i * 8 + u
@@ -275,13 +286,13 @@
             y_ref[src, rows, :] = y_ref[src, rows, :] + jnp.where(on, t, 0.0)
 
         for i in range(HEAD):
-            w = weights[i * 32 : i * 32 + 32, :]
+            w = weights[i * 16 : i * 16 + 16, :]
             terms = [term(i, u, w) for u in range(8)]
             for u in range(8):
                 add(i, u, terms[u])
 
         def body(i, carry):
-            w = weights[pl.ds(pl.multiple_of(i * 32, 32), 32), :]
+            w = weights[pl.ds(pl.multiple_of(i * 16, 16), 16), :]
             terms = [term(i, u, w) for u in range(8)]
             for u in range(8):
                 add(i, u, terms[u])
@@ -291,13 +302,12 @@
 
     products(ext, range(3))
     project(ext)
-    for t in range(3):
-        older = None if first else (lambda src, t=t: older_ref[src, t * 8 : t * 8 + 8, :])
-        combine(ext, mid, older, t, coef1)
+    older = None if first else (lambda src, t: older_ref[src, t * 8 : t * 8 + 8, :])
+    combine(ext, mid, older, (0, 1, 2), coef1)
     spread(mid, coef1[0])
     products(mid, (1,))
     project(mid)
-    combine(mid, new, lambda src: ext[src, 16:24, :], 1, coef2)
+    combine(mid, new, lambda src, t: ext[src, 16:24, :], (1,), coef2)
     spread(new, coef2[0])
     out_ref[...] = new[:, 16:24, :]
     if not last:
@@ -330,7 +340,7 @@
             pltpu.VMEM((3, 72, 8, 128), F32),
             pltpu.VMEM((3, 64, 8, 128), F32),
             pltpu.VMEM((3, 64, 8, 128), F32),
-            pltpu.VMEM((256, 128), F32),
+            pltpu.VMEM((128, 128), F32),
         ],
         compiler_params=VMEM,
     )(*ins)
@@ -414,42 +424,52 @@
 OMEGA = DAMPING / 6.0
 
 
-def cell_index(shape):
-    return np.indices(shape).reshape(len(shape), -1)
-
-
-def placing(rows, columns, weight):
-    same = np.all(rows[:, :, None] == columns[:, None, :], axis=0)
-    return (weight * same).astype(jnp.bfloat16)
-
-
-def level_matrices():
-    x, y = cell_index((16, 32))
-    fine, coarse = np.stack([x // 2, y // 2]), np.stack(cell_index((8, 16)))
-    down1, up1 = placing(fine, coarse, 0.5), placing(coarse, fine, 1.0)
-    x, y = cell_index((16, 16))
-    fine, coarse = np.stack([x // 2, y // 2]), np.stack(cell_index((16, 8)))
-    down2, up2 = placing(fine, coarse, 0.5), placing(coarse, fine, 1.0)
-
-    def beside(nx, ny, used):
-        x, y = cell_index((nx, ny))
-        dx, dy = x[None, :] - x[:, None], y[None, :] - y[:, None]
-        live = np.logical_and(x[None, :] < used, x[:, None] < used)
-        own = np.logical_and(np.abs(dx) + np.abs(dy) == 1, live)
-        to_next = np.logical_and(dx == 1 - nx, dy == 0)
-        to_last = np.logical_and(dx == nx - 1, dy == 0)
-        return [m.astype(jnp.bfloat16) for m in (own, to_next, to_last)]
-
-    near1 = np.concatenate(beside(4, 32, 4), axis=1)
-    near2 = np.concatenate(beside(8, 16, 8), axis=1)
-    near3 = beside(16, 8, 8)[0]
-    return down1, up1, down2, up2, near1, near2, near3
-
-
-def xy_products(ref, r, mat_ref, couplings, t):
+def lane_pairs(rows, columns):
+    shape = (rows, columns)
+    return lax.broadcasted_iota(jnp.int32, shape, 0), lax.broadcasted_iota(jnp.int32, shape, 1)
+
+
+def filled(where, value):
+    return jnp.where(where, value, 0.0).astype(BF16)
+
+
+def both(*conditions):
+    return functools.reduce(jnp.logical_and, conditions)
+
+
+def transfers(fine_x, fine_y, down):
+    fine, coarse = fine_x * fine_y, 128
+    i, o = lane_pairs(fine, coarse) if down else lane_pairs(coarse, fine)
+    f, c = (i, o) if down else (o, i)
+    same = both(
+        (f // fine_y) // 2 == c // (fine_y // 2), (f % fine_y) // 2 == c % (fine_y // 2)
+    )
+    return filled(same, 0.5 if down else 1.0)
+
+
+def beside(nx, ny, used):
+    i, o = lane_pairs(128, 128)
+    dx, dy = o // ny - i // ny, o % ny - i % ny
+    parts = [filled(both(jnp.abs(dx) + jnp.abs(dy) == 1, i // ny < used, o // ny < used), 1.0)]
+    if used == nx:
+        parts += [filled(both(dx == d, dy == 0), 1.0) for d in (1 - nx, nx - 1)]
+    return jnp.concatenate(parts, axis=1)
+
+
+def block_neighbours():
+    i, o = lane_pairs(128, 128)
+    half = i // 64 == o // 64
+    dx, dy = (o // 8) % 8 - (i // 8) % 8, o % 8 - i % 8
+    parts = [both(half, jnp.abs(dx) + jnp.abs(dy) == 1)]
+    parts += [both(half, dx == d, dy == 0) for d in (-7, 7)]
+    parts += [both(half, dx == 0, dy == d) for d in (-7, 7)]
+    return jnp.concatenate([filled(p, 1.0) for p in parts], axis=1)
+
+
+def xy_products(ref, r, mat, couplings, t):
     c_own, c_xu, c_xd, c_yu, c_yd = couplings
     x = ref[:, r : r + 8, :].reshape(512, 128)
-    y = dot2(x, mat_ref[...]).reshape(64, 8, 640)
+    y = dot2(x, mat).reshape(64, 8, 640)
     c_own[t, :, :, :] = y[:, :, 0:128]
     c_xu[t, 8:72, :, :] = y[:, :, 128:256]
     c_xd[t, 0:64, :, :] = y[:, :, 256:384]
@@ -489,9 +509,9 @@
     return jnp.logical_and(z >= 0, z < 128)
 
 
-def relax(ref, rows, mat_ref, couplings, update):
+def relax(ref, rows, mat, couplings, update):
     for t, r in enumerate(rows):
-        xy_products(ref, r, mat_ref, couplings, t)
+        xy_products(ref, r, mat, couplings, t)
     for t, r in enumerate(rows):
 
         def body(xb, carry, t=t, r=r):
@@ -505,7 +525,8 @@
         lax.fori_loop(0, 8, body, 0)
 
 
-def source_kernel(scalars, occ, own_ref, mat_ref, sent_ref, v, w, r0, *couplings):
+def source_kernel(scalars, occ, own_ref, sent_ref, v, w, r0, *couplings):
+    mat = block_neighbours()
     low = lanes_low((8, 128))
     slab, occupation = scalars[0], occ[scalars[1]] / 64.0
     zero = jnp.zeros((8, 128), F32)
@@ -534,8 +555,8 @@
     def residual(src, r, c, near):
         r0[src, r : r + 8, :] = v[src, r : r + 8, :] * (1.0 / OMEGA) - 6.0 * c + near
 
-    relax(v, (13, 19), mat_ref, couplings, second)
-    relax(w, (14, 18), mat_ref, couplings, residual)
+    relax(v, (13, 19), mat, couplings, second)
+    relax(w, (14, 18), mat, couplings, residual)
     rows = []
     for xb in range(8):
         parts = []
@@ -566,17 +587,17 @@
         sent_ref[e] = sent
 
 
-def source_step(scalars, occupations, own, near):
+def source_step(scalars, occupations, own):
     smem = pl.BlockSpec(memory_space=pltpu.SMEM)
     vmem = pl.BlockSpec(memory_space=pltpu.VMEM)
     return pl.pallas_call(
         source_kernel,
         out_shape=jax.ShapeDtypeStruct((8, 80, 128), F32),
-        in_specs=[smem, smem, vmem, vmem],
+        in_specs=[smem, smem, vmem],
         out_specs=vmem,
         scratch_shapes=[pltpu.VMEM((64, 40, 128), F32)] * 3 + COUPLINGS,
         compiler_params=VMEM,
-    )(scalars, occupations, own, near)
+    )(scalars, occupations, own)
 
 
 def double_rows(scratch, value, n):
@@ -584,12 +605,12 @@
     scratch[:, pl.ds(1, n, stride=2), :] = value
 
 
-def coarse_solve(g, v, r1, v2, r2, v3, r3, mats):
-    down1, up1, down2, up2, near1, near2, near3 = mats
+def coarse_solve(g, v, r1, v2, r2, v3, r3):
+    near1, near2, near3 = beside(4, 32, 4), beside(8, 16, 8), beside(16, 8, 8)
 
     def near(ref, blocks, planes, mat):
         rows = ref[:, 8 : 8 + planes, :]
-        y = dot2(rows.reshape(blocks * planes, 128), mat[...])
+        y = dot2(rows.reshape(blocks * planes, 128), mat)
         y = y.reshape(blocks, planes, -1)
         total = y[:, :, 0:128] + ref[:, 7 : 7 + planes, :] + ref[:, 9 : 9 + planes, :]
         if blocks > 1:
@@ -616,7 +637,7 @@
     r1[...] = residual(v, g1, 8, 64, near1)
     pair = r1[:, pl.ds(0, 32, stride=2), :] + r1[:, pl.ds(1, 32, stride=2), :]
     rows = [jnp.concatenate([pair[4 * b + e] for e in range(4)], axis=1) for b in range(2)]
-    d = jnp.dot(halves(jnp.concatenate(rows, axis=0), 0), down1[...], preferred_element_type=F32)
+    d = jnp.dot(halves(jnp.concatenate(rows, axis=0), 0), transfers(16, 32, True), preferred_element_type=F32)
     s2 = (d[0:64] + d[64:128]).reshape(2, 32, 128)
     g2 = lambda: s2
     v2[:, 8:40, :] = OMEGA * s2
@@ -624,20 +645,20 @@
     r2[...] = residual(v2, g2, 2, 32, near2)
     pair = r2[:, pl.ds(0, 16, stride=2), :] + r2[:, pl.ds(1, 16, stride=2), :]
     both = jnp.concatenate([pair[0], pair[1]], axis=1)
-    d = jnp.dot(halves(both, 0), down2[...], preferred_element_type=F32)
+    d = jnp.dot(halves(both, 0), transfers(16, 16, True), preferred_element_type=F32)
     s3 = (d[0:16] + d[16:32]).reshape(1, 16, 128)
     g3 = lambda: s3
     v3[:, 8:24, :] = OMEGA * s3
     for _ in range(COARSE - 1):
         sweep(v3, g3, 1, 16, near3)
     double_rows(r3, v3[:, 8:24, :], 16)
-    up = dot2(r3[0], up2[...])
+    up = dot2(r3[0], transfers(16, 16, False))
     for b in range(2):
         v2[b, 8:40, :] = v2[b, 8:40, :] + up[:, b * 128 : b * 128 + 128]
     for _ in range(POST):
         sweep(v2, g2, 2, 32, near2)
     double_rows(r1.at[0:2], v2[:, 8:40, :], 32)
-    up = dot2(r1[0:2].reshape(128, 128), up1[...])
+    up = dot2(r1[0:2].reshape(128, 128), transfers(16, 32, False))
     for b in range(8):
         part = up[(b // 4) * 64 : (b // 4) * 64 + 64, (b % 4) * 128 : (b % 4) * 128 + 128]
         v[b, 8:72, :] = v[b, 8:72, :] + part
@@ -645,10 +666,11 @@
         sweep(v, g1, 8, 64, near1)
 
 
-def finish_kernel(scalars, occ, got_ref, prev_ref, y_ref, next_ref, mat_ref, *refs):
-    mats, out_ref = refs[:7], refs[7]
-    fx, va, vb, up, g, v, r1, v2, r2, v3, r3, wide = refs[8:20]
-    couplings = refs[20:]
+def finish_kernel(scalars, occ, got_ref, prev_ref, y_ref, next_ref, *refs):
+    mat = block_neighbours()
+    out_ref = refs[0]
+    fx, va, vb, up, g, v, r1, v2, r2, v3, r3, wide = refs[1:13]
+    couplings = refs[13:]
     low = lanes_low((8, 128))
     slab, factor = scalars[0], OMEGA * (occ[scalars[1]] / 64.0)
 
@@ -662,7 +684,7 @@
             if s < 7:
                 row = 8 + 8 * s + 8
                 g[xb, row : row + 1, :] = g[xb, row : row + 1, :] + got_ref[SLAB_DEVICE[s], 72 + xb : 73 + xb, :]
-    coarse_solve(g, v, r1, v2, r2, v3, r3, mats)
+    coarse_solve(g, v, r1, v2, r2, v3, r3)
     double_rows(wide, v[:, pl.ds(8 * slab + 4, 16), :], 16)
     i = lax.broadcasted_iota(jnp.int32, (128, 128), 0)
     o = lax.broadcasted_iota(jnp.int32, (128, 128), 1)
@@ -710,16 +732,16 @@
     def fifth(src, r, c, near):
         out_ref[src, 8:16, :] = swept(src, r, c, near)
 
-    relax(fx, (14, 18), mat_ref, couplings, second)
+    relax(fx, (14, 18), mat, couplings, second)
     lax.fori_loop(0, 8, add_up, 0)
-    relax(va, (15, 17), mat_ref, couplings, fourth)
-    relax(vb, (16,), mat_ref, couplings, fifth)
-
-
-def finish_step(scalars, occupations, got, halo, own, near, levels):
+    relax(va, (15, 17), mat, couplings, fourth)
+    relax(vb, (16,), mat, couplings, fifth)
+
+
+def finish_step(scalars, occupations, got, halo, own):
     smem = pl.BlockSpec(memory_space=pltpu.SMEM)
     vmem = pl.BlockSpec(memory_space=pltpu.VMEM)
-    ins = [scalars, occupations, got, halo[0], own, halo[1], near, *levels]
+    ins = [scalars, occupations, got, halo[0], own, halo[1]]
     return pl.pallas_call(
         finish_kernel,
         out_shape=jax.ShapeDtypeStruct((64, 16, 128), F32),
@@ -790,12 +812,10 @@
             older = outs.pop(0)
 
     scalars = jnp.stack([slab, 2 * lax.axis_index("yhi") + lax.axis_index("xhi")]).astype(jnp.int32)
-    near = jnp.asarray(coupling((0.0, 1.0))[0])
-    levels = [jnp.asarray(m) for m in level_matrices()]
     halo = exchange(own, GROUP, 1, 8, SLAB_DEVICE)
-    sent = source_step(scalars, occupations, own, near)
+    sent = source_step(scalars, occupations, own)
     got = lax.all_to_all(sent, GROUP, 0, 0, tiled=True)
-    packed = finish_step(scalars, occupations, got, halo, own, near, levels)
+    packed = finish_step(scalars, occupations, got, halo, own)
     back = lax.all_to_all(packed, PLANE, 0, 0, tiled=True)
     filtered, part = unpack(back)
     hartree = jnp.sum(lax.all_to_all(part, BAND, 0, 0, tiled=True), axis=0)

time: 171 us -> 164 us (0.959)
  local copies, waits for them, and re-layouts: 9.14 us -> 3.96 us
  Pallas kernels: 35.4 us -> 33.1 us
    unnamed x46 -> x18, local copies, waits for them, and re-layouts: 8.24 us -> 3.06 us
    pallas_call x4, Pallas kernels: 20 us -> 17.5 us  [double_step(): pl.pallas_call(functools.partial(double_kernel, first, last, coef1, coef2...]
where the time goes in v4:
time: 164 us; the launch traced here: 163 us
  blocking collectives  45.7 us (28%)
  waiting for transfers between devices  40.4 us (25%)
  starting transfers between devices  36.6 us (22%)
  Pallas kernels  33.1 us (20%)
  local copies, waits for them, and re-layouts  3.96 us (2%)
  other arithmetic  2.54 us (2%)
    all_to_all x1, blocking collectives, local(): back = lax.all_to_all(packed, PLANE, 0, 0, tiled=True)  23.4 us
    all_to_all x1, blocking collectives, local(): hartree = jnp.sum(lax.all_to_all(part, BAND, 0, 0, tiled=True), axis=0)  22.3 us
    ppermute x5, waiting for transfers between devices, exchange(): lax.ppermute(lax.slice_in_dim(value, length - width, length, axis=dim), a...  19 us
    pallas_call x4, Pallas kernels, double_step(): pl.pallas_call(functools.partial(double_kernel, first, last, coef1, coef2...  17.5 us
    ppermute x5, starting transfers between devices, exchange(): lax.ppermute(lax.slice_in_dim(value, 0, width, axis=dim), axes, down)  11.4 us
    all_to_all x1, waiting for transfers between devices, local(): own = lax.all_to_all(packed, PLANE, 0, 0, tiled=True)  11.2 us
    ppermute x5, starting transfers between devices, exchange(): lax.ppermute(lax.slice_in_dim(value, length - width, length, axis=dim), a...  11.1 us
    all_to_all x1, starting transfers between devices, local(): own = lax.all_to_all(packed, PLANE, 0, 0, tiled=True)  10.7 us
  transfers between devices with their start and end apart: 12, of which 11 were waited for; matrix products, arithmetic and copies ran while one was open for 2% of the time, Pallas kernels for 2%

profile of v4, /device:TPU:6, one launch (start us, length us, event | category | flops | bytes accessed | tf_op | source)
XLA Modules:
  0.0 163.2 jit_solution(7364741650360835452)
XLA Ops:
  3.5 10.7 %all-to-all-start = ((f32[64,16,128]{2,1,0:T(8,128)}), f32[64,16,128]{2,1,0:T(8,128)S(1)}, u32[]{:S(2)}, u32[]{:S(2)}) async-start(f32[64,16,128]{2,1,0:T(8,128)} %shard_map.113), calls=%async_computation | async-start | bytes 1048576 | tf_op jit(solution)/shard_map/all_to_all | solution.py:790
  17.1 3.1 %shard_map.114.refs_0_.refs_2_ = f32[64,2,8,128]{3,2,1,0:T(8,128)S(1)} custom-call(f32[64,4,512]{2,1,0:T(4,128)S(1)} %copy-done.2, bf16[512,128]{1,0:T(8,128)(2,1)S(1)} %copy-done.4), custom_call_target="tpu_custom_call" | custom-call | tf_op jit(solution)/shard_map/pallas_call | solution.py:141
  20.6 11.2 %all-to-all-done.own_ref = f32[64,16,128]{2,1,0:T(8,128)S(1)} async-done(((f32[64,16,128]{2,1,0:T(8,128)}), f32[64,16,128]{2,1,0:T(8,128)S(1)}, u32[]{:S(2)}, u32[]{:S(2)}) %all-to-all-start) | async-done | bytes 524320 | tf_op jit(solution)/shard_map/all_to_all | solution.py:790
  31.8 2.6 %collective-permute-start.1 = (f32[64,16,128]{2,1,0:T(8,128)S(1)}, f32[64,16,128]{2,1,0:T(8,128)S(1)}, u32[]{:S(2)}, u32[]{:S(2)}) collective-permute-start(f32[64,16,128]{2,1,0:T(8,128)S(1)} %all-to-all-done.own_ref), channel_id=1, source_target_pairs={{8,0},{1,8},{9,1},{3,9},{11,3},{2,11},{10,2},{12,4},{5,12},{13,5},... | collective-permute-start | bytes 1572872 | tf_op jit(solution)/shard_map/ppermute | solution.py:775
  37.2 3.9 %collective-permute-done.1.next_ref = f32[64,16,128]{2,1,0:T(8,128)S(1)} collective-permute-done((f32[64,16,128]{2,1,0:T(8,128)S(1)}, f32[64,16,128]{2,1,0:T(8,128)S(1)}, u32[]{:S(2)}, u32[]{:S(2)}) %collective-permute-start.1) | collective-permute-done | bytes 524320 | tf_op jit(solution)/shard_map/ppermute | solution.py:775
  41.1 3.8 %collective-permute-done.prev_ref = f32[64,16,128]{2,1,0:T(8,128)S(1)} collective-permute-done((f32[64,16,128]{2,1,0:T(8,128)S(1)}, f32[64,16,128]{2,1,0:T(8,128)S(1)}, u32[]{:S(2)}, u32[]{:S(2)}) %collective-permute-start) | collective-permute-done | bytes 524320 | tf_op jit(solution)/shard_map/ppermute | solution.py:774
  44.9 4.3 %shard_map.115 = (f32[64,8,128]{2,1,0:T(8,128)S(1)}, f32[64,24,128]{2,1,0:T(8,128)S(1)}, f32[64,24,128]{2,1,0:T(8,128)S(1)}) custom-call(s32[9,64]{1,0:T(8,128)S(1)} %stack.39.lists, f32[4,64]{1,0:T(4,128)S(1)} %select_reduce_fusion.strength, f32[64,16,128]{2,1,0:T(8,128)S(1)} %collective-permute-done.prev_ref, f32[64,16,128]{2,1,0:T(8,128)S(1)} %all-to-all-done.own_ref, ...), custom_call_target="tpu_custom_call" | custom-call | tf_op jit(solution)/shard_map/pallas_call | solution.py:329
  51.2 2.4 %collective-permute-start.2 = (f32[64,8,128]{2,1,0:T(8,128)S(1)}, f32[64,8,128]{2,1,0:T(8,128)S(1)}, u32[]{:S(2)}, u32[]{:S(2)}) collective-permute-start(f32[64,8,128]{2,1,0:T(8,128)S(1)} %get-tuple-element.47.own_ref), channel_id=1, source_target_pairs={{0,8},{8,1},{1,9},{9,3},{3,11},{11,2},{2,10},{4,12},{12,5},{5,13},... | collective-permute-start | bytes 786440 | tf_op jit(solution)/shard_map/ppermute | solution.py:774
  55.1 3.8 %collective-permute-done.2.prev_ref = f32[64,8,128]{2,1,0:T(8,128)S(1)} collective-permute-done((f32[64,8,128]{2,1,0:T(8,128)S(1)}, f32[64,8,128]{2,1,0:T(8,128)S(1)}, u32[]{:S(2)}, u32[]{:S(2)}) %collective-permute-start.2) | collective-permute-done | bytes 262176 | tf_op jit(solution)/shard_map/ppermute | solution.py:774
  58.9 4.4 %shard_map.116 = (f32[64,8,128]{2,1,0:T(8,128)S(1)}, f32[64,24,128]{2,1,0:T(8,128)S(1)}) custom-call(s32[9,64]{1,0:T(8,128)S(1)} %stack.39.lists, f32[4,64]{1,0:T(4,128)S(1)} %select_reduce_fusion.strength, f32[64,8,128]{2,1,0:T(8,128)S(1)} %collective-permute-done.2.prev_ref, f32[64,8,128]{2,1,0:T(8,128)S(1)} %get-tuple-element.47.own_ref, ...), custom_call_target="tpu_custom_call" | custom-call | tf_op jit(solution)/shard_map/pallas_call | solution.py:329
  65.2 2.4 %collective-permute-start.4 = (f32[64,8,128]{2,1,0:T(8,128)S(1)}, f32[64,8,128]{2,1,0:T(8,128)S(1)}, u32[]{:S(2)}, u32[]{:S(2)}) collective-permute-start(f32[64,8,128]{2,1,0:T(8,128)S(1)} %get-tuple-element.50.own_ref), channel_id=1, source_target_pairs={{0,8},{8,1},{1,9},{9,3},{3,11},{11,2},{2,10},{4,12},{12,5},{5,13},... | collective-permute-start | bytes 786440 | tf_op jit(solution)/shard_map/ppermute | solution.py:774
  69.1 3.8 %collective-permute-done.4.prev_ref = f32[64,8,128]{2,1,0:T(8,128)S(1)} collective-permute-done((f32[64,8,128]{2,1,0:T(8,128)S(1)}, f32[64,8,128]{2,1,0:T(8,128)S(1)}, u32[]{:S(2)}, u32[]{:S(2)}) %collective-permute-start.4) | collective-permute-done | bytes 262176 | tf_op jit(solution)/shard_map/ppermute | solution.py:774
  72.9 4.4 %shard_map.117 = (f32[64,8,128]{2,1,0:T(8,128)S(1)}, f32[64,24,128]{2,1,0:T(8,128)S(1)}) custom-call(s32[9,64]{1,0:T(8,128)S(1)} %stack.39.lists, f32[4,64]{1,0:T(4,128)S(1)} %select_reduce_fusion.strength, f32[64,8,128]{2,1,0:T(8,128)S(1)} %collective-permute-done.4.prev_ref, f32[64,8,128]{2,1,0:T(8,128)S(1)} %get-tuple-element.50.own_ref, ...), custom_call_target="tpu_custom_call" | custom-call | tf_op jit(solution)/shard_map/pallas_call | solution.py:329
  79.3 2.4 %collective-permute-start.6 = (f32[64,8,128]{2,1,0:T(8,128)S(1)}, f32[64,8,128]{2,1,0:T(8,128)S(1)}, u32[]{:S(2)}, u32[]{:S(2)}) collective-permute-start(f32[64,8,128]{2,1,0:T(8,128)S(1)} %get-tuple-element.52.own_ref), channel_id=1, source_target_pairs={{0,8},{8,1},{1,9},{9,3},{3,11},{11,2},{2,10},{4,12},{12,5},{5,13},... | collective-permute-start | bytes 786440 | tf_op jit(solution)/shard_map/ppermute | solution.py:774
  83.2 3.8 %collective-permute-done.6.prev_ref = f32[64,8,128]{2,1,0:T(8,128)S(1)} collective-permute-done((f32[64,8,128]{2,1,0:T(8,128)S(1)}, f32[64,8,128]{2,1,0:T(8,128)S(1)}, u32[]{:S(2)}, u32[]{:S(2)}) %collective-permute-start.6) | collective-permute-done | bytes 262176 | tf_op jit(solution)/shard_map/ppermute | solution.py:774
  87.0 4.3 %shard_map.118.own_ref.y_ref = f32[64,8,128]{2,1,0:T(8,128)S(1)} custom-call(s32[9,64]{1,0:T(8,128)S(1)} %stack.39.lists, f32[4,64]{1,0:T(4,128)S(1)} %select_reduce_fusion.strength, f32[64,8,128]{2,1,0:T(8,128)S(1)} %collective-permute-done.6.prev_ref, f32[64,8,128]{2,1,0:T(8,128)S(1)} %get-tuple-element.52.own_ref, ...), custom_call_target="tpu_custom_call" | custom-call | tf_op jit(solution)/shard_map/pallas_call | solution.py:329
  91.3 4.0 %shard_map.119 = f32[8,80,128]{2,1,0:T(8,128)} custom-call(s32[2]{0:T(128)S(1)} %pad_add_fusion.scalars, f32[8]{0:T(128)S(1)} %copy-done.6, f32[64,8,128]{2,1,0:T(8,128)S(1)} %shard_map.118.own_ref.y_ref), custom_call_target="tpu_custom_call" | custom-call | tf_op jit(solution)/shard_map/pallas_call | solution.py:593
  95.3 3.4 %all-to-all-start.1 = ((f32[8,80,128]{2,1,0:T(8,128)}), f32[8,80,128]{2,1,0:T(8,128)S(1)}, u32[]{:S(2)}, u32[]{:S(2)}) async-start(f32[8,80,128]{2,1,0:T(8,128)} %shard_map.119), calls=%async_computation.1 | async-start | bytes 655360 | tf_op jit(solution)/shard_map/all_to_all | solution.py:817
  98.7 3.0 %collective-permute-start.9 = (f32[64,8,128]{2,1,0:T(8,128)S(1)}, f32[64,8,128]{2,1,0:T(8,128)S(1)}, u32[]{:S(2)}, u32[]{:S(2)}) collective-permute-start(f32[64,8,128]{2,1,0:T(8,128)S(1)} %shard_map.118.own_ref.y_ref), channel_id=1, source_target_pairs={{8,0},{1,8},{9,1},{3,9},{11,3},{2,11},{10,2},{12,4},{5,12},{13,5},... | collective-permute-start | bytes 786440 | tf_op jit(solution)/shard_map/ppermute | solution.py:775
  103.7 2.0 %collective-permute-done.9.next_ref = f32[64,8,128]{2,1,0:T(8,128)S(1)} collective-permute-done((f32[64,8,128]{2,1,0:T(8,128)S(1)}, f32[64,8,128]{2,1,0:T(8,128)S(1)}, u32[]{:S(2)}, u32[]{:S(2)}) %collective-permute-start.9) | collective-permute-done | bytes 262176 | tf_op jit(solution)/shard_map/ppermute | solution.py:775
  105.7 3.7 %collective-permute-done.8.prev_ref = f32[64,8,128]{2,1,0:T(8,128)S(1)} collective-permute-done((f32[64,8,128]{2,1,0:T(8,128)S(1)}, f32[64,8,128]{2,1,0:T(8,128)S(1)}, u32[]{:S(2)}, u32[]{:S(2)}) %collective-permute-start.8) | collective-permute-done | bytes 262176 | tf_op jit(solution)/shard_map/ppermute | solution.py:774
  109.4 6.4 %shard_map.120 = f32[64,16,128]{2,1,0:T(8,128)S(1)} custom-call(s32[2]{0:T(128)S(1)} %pad_add_fusion.scalars, f32[8]{0:T(128)S(1)} %copy-done.6, f32[8,80,128]{2,1,0:T(8,128)S(1)} %all-to-all-done.1.got_ref, f32[64,8,128]{2,1,0:T(8,128)S(1)} %collective-permute-done.8.prev_ref, f32[64,8,128]{2,1,0:T(8,128)S(1)} %shard_map.118.own_ref.y_ref, ...), custom_call_target="tpu_custom_call" | custom-call | tf_op jit(solution)/shard_map/pallas_call | solution.py:745
  115.9 23.4 %all_to_all.20.in_ref = f32[64,16,128]{2,1,0:T(8,128)S(1)} all-to-all(f32[64,16,128]{2,1,0:T(8,128)S(1)} %shard_map.120), channel_id=1, replica_groups=mesh['z'=8,'yhi'=4,'core'=2,'xhi'=2,'xlo'=2,'ylo'=2] {'yhi','core','xhi'..., dimensions={0} | all-to-all | bytes 1048576 | tf_op jit(solution)/shard_map/all_to_all | solution.py:819
  140.2 22.3 %all_to_all.21 = f32[8,64,128]{2,1,0:T(8,128)S(1)} all-to-all(f32[8,64,128]{2,1,0:T(8,128)S(1)} %get-tuple-element.55), channel_id=1, replica_groups=mesh['z'=8,'yhi'=4,'core'=2,'xhi'=2,'xlo'=2,'ylo'=2] {'z'}, dimensions={0} | all-to-all | bytes 524288 | tf_op jit(solution)/shard_map/all_to_all | solution.py:821
  (43 shorter events, 22.4 us)
Async XLA Ops:
  0.6 1.0 copy-start.3
  1.6 0.8 copy-start.5
  3.5 13.6 %copy-start.2 = (f32[64,4,512]{2,1,0:T(4,128)S(1)}, f32[64,4,512]{2,1,0:T(4,128)}, u32[]{:S(2)}) copy-start(f32[64,4,512]{2,1,0:T(4,128)} %proj_ref.1) | copy-start | bytes 1572868
  3.5 13.6 %copy-start.4 = (bf16[512,128]{1,0:T(8,128)(2,1)S(1)}, bf16[512,128]{1,0:T(8,128)(2,1)}, u32[]{:S(2)}) copy-start(bf16[512,128]{1,0:T(8,128)(2,1)} %constant.129.clone.pick_ref) | copy-start | bytes 393220
  3.5 28.3 %all-to-all-start = ((f32[64,16,128]{2,1,0:T(8,128)}), f32[64,16,128]{2,1,0:T(8,128)S(1)}, u32[]{:S(2)}, u32[]{:S(2)}) async-start(f32[64,16,128]{2,1,0:T(8,128)} %shard_map.113), calls=%async_computation | async-start | bytes 1048576 | tf_op jit(solution)/shard_map/all_to_all | solution.py:790
  14.2 0.7 copy-start.8
  17.1 27.8 %copy-start = (bf16[128,640]{1,0:T(8,128)(2,1)S(1)}, bf16[128,640]{1,0:T(8,128)(2,1)}, u32[]{:S(2)}) copy-start(bf16[128,640]{1,0:T(8,128)(2,1)} %constant.128.clone.refs_2_.refs_4_) | copy-start | bytes 491524
  17.1 27.8 %copy-start.1 = (bf16[128,640]{1,0:T(8,128)(2,1)S(1)}, bf16[128,640]{1,0:T(8,128)(2,1)}, u32[]{:S(2)}) copy-start(bf16[128,640]{1,0:T(8,128)(2,1)} %constant.127.clone.refs_1_.refs_3_) | copy-start | bytes 491524
  31.8 9.3 %collective-permute-start.1 = (f32[64,16,128]{2,1,0:T(8,128)S(1)}, f32[64,16,128]{2,1,0:T(8,128)S(1)}, u32[]{:S(2)}, u32[]{:S(2)}) collective-permute-start(f32[64,16,128]{2,1,0:T(8,128)S(1)} %all-to-all-done.own_ref), channel_id=1, source_target_pairs={{8,0},{1,8},{9,1},{3,9},{11,3},{2,11},{10,2},{12,4},{5,12},{13,5},... | collective-permute-start | bytes 1572872 | tf_op jit(solution)/shard_map/ppermute | solution.py:775
  34.4 10.5 %collective-permute-start = (f32[64,16,128]{2,1,0:T(8,128)S(1)}, f32[64,16,128]{2,1,0:T(8,128)S(1)}, u32[]{:S(2)}, u32[]{:S(2)}) collective-permute-start(f32[64,16,128]{2,1,0:T(8,128)S(1)} %all-to-all-done.own_ref), channel_id=1, source_target_pairs={{0,8},{8,1},{1,9},{9,3},{3,11},{11,2},{2,10},{4,12},{12,5},{5,13},... | collective-permute-start | bytes 1572872 | tf_op jit(solution)/shard_map/ppermute | solution.py:774
  36.4 0.7 copy-start.7
  49.3 5.8 %collective-permute-start.3 = (f32[64,8,128]{2,1,0:T(8,128)S(1)}, f32[64,8,128]{2,1,0:T(8,128)S(1)}, u32[]{:S(2)}, u32[]{:S(2)}) collective-permute-start(f32[64,8,128]{2,1,0:T(8,128)S(1)} %get-tuple-element.47.own_ref), channel_id=1, source_target_pairs={{8,0},{1,8},{9,1},{3,9},{11,3},{2,11},{10,2},{12,4},{5,12},{13,5},... | collective-permute-start | bytes 786440 | tf_op jit(solution)/shard_map/ppermute | solution.py:775
  51.2 7.7 %collective-permute-start.2 = (f32[64,8,128]{2,1,0:T(8,128)S(1)}, f32[64,8,128]{2,1,0:T(8,128)S(1)}, u32[]{:S(2)}, u32[]{:S(2)}) collective-permute-start(f32[64,8,128]{2,1,0:T(8,128)S(1)} %get-tuple-element.47.own_ref), channel_id=1, source_target_pairs={{0,8},{8,1},{1,9},{9,3},{3,11},{11,2},{2,10},{4,12},{12,5},{5,13},... | collective-permute-start | bytes 786440 | tf_op jit(solution)/shard_map/ppermute | solution.py:774
  63.3 5.8 %collective-permute-start.5 = (f32[64,8,128]{2,1,0:T(8,128)S(1)}, f32[64,8,128]{2,1,0:T(8,128)S(1)}, u32[]{:S(2)}, u32[]{:S(2)}) collective-permute-start(f32[64,8,128]{2,1,0:T(8,128)S(1)} %get-tuple-element.50.own_ref), channel_id=1, source_target_pairs={{8,0},{1,8},{9,1},{3,9},{11,3},{2,11},{10,2},{12,4},{5,12},{13,5},... | collective-permute-start | bytes 786440 | tf_op jit(solution)/shard_map/ppermute | solution.py:775
  65.2 7.7 %collective-permute-start.4 = (f32[64,8,128]{2,1,0:T(8,128)S(1)}, f32[64,8,128]{2,1,0:T(8,128)S(1)}, u32[]{:S(2)}, u32[]{:S(2)}) collective-permute-start(f32[64,8,128]{2,1,0:T(8,128)S(1)} %get-tuple-element.50.own_ref), channel_id=1, source_target_pairs={{0,8},{8,1},{1,9},{9,3},{3,11},{11,2},{2,10},{4,12},{12,5},{5,13},... | collective-permute-start | bytes 786440 | tf_op jit(solution)/shard_map/ppermute | solution.py:774
  77.4 5.8 %collective-permute-start.7 = (f32[64,8,128]{2,1,0:T(8,128)S(1)}, f32[64,8,128]{2,1,0:T(8,128)S(1)}, u32[]{:S(2)}, u32[]{:S(2)}) collective-permute-start(f32[64,8,128]{2,1,0:T(8,128)S(1)} %get-tuple-element.52.own_ref), channel_id=1, source_target_pairs={{8,0},{1,8},{9,1},{3,9},{11,3},{2,11},{10,2},{12,4},{5,12},{13,5},... | collective-permute-start | bytes 786440 | tf_op jit(solution)/shard_map/ppermute | solution.py:775
  79.3 7.7 %collective-permute-start.6 = (f32[64,8,128]{2,1,0:T(8,128)S(1)}, f32[64,8,128]{2,1,0:T(8,128)S(1)}, u32[]{:S(2)}, u32[]{:S(2)}) collective-permute-start(f32[64,8,128]{2,1,0:T(8,128)S(1)} %get-tuple-element.52.own_ref), channel_id=1, source_target_pairs={{0,8},{8,1},{1,9},{9,3},{3,11},{11,2},{2,10},{4,12},{12,5},{5,13},... | collective-permute-start | bytes 786440 | tf_op jit(solution)/shard_map/ppermute | solution.py:774
  87.0 4.3 %copy-start.6 = (f32[8]{0:T(128)S(1)}, f32[8]{0:T(128)}, u32[]{:S(2)}) copy-start(f32[8]{0:T(128)} %occ.3) | copy-start | bytes 100
  95.3 14.1 %all-to-all-start.1 = ((f32[8,80,128]{2,1,0:T(8,128)}), f32[8,80,128]{2,1,0:T(8,128)S(1)}, u32[]{:S(2)}, u32[]{:S(2)}) async-start(f32[8,80,128]{2,1,0:T(8,128)} %shard_map.119), calls=%async_computation.1 | async-start | bytes 655360 | tf_op jit(solution)/shard_map/all_to_all | solution.py:817
  98.7 7.0 %collective-permute-start.9 = (f32[64,8,128]{2,1,0:T(8,128)S(1)}, f32[64,8,128]{2,1,0:T(8,128)S(1)}, u32[]{:S(2)}, u32[]{:S(2)}) collective-permute-start(f32[64,8,128]{2,1,0:T(8,128)S(1)} %shard_map.118.own_ref.y_ref), channel_id=1, source_target_pairs={{8,0},{1,8},{9,1},{3,9},{11,3},{2,11},{10,2},{12,4},{5,12},{13,5},... | collective-permute-start | bytes 786440 | tf_op jit(solution)/shard_map/ppermute | solution.py:775
  101.7 7.7 %collective-permute-start.8 = (f32[64,8,128]{2,1,0:T(8,128)S(1)}, f32[64,8,128]{2,1,0:T(8,128)S(1)}, u32[]{:S(2)}, u32[]{:S(2)}) collective-permute-start(f32[64,8,128]{2,1,0:T(8,128)S(1)} %shard_map.118.own_ref.y_ref), channel_id=1, source_target_pairs={{0,8},{8,1},{1,9},{9,3},{3,11},{11,2},{2,10},{4,12},{12,5},{5,13},... | collective-permute-start | bytes 786440 | tf_op jit(solution)/shard_map/ppermute | solution.py:774

commit v5 on v4

--- a/solution.py
+++ b/solution.py
@@ -34,7 +34,6 @@
 CHIPS = ((0, 0), (0, 1), (1, 1), (1, 0))
 SLAB_DEVICE = [c * 4 + xl * 2 + yl for xl, yl in CHIPS for c in (0, 1)]
 VMEM = pltpu.CompilerParams(vmem_limit_bytes=12 * 1024 * 1024)
-FILL = 64
 HEAD = 3
 F32 = jnp.float32
 BF16 = jnp.bfloat16
@@ -145,6 +144,26 @@
     )(proj, pick)
 
 
+def keep_couplings(couplings, t, y):
+    y = y.reshape(64, 8, 640)
+    for e, ref in enumerate(couplings):
+        ref[t] = y[:, :, e * 128 : e * 128 + 128]
+
+
+def xy_sum(couplings, t, src):
+    own, from_x, to_x, from_y, to_y = couplings
+    total = own[t, src]
+    if src >= 8:
+        total = total + from_x[t, src - 8]
+    if src < 56:
+        total = total + to_x[t, src + 8]
+    if src % 8 > 0:
+        total = total + from_y[t, src - 1]
+    if src % 8 < 7:
+        total = total + to_y[t, src + 1]
+    return total
+
+
 ID, SRC, ROW, UPPER, ROW_L, ON_L, ROW_U, ON_U, META = range(9)
 
 
@@ -162,20 +181,15 @@
     if first:
         pot_ref = refs.pop(0)
     mid_ref = None if last else refs.pop(0)
-    ext, mid, new, c_own, c_xu, c_xd, c_yu, c_yd, weights = refs
+    ext, mid, new, *couplings, weights = refs
     low = lanes_low((8, 128))
     count = lists[META, 0]
     below = lists[META, 1] > 0
     above = lists[META, 2] > 0
     zero8 = jnp.zeros((8, 128), F32)
 
-    for t in range(3):
-        for e in range(8):
-            c_xu[t, e, :, :] = zero8
-            c_xd[t, 64 + e, :, :] = zero8
-    def fill(i, carry):
-        for u in range(FILL):
-            src = i * FILL + u
+    def fill():
+        for src in range(64):
             p, o, n = prev_ref[src, 0:8, :], own_ref[src, 0:8, :], next_ref[src, 0:8, :]
             ext[src, 0:8, :] = p
             ext[src, 8:16, :] = swap(jnp.where(low, o, p))
@@ -188,23 +202,16 @@
                 pot_ref[src, 0:8, :] = swap(jnp.where(low, o, p)) + shift
                 pot_ref[src, 8:16, :] = o + shift
                 pot_ref[src, 16:24, :] = swap(jnp.where(low, n, o)) + shift
-        return carry
-
-    lax.fori_loop(0, 64 // FILL, fill, 0)
+
+    fill()
 
     def products(f_ref, tiles):
         for t in tiles:
-            x = f_ref[:, t * 8 + 8 : t * 8 + 16, :].reshape(512, 128)
-            both = halves(x, 1)
+            x = halves(f_ref[:, t * 8 + 8 : t * 8 + 16, :].reshape(512, 128), 1)
             m = mat_ref[...]
-            y = jnp.dot(both, jnp.concatenate([m, m], axis=0), preferred_element_type=F32)
-            y = y + jnp.dot(both[:, 0:128], mat_low_ref[...], preferred_element_type=F32)
-            y = y.reshape(64, 8, 640)
-            c_own[t, :, :, :] = y[:, :, 0:128]
-            c_xu[t, 8:72, :, :] = y[:, :, 128:256]
-            c_xd[t, 0:64, :, :] = y[:, :, 256:384]
-            c_yu[t, :, :, :] = y[:, :, 384:512]
-            c_yd[t, :, :, :] = y[:, :, 512:640]
+            y = jnp.dot(x, jnp.concatenate([m, m], axis=0), preferred_element_type=F32)
+            y = y + jnp.dot(x[:, 0:128], mat_low_ref[...], preferred_element_type=F32)
+            keep_couplings(couplings, t, y)
 
     def project(f_ref):
         def chunk(i):
@@ -231,37 +238,25 @@
     def combine(f_ref, y_ref, older, tiles, coef):
         a, b = coef
 
-        def body(xb, carry):
-            for yb in range(8):
-                src = xb * 8 + yb
-                rows = {}
-                for t in tiles:
-                    for o in range(t * 8 + 8 - REACH, t * 8 + 9 + REACH):
-                        if o not in rows:
-                            rows[o] = f_ref[src, o : o + 8, :]
-                done = []
-                for t in tiles:
-                    r = t * 8 + 8
-                    total = c_own[t, src] + c_xu[t, src] + c_xd[t, src + 8]
-                    if yb > 0:
-                        total = total + c_yu[t, src - 1]
-                    if yb < 7:
-                        total = total + c_yd[t, src + 1]
-                    for k in range(1, REACH + 1):
-                        total = total + HALF[k] * (rows[r + k] + rows[r - k])
-                    total = a * (total + pot_ref[src, t * 8 : t * 8 + 8, :] * rows[r])
-                    if older is not None:
-                        total = total - b * older(src, t)
-                    if t == 0:
-                        total = jnp.where(jnp.logical_or(below, jnp.logical_not(low)), total, 0.0)
-                    if t == 2:
-                        total = jnp.where(jnp.logical_or(above, low), total, 0.0)
-                    done.append(total)
-                for t, total in zip(tiles, done):
-                    y_ref[src, t * 8 + 8 : t * 8 + 16, :] = total
-            return carry
-
-        lax.fori_loop(0, 8, body, 0)
+        for src in range(64):
+            rows = {}
+            for t in tiles:
+                for o in range(t * 8 + 8 - REACH, t * 8 + 9 + REACH):
+                    if o not in rows:
+                        rows[o] = f_ref[src, o : o + 8, :]
+            for t in tiles:
+                r = t * 8 + 8
+                total = xy_sum(couplings, t, src)
+                for k in range(1, REACH + 1):
+                    total = total + HALF[k] * (rows[r + k] + rows[r - k])
+                total = a * (total + pot_ref[src, t * 8 : t * 8 + 8, :] * rows[r])
+                if older is not None:
+                    total = total - b * older(src, t)
+                if t == 0:
+                    total = jnp.where(jnp.logical_or(below, jnp.logical_not(low)), total, 0.0)
+                if t == 2:
+                    total = jnp.where(jnp.logical_or(above, low), total, 0.0)
+                y_ref[src, r : r + 8, :] = total
 
     def spread(y_ref, a):
         low_row = lanes_low((1, 128))
@@ -335,11 +330,7 @@
             pltpu.VMEM((64, 40, 128), F32),
             pltpu.VMEM((64, 40, 128), F32),
             pltpu.VMEM((64, 40, 128), F32),
-            pltpu.VMEM((3, 64, 8, 128), F32),
-            pltpu.VMEM((3, 72, 8, 128), F32),
-            pltpu.VMEM((3, 72, 8, 128), F32),
-            pltpu.VMEM((3, 64, 8, 128), F32),
-            pltpu.VMEM((3, 64, 8, 128), F32),
+            *[pltpu.VMEM((3, 64, 8, 128), F32)] * 5,
             pltpu.VMEM((128, 128), F32),
         ],
         compiler_params=VMEM,
@@ -466,38 +457,7 @@
     return jnp.concatenate([filled(p, 1.0) for p in parts], axis=1)
 
 
-def xy_products(ref, r, mat, couplings, t):
-    c_own, c_xu, c_xd, c_yu, c_yd = couplings
-    x = ref[:, r : r + 8, :].reshape(512, 128)
-    y = dot2(x, mat).reshape(64, 8, 640)
-    c_own[t, :, :, :] = y[:, :, 0:128]
-    c_xu[t, 8:72, :, :] = y[:, :, 128:256]
-    c_xd[t, 0:64, :, :] = y[:, :, 256:384]
-    c_yu[t, :, :, :] = y[:, :, 384:512]
-    c_yd[t, :, :, :] = y[:, :, 512:640]
-
-
-def xy_sum(couplings, t, xb, yb):
-    c_own, c_xu, c_xd, c_yu, c_yd = couplings
-    src = xb * 8 + yb
-    total = c_own[t, src] + c_xu[t, src] + c_xd[t, src + 8]
-    if yb > 0:
-        total = total + c_yu[t, src - 1]
-    if yb < 7:
-        total = total + c_yd[t, src + 1]
-    return total
-
-
-def clear_borders(couplings, tiles):
-    zero = jnp.zeros((8, 8, 128), F32)
-    for t in range(tiles):
-        couplings[1][t, 0:8] = zero
-        couplings[2][t, 64:72] = zero
-
-
-COUPLINGS = [
-    pltpu.VMEM((2, n, 8, 128), F32) for n in (64, 72, 72, 64, 64)
-]
+COUPLINGS = [pltpu.VMEM((2, 64, 8, 128), F32)] * 5
 
 
 def inside_slab_range(slab, r):
@@ -511,18 +471,12 @@
 
 def relax(ref, rows, mat, couplings, update):
     for t, r in enumerate(rows):
-        xy_products(ref, r, mat, couplings, t)
-    for t, r in enumerate(rows):
-
-        def body(xb, carry, t=t, r=r):
-            for yb in range(8):
-                src = xb * 8 + yb
-                near = xy_sum(couplings, t, xb, yb)
-                near = near + ref[src, r - 1 : r + 7, :] + ref[src, r + 1 : r + 9, :]
-                update(src, r, ref[src, r : r + 8, :], near)
-            return carry
-
-        lax.fori_loop(0, 8, body, 0)
+        keep_couplings(couplings, t, dot2(ref[:, r : r + 8, :].reshape(512, 128), mat))
+    for src in range(64):
+        for t, r in enumerate(rows):
+            near = xy_sum(couplings, t, src)
+            near = near + ref[src, r - 1 : r + 7, :] + ref[src, r + 1 : r + 9, :]
+            update(src, r, ref[src, r : r + 8, :], near)
 
 
 def source_kernel(scalars, occ, own_ref, sent_ref, v, w, r0, *couplings):
@@ -531,9 +485,8 @@
     slab, occupation = scalars[0], occ[scalars[1]] / 64.0
     zero = jnp.zeros((8, 128), F32)
 
-    def fill(i, carry):
-        for u in range(16):
-            src = i * 16 + u
+    def fill():
+        for src in range(64):
             y = own_ref[src]
             o = OMEGA * (occupation * y * y)
             v[src, 0:8, :] = zero
@@ -543,10 +496,8 @@
             v[src, 32:40, :] = zero
             w[src, 8:16, :] = zero
             w[src, 24:32, :] = zero
-        return carry
-
-    lax.fori_loop(0, 4, fill, 0)
-    clear_borders(couplings, 2)
+
+    fill()
     keep = {r: inside_slab_range(slab, r) for r in (13, 19)}
 
     def second(src, r, c, near):
@@ -694,34 +645,28 @@
     )
     up[...] = dot2(wide[...].reshape(256, 128), spread).reshape(8, 32, 1024)
 
-    def fill(i, carry):
-        for u in range(16):
-            src = i * 16 + u
+    def fill():
+        for src in range(64):
             p, o, n = (factor * jnp.square(ref[src]) for ref in (prev_ref, y_ref, next_ref))
             fx[src, 8:16, :] = swap(jnp.where(low, o, p))
             fx[src, 16:24, :] = o
             fx[src, 24:32, :] = swap(jnp.where(low, n, o))
             out_ref[src, 0:8, :] = y_ref[src]
-        return carry
-
-    lax.fori_loop(0, 4, fill, 0)
-    clear_borders(couplings, 2)
+
+    fill()
     keep = {r: inside_slab_range(slab, r) for r in (14, 18, 15, 17)}
 
     def second(src, r, c, near):
         va[src, r : r + 8, :] = jnp.where(keep[r], 1.2 * c + OMEGA * near, 0.0)
 
-    def add_up(xb, carry):
-        for yb in range(8):
-            src = xb * 8 + yb
+    def add_up():
+        for src in range(64):
+            xb, lanes = src // 8, slice(src % 8 * 128, src % 8 * 128 + 128)
             for r, n in ((14, 8), (22, 4)):
                 e = jnp.where(
-                    lanes_low((n, 128)),
-                    up[xb, r - 8 : r - 8 + n, yb * 128 : yb * 128 + 128],
-                    up[xb, r : r + n, yb * 128 : yb * 128 + 128],
+                    lanes_low((n, 128)), up[xb, r - 8 : r - 8 + n, lanes], up[xb, r : r + n, lanes]
                 )
                 va[src, r : r + n, :] = va[src, r : r + n, :] + e
-        return carry
 
     def swept(src, r, c, near):
         return c + (fx[src, r : r + 8, :] - DAMPING * c + OMEGA * near)
@@ -733,7 +678,7 @@
         out_ref[src, 8:16, :] = swept(src, r, c, near)
 
     relax(fx, (14, 18), mat, couplings, second)
-    lax.fori_loop(0, 8, add_up, 0)
+    add_up()
     relax(va, (15, 17), mat, couplings, fourth)
     relax(vb, (16,), mat, couplings, fifth)
 

time: 164 us -> 163 us (level)
  Pallas kernels: 33.1 us -> 29.4 us
  starting transfers between devices: 36.6 us -> 38.5 us
    all_to_all x1, starting transfers between devices: 3.38 us -> 5.15 us  [local(): got = lax.all_to_all(sent, GROUP, 0, 0, tiled=True)]
where the time goes in v5:
time: 163 us
  blocking collectives  46.3 us (28%)
  waiting for transfers between devices  41.1 us (25%)
  starting transfers between devices  38.5 us (24%)
  Pallas kernels  29.4 us (18%)
  local copies, waits for them, and re-layouts  3.96 us (2%)
  other arithmetic  2.54 us (2%)
    all_to_all x1, blocking collectives, local(): back = lax.all_to_all(packed, PLANE, 0, 0, tiled=True)  24 us
    all_to_all x1, blocking collectives, local(): hartree = jnp.sum(lax.all_to_all(part, BAND, 0, 0, tiled=True), axis=0)  22.3 us
    ppermute x5, waiting for transfers between devices, exchange(): lax.ppermute(lax.slice_in_dim(value, length - width, length, axis=dim), a...  19.7 us
    pallas_call x4, Pallas kernels, double_step(): pl.pallas_call(functools.partial(double_kernel, first, last, coef1, coef2...  16.8 us
    ppermute x5, starting transfers between devices, exchange(): lax.ppermute(lax.slice_in_dim(value, 0, width, axis=dim), axes, down)  11.5 us
    all_to_all x1, waiting for transfers between devices, local(): own = lax.all_to_all(packed, PLANE, 0, 0, tiled=True)  11.2 us
    ppermute x5, starting transfers between devices, exchange(): lax.ppermute(lax.slice_in_dim(value, length - width, length, axis=dim), a...  11.1 us
    all_to_all x1, starting transfers between devices, local(): own = lax.all_to_all(packed, PLANE, 0, 0, tiled=True)  10.7 us
  transfers between devices with their start and end apart: 12, of which 11 were waited for; matrix products, arithmetic and copies ran while one was open for 2% of the time, Pallas kernels for 2%

profile of v5, /device:TPU:6, one launch (start us, length us, event | category | flops | bytes accessed | tf_op | source)
XLA Modules:
  0.0 162.6 jit_solution(13793230077071042781)
XLA Ops:
  3.5 10.7 %all-to-all-start = ((f32[64,16,128]{2,1,0:T(8,128)}), f32[64,16,128]{2,1,0:T(8,128)S(1)}, u32[]{:S(2)}, u32[]{:S(2)}) async-start(f32[64,16,128]{2,1,0:T(8,128)} %shard_map.113), calls=%async_computation | async-start | bytes 1048576 | tf_op jit(solution)/shard_map/all_to_all | solution.py:735
  17.1 3.1 %shard_map.114.refs_0_.refs_2_ = f32[64,2,8,128]{3,2,1,0:T(8,128)S(1)} custom-call(f32[64,4,512]{2,1,0:T(4,128)S(1)} %copy-done.2, bf16[512,128]{1,0:T(8,128)(2,1)S(1)} %copy-done.4), custom_call_target="tpu_custom_call" | custom-call | tf_op jit(solution)/shard_map/pallas_call | solution.py:140
  20.6 11.2 %all-to-all-done.own_ref = f32[64,16,128]{2,1,0:T(8,128)S(1)} async-done(((f32[64,16,128]{2,1,0:T(8,128)}), f32[64,16,128]{2,1,0:T(8,128)S(1)}, u32[]{:S(2)}, u32[]{:S(2)}) %all-to-all-start) | async-done | bytes 524320 | tf_op jit(solution)/shard_map/all_to_all | solution.py:735
  31.8 2.6 %collective-permute-start.1 = (f32[64,16,128]{2,1,0:T(8,128)S(1)}, f32[64,16,128]{2,1,0:T(8,128)S(1)}, u32[]{:S(2)}, u32[]{:S(2)}) collective-permute-start(f32[64,16,128]{2,1,0:T(8,128)S(1)} %all-to-all-done.own_ref), channel_id=1, source_target_pairs={{8,0},{1,8},{9,1},{3,9},{11,3},{2,11},{10,2},{12,4},{5,12},{13,5},... | collective-permute-start | bytes 1572872 | tf_op jit(solution)/shard_map/ppermute | solution.py:720
  37.2 3.9 %collective-permute-done.1.next_ref = f32[64,16,128]{2,1,0:T(8,128)S(1)} collective-permute-done((f32[64,16,128]{2,1,0:T(8,128)S(1)}, f32[64,16,128]{2,1,0:T(8,128)S(1)}, u32[]{:S(2)}, u32[]{:S(2)}) %collective-permute-start.1) | collective-permute-done | bytes 524320 | tf_op jit(solution)/shard_map/ppermute | solution.py:720
  41.1 3.8 %collective-permute-done.prev_ref = f32[64,16,128]{2,1,0:T(8,128)S(1)} collective-permute-done((f32[64,16,128]{2,1,0:T(8,128)S(1)}, f32[64,16,128]{2,1,0:T(8,128)S(1)}, u32[]{:S(2)}, u32[]{:S(2)}) %collective-permute-start) | collective-permute-done | bytes 524320 | tf_op jit(solution)/shard_map/ppermute | solution.py:719
  44.9 4.1 %shard_map.115 = (f32[64,8,128]{2,1,0:T(8,128)S(1)}, f32[64,24,128]{2,1,0:T(8,128)S(1)}, f32[64,24,128]{2,1,0:T(8,128)S(1)}) custom-call(s32[9,64]{1,0:T(8,128)S(1)} %stack.39.lists, f32[4,64]{1,0:T(4,128)S(1)} %select_reduce_fusion.strength, f32[64,16,128]{2,1,0:T(8,128)S(1)} %collective-permute-done.prev_ref, f32[64,16,128]{2,1,0:T(8,128)S(1)} %all-to-all-done.own_ref, ...), custom_call_target="tpu_custom_call" | custom-call | tf_op jit(solution)/shard_map/pallas_call | solution.py:324
  50.9 2.4 %collective-permute-start.2 = (f32[64,8,128]{2,1,0:T(8,128)S(1)}, f32[64,8,128]{2,1,0:T(8,128)S(1)}, u32[]{:S(2)}, u32[]{:S(2)}) collective-permute-start(f32[64,8,128]{2,1,0:T(8,128)S(1)} %get-tuple-element.47.own_ref), channel_id=1, source_target_pairs={{0,8},{8,1},{1,9},{9,3},{3,11},{11,2},{2,10},{4,12},{12,5},{5,13},... | collective-permute-start | bytes 786440 | tf_op jit(solution)/shard_map/ppermute | solution.py:719
  54.8 3.8 %collective-permute-done.2.prev_ref = f32[64,8,128]{2,1,0:T(8,128)S(1)} collective-permute-done((f32[64,8,128]{2,1,0:T(8,128)S(1)}, f32[64,8,128]{2,1,0:T(8,128)S(1)}, u32[]{:S(2)}, u32[]{:S(2)}) %collective-permute-start.2) | collective-permute-done | bytes 262176 | tf_op jit(solution)/shard_map/ppermute | solution.py:719
  58.6 4.2 %shard_map.116 = (f32[64,8,128]{2,1,0:T(8,128)S(1)}, f32[64,24,128]{2,1,0:T(8,128)S(1)}) custom-call(s32[9,64]{1,0:T(8,128)S(1)} %stack.39.lists, f32[4,64]{1,0:T(4,128)S(1)} %select_reduce_fusion.strength, f32[64,8,128]{2,1,0:T(8,128)S(1)} %collective-permute-done.2.prev_ref, f32[64,8,128]{2,1,0:T(8,128)S(1)} %get-tuple-element.47.own_ref, ...), custom_call_target="tpu_custom_call" | custom-call | tf_op jit(solution)/shard_map/pallas_call | solution.py:324
  64.8 2.4 %collective-permute-start.4 = (f32[64,8,128]{2,1,0:T(8,128)S(1)}, f32[64,8,128]{2,1,0:T(8,128)S(1)}, u32[]{:S(2)}, u32[]{:S(2)}) collective-permute-start(f32[64,8,128]{2,1,0:T(8,128)S(1)} %get-tuple-element.50.own_ref), channel_id=1, source_target_pairs={{0,8},{8,1},{1,9},{9,3},{3,11},{11,2},{2,10},{4,12},{12,5},{5,13},... | collective-permute-start | bytes 786440 | tf_op jit(solution)/shard_map/ppermute | solution.py:719
  68.7 3.8 %collective-permute-done.4.prev_ref = f32[64,8,128]{2,1,0:T(8,128)S(1)} collective-permute-done((f32[64,8,128]{2,1,0:T(8,128)S(1)}, f32[64,8,128]{2,1,0:T(8,128)S(1)}, u32[]{:S(2)}, u32[]{:S(2)}) %collective-permute-start.4) | collective-permute-done | bytes 262176 | tf_op jit(solution)/shard_map/ppermute | solution.py:719
  72.5 4.4 %shard_map.117 = (f32[64,8,128]{2,1,0:T(8,128)S(1)}, f32[64,24,128]{2,1,0:T(8,128)S(1)}) custom-call(s32[9,64]{1,0:T(8,128)S(1)} %stack.39.lists, f32[4,64]{1,0:T(4,128)S(1)} %select_reduce_fusion.strength, f32[64,8,128]{2,1,0:T(8,128)S(1)} %collective-permute-done.4.prev_ref, f32[64,8,128]{2,1,0:T(8,128)S(1)} %get-tuple-element.50.own_ref, ...), custom_call_target="tpu_custom_call" | custom-call | tf_op jit(solution)/shard_map/pallas_call | solution.py:324
  78.8 2.4 %collective-permute-start.6 = (f32[64,8,128]{2,1,0:T(8,128)S(1)}, f32[64,8,128]{2,1,0:T(8,128)S(1)}, u32[]{:S(2)}, u32[]{:S(2)}) collective-permute-start(f32[64,8,128]{2,1,0:T(8,128)S(1)} %get-tuple-element.52.own_ref), channel_id=1, source_target_pairs={{0,8},{8,1},{1,9},{9,3},{3,11},{11,2},{2,10},{4,12},{12,5},{5,13},... | collective-permute-start | bytes 786440 | tf_op jit(solution)/shard_map/ppermute | solution.py:719
  82.7 4.5 %collective-permute-done.6.prev_ref = f32[64,8,128]{2,1,0:T(8,128)S(1)} collective-permute-done((f32[64,8,128]{2,1,0:T(8,128)S(1)}, f32[64,8,128]{2,1,0:T(8,128)S(1)}, u32[]{:S(2)}, u32[]{:S(2)}) %collective-permute-start.6) | collective-permute-done | bytes 262176 | tf_op jit(solution)/shard_map/ppermute | solution.py:719
  87.1 4.1 %shard_map.118.own_ref.y_ref = f32[64,8,128]{2,1,0:T(8,128)S(1)} custom-call(s32[9,64]{1,0:T(8,128)S(1)} %stack.39.lists, f32[4,64]{1,0:T(4,128)S(1)} %select_reduce_fusion.strength, f32[64,8,128]{2,1,0:T(8,128)S(1)} %collective-permute-done.6.prev_ref, f32[64,8,128]{2,1,0:T(8,128)S(1)} %get-tuple-element.52.own_ref, ...), custom_call_target="tpu_custom_call" | custom-call | tf_op jit(solution)/shard_map/pallas_call | solution.py:324
  91.2 2.7 %shard_map.119 = f32[8,80,128]{2,1,0:T(8,128)} custom-call(s32[2]{0:T(128)S(1)} %pad_add_fusion.scalars, f32[8]{0:T(128)S(1)} %copy-done.6, f32[64,8,128]{2,1,0:T(8,128)S(1)} %shard_map.118.own_ref.y_ref), custom_call_target="tpu_custom_call" | custom-call | tf_op jit(solution)/shard_map/pallas_call | solution.py:544
  94.0 5.1 %all-to-all-start.1 = ((f32[8,80,128]{2,1,0:T(8,128)}), f32[8,80,128]{2,1,0:T(8,128)S(1)}, u32[]{:S(2)}, u32[]{:S(2)}) async-start(f32[8,80,128]{2,1,0:T(8,128)} %shard_map.119), calls=%async_computation.1 | async-start | bytes 655360 | tf_op jit(solution)/shard_map/all_to_all | solution.py:762
  99.1 3.1 %collective-permute-start.9 = (f32[64,8,128]{2,1,0:T(8,128)S(1)}, f32[64,8,128]{2,1,0:T(8,128)S(1)}, u32[]{:S(2)}, u32[]{:S(2)}) collective-permute-start(f32[64,8,128]{2,1,0:T(8,128)S(1)} %shard_map.118.own_ref.y_ref), channel_id=1, source_target_pairs={{8,0},{1,8},{9,1},{3,9},{11,3},{2,11},{10,2},{12,4},{5,12},{13,5},... | collective-permute-start | bytes 786440 | tf_op jit(solution)/shard_map/ppermute | solution.py:720
  104.2 2.0 %collective-permute-done.9.next_ref = f32[64,8,128]{2,1,0:T(8,128)S(1)} collective-permute-done((f32[64,8,128]{2,1,0:T(8,128)S(1)}, f32[64,8,128]{2,1,0:T(8,128)S(1)}, u32[]{:S(2)}, u32[]{:S(2)}) %collective-permute-start.9) | collective-permute-done | bytes 262176 | tf_op jit(solution)/shard_map/ppermute | solution.py:720
  106.2 3.7 %collective-permute-done.8.prev_ref = f32[64,8,128]{2,1,0:T(8,128)S(1)} collective-permute-done((f32[64,8,128]{2,1,0:T(8,128)S(1)}, f32[64,8,128]{2,1,0:T(8,128)S(1)}, u32[]{:S(2)}, u32[]{:S(2)}) %collective-permute-start.8) | collective-permute-done | bytes 262176 | tf_op jit(solution)/shard_map/ppermute | solution.py:719
  109.9 4.8 %shard_map.120 = f32[64,16,128]{2,1,0:T(8,128)S(1)} custom-call(s32[2]{0:T(128)S(1)} %pad_add_fusion.scalars, f32[8]{0:T(128)S(1)} %copy-done.6, f32[8,80,128]{2,1,0:T(8,128)S(1)} %all-to-all-done.1.got_ref, f32[64,8,128]{2,1,0:T(8,128)S(1)} %collective-permute-done.8.prev_ref, f32[64,8,128]{2,1,0:T(8,128)S(1)} %shard_map.118.own_ref.y_ref, ...), custom_call_target="tpu_custom_call" | custom-call | tf_op jit(solution)/shard_map/pallas_call | solution.py:690
  114.7 24.0 %all_to_all.20.in_ref = f32[64,16,128]{2,1,0:T(8,128)S(1)} all-to-all(f32[64,16,128]{2,1,0:T(8,128)S(1)} %shard_map.120), channel_id=1, replica_groups=mesh['z'=8,'yhi'=4,'core'=2,'xhi'=2,'xlo'=2,'ylo'=2] {'yhi','core','xhi'..., dimensions={0} | all-to-all | bytes 1048576 | tf_op jit(solution)/shard_map/all_to_all | solution.py:764
  139.6 22.3 %all_to_all.21 = f32[8,64,128]{2,1,0:T(8,128)S(1)} all-to-all(f32[8,64,128]{2,1,0:T(8,128)S(1)} %get-tuple-element.55), channel_id=1, replica_groups=mesh['z'=8,'yhi'=4,'core'=2,'xhi'=2,'xlo'=2,'ylo'=2] {'z'}, dimensions={0} | all-to-all | bytes 524288 | tf_op jit(solution)/shard_map/all_to_all | solution.py:766
  (43 shorter events, 22.4 us)
Async XLA Ops:
  0.6 1.0 copy-start.3
  1.6 0.8 copy-start.5
  3.5 13.6 %copy-start.2 = (f32[64,4,512]{2,1,0:T(4,128)S(1)}, f32[64,4,512]{2,1,0:T(4,128)}, u32[]{:S(2)}) copy-start(f32[64,4,512]{2,1,0:T(4,128)} %proj_ref.1) | copy-start | bytes 1572868
  3.5 13.6 %copy-start.4 = (bf16[512,128]{1,0:T(8,128)(2,1)S(1)}, bf16[512,128]{1,0:T(8,128)(2,1)}, u32[]{:S(2)}) copy-start(bf16[512,128]{1,0:T(8,128)(2,1)} %constant.129.clone.pick_ref) | copy-start | bytes 393220
  3.5 28.3 %all-to-all-start = ((f32[64,16,128]{2,1,0:T(8,128)}), f32[64,16,128]{2,1,0:T(8,128)S(1)}, u32[]{:S(2)}, u32[]{:S(2)}) async-start(f32[64,16,128]{2,1,0:T(8,128)} %shard_map.113), calls=%async_computation | async-start | bytes 1048576 | tf_op jit(solution)/shard_map/all_to_all | solution.py:735
  14.2 0.7 copy-start.8
  17.1 27.8 %copy-start = (bf16[128,640]{1,0:T(8,128)(2,1)S(1)}, bf16[128,640]{1,0:T(8,128)(2,1)}, u32[]{:S(2)}) copy-start(bf16[128,640]{1,0:T(8,128)(2,1)} %constant.128.clone.refs_2_.refs_4_) | copy-start | bytes 491524
  17.1 27.8 %copy-start.1 = (bf16[128,640]{1,0:T(8,128)(2,1)S(1)}, bf16[128,640]{1,0:T(8,128)(2,1)}, u32[]{:S(2)}) copy-start(bf16[128,640]{1,0:T(8,128)(2,1)} %constant.127.clone.refs_1_.refs_3_) | copy-start | bytes 491524
  31.8 9.3 %collective-permute-start.1 = (f32[64,16,128]{2,1,0:T(8,128)S(1)}, f32[64,16,128]{2,1,0:T(8,128)S(1)}, u32[]{:S(2)}, u32[]{:S(2)}) collective-permute-start(f32[64,16,128]{2,1,0:T(8,128)S(1)} %all-to-all-done.own_ref), channel_id=1, source_target_pairs={{8,0},{1,8},{9,1},{3,9},{11,3},{2,11},{10,2},{12,4},{5,12},{13,5},... | collective-permute-start | bytes 1572872 | tf_op jit(solution)/shard_map/ppermute | solution.py:720
  34.4 10.5 %collective-permute-start = (f32[64,16,128]{2,1,0:T(8,128)S(1)}, f32[64,16,128]{2,1,0:T(8,128)S(1)}, u32[]{:S(2)}, u32[]{:S(2)}) collective-permute-start(f32[64,16,128]{2,1,0:T(8,128)S(1)} %all-to-all-done.own_ref), channel_id=1, source_target_pairs={{0,8},{8,1},{1,9},{9,3},{3,11},{11,2},{2,10},{4,12},{12,5},{5,13},... | collective-permute-start | bytes 1572872 | tf_op jit(solution)/shard_map/ppermute | solution.py:719
  36.4 0.7 copy-start.7
  49.0 5.8 %collective-permute-start.3 = (f32[64,8,128]{2,1,0:T(8,128)S(1)}, f32[64,8,128]{2,1,0:T(8,128)S(1)}, u32[]{:S(2)}, u32[]{:S(2)}) collective-permute-start(f32[64,8,128]{2,1,0:T(8,128)S(1)} %get-tuple-element.47.own_ref), channel_id=1, source_target_pairs={{8,0},{1,8},{9,1},{3,9},{11,3},{2,11},{10,2},{12,4},{5,12},{13,5},... | collective-permute-start | bytes 786440 | tf_op jit(solution)/shard_map/ppermute | solution.py:720
  50.9 7.7 %collective-permute-start.2 = (f32[64,8,128]{2,1,0:T(8,128)S(1)}, f32[64,8,128]{2,1,0:T(8,128)S(1)}, u32[]{:S(2)}, u32[]{:S(2)}) collective-permute-start(f32[64,8,128]{2,1,0:T(8,128)S(1)} %get-tuple-element.47.own_ref), channel_id=1, source_target_pairs={{0,8},{8,1},{1,9},{9,3},{3,11},{11,2},{2,10},{4,12},{12,5},{5,13},... | collective-permute-start | bytes 786440 | tf_op jit(solution)/shard_map/ppermute | solution.py:719
  62.9 5.8 %collective-permute-start.5 = (f32[64,8,128]{2,1,0:T(8,128)S(1)}, f32[64,8,128]{2,1,0:T(8,128)S(1)}, u32[]{:S(2)}, u32[]{:S(2)}) collective-permute-start(f32[64,8,128]{2,1,0:T(8,128)S(1)} %get-tuple-element.50.own_ref), channel_id=1, source_target_pairs={{8,0},{1,8},{9,1},{3,9},{11,3},{2,11},{10,2},{12,4},{5,12},{13,5},... | collective-permute-start | bytes 786440 | tf_op jit(solution)/shard_map/ppermute | solution.py:720
  64.8 7.7 %collective-permute-start.4 = (f32[64,8,128]{2,1,0:T(8,128)S(1)}, f32[64,8,128]{2,1,0:T(8,128)S(1)}, u32[]{:S(2)}, u32[]{:S(2)}) collective-permute-start(f32[64,8,128]{2,1,0:T(8,128)S(1)} %get-tuple-element.50.own_ref), channel_id=1, source_target_pairs={{0,8},{8,1},{1,9},{9,3},{3,11},{11,2},{2,10},{4,12},{12,5},{5,13},... | collective-permute-start | bytes 786440 | tf_op jit(solution)/shard_map/ppermute | solution.py:719
  76.9 5.8 %collective-permute-start.7 = (f32[64,8,128]{2,1,0:T(8,128)S(1)}, f32[64,8,128]{2,1,0:T(8,128)S(1)}, u32[]{:S(2)}, u32[]{:S(2)}) collective-permute-start(f32[64,8,128]{2,1,0:T(8,128)S(1)} %get-tuple-element.52.own_ref), channel_id=1, source_target_pairs={{8,0},{1,8},{9,1},{3,9},{11,3},{2,11},{10,2},{12,4},{5,12},{13,5},... | collective-permute-start | bytes 786440 | tf_op jit(solution)/shard_map/ppermute | solution.py:720
  78.8 8.3 %collective-permute-start.6 = (f32[64,8,128]{2,1,0:T(8,128)S(1)}, f32[64,8,128]{2,1,0:T(8,128)S(1)}, u32[]{:S(2)}, u32[]{:S(2)}) collective-permute-start(f32[64,8,128]{2,1,0:T(8,128)S(1)} %get-tuple-element.52.own_ref), channel_id=1, source_target_pairs={{0,8},{8,1},{1,9},{9,3},{3,11},{11,2},{2,10},{4,12},{12,5},{5,13},... | collective-permute-start | bytes 786440 | tf_op jit(solution)/shard_map/ppermute | solution.py:719
  87.1 4.1 %copy-start.6 = (f32[8]{0:T(128)S(1)}, f32[8]{0:T(128)}, u32[]{:S(2)}) copy-start(f32[8]{0:T(128)} %occ.3) | copy-start | bytes 100
  94.0 16.0 %all-to-all-start.1 = ((f32[8,80,128]{2,1,0:T(8,128)}), f32[8,80,128]{2,1,0:T(8,128)S(1)}, u32[]{:S(2)}, u32[]{:S(2)}) async-start(f32[8,80,128]{2,1,0:T(8,128)} %shard_map.119), calls=%async_computation.1 | async-start | bytes 655360 | tf_op jit(solution)/shard_map/all_to_all | solution.py:762
  99.1 7.1 %collective-permute-start.9 = (f32[64,8,128]{2,1,0:T(8,128)S(1)}, f32[64,8,128]{2,1,0:T(8,128)S(1)}, u32[]{:S(2)}, u32[]{:S(2)}) collective-permute-start(f32[64,8,128]{2,1,0:T(8,128)S(1)} %shard_map.118.own_ref.y_ref), channel_id=1, source_target_pairs={{8,0},{1,8},{9,1},{3,9},{11,3},{2,11},{10,2},{12,4},{5,12},{13,5},... | collective-permute-start | bytes 786440 | tf_op jit(solution)/shard_map/ppermute | solution.py:720
  102.2 7.7 %collective-permute-start.8 = (f32[64,8,128]{2,1,0:T(8,128)S(1)}, f32[64,8,128]{2,1,0:T(8,128)S(1)}, u32[]{:S(2)}, u32[]{:S(2)}) collective-permute-start(f32[64,8,128]{2,1,0:T(8,128)S(1)} %shard_map.118.own_ref.y_ref), channel_id=1, source_target_pairs={{0,8},{8,1},{1,9},{9,3},{3,11},{11,2},{2,10},{4,12},{12,5},{5,13},... | collective-permute-start | bytes 786440 | tf_op jit(solution)/shard_map/ppermute | solution.py:719

commit v6 on v5

--- a/solution.py
+++ b/solution.py
@@ -479,7 +479,7 @@
             update(src, r, ref[src, r : r + 8, :], near)
 
 
-def source_kernel(scalars, occ, own_ref, sent_ref, v, w, r0, *couplings):
+def source_kernel(scalars, occ, own_ref, sent_ref, up_ref, down_ref, v, w, r0, *couplings):
     mat = block_neighbours()
     low = lanes_low((8, 128))
     slab, occupation = scalars[0], occ[scalars[1]] / 64.0
@@ -498,6 +498,13 @@
             w[src, 24:32, :] = zero
 
     fill()
+    low3 = lanes_low((3, 128))
+    for src in range(32):
+        rows = slice(src * 3, src * 3 + 3)
+        a, b = v[src, 21:24, :], v[src + 32, 21:24, :]
+        up_ref[rows, :] = jnp.where(low3, swap(a), b)
+        a, b = v[src, 16:19, :], v[src + 32, 16:19, :]
+        down_ref[rows, :] = jnp.where(low3, a, swap(b))
     keep = {r: inside_slab_range(slab, r) for r in (13, 19)}
 
     def second(src, r, c, near):
@@ -543,9 +550,13 @@
     vmem = pl.BlockSpec(memory_space=pltpu.VMEM)
     return pl.pallas_call(
         source_kernel,
-        out_shape=jax.ShapeDtypeStruct((8, 80, 128), F32),
+        out_shape=(
+            jax.ShapeDtypeStruct((8, 80, 128), F32),
+            jax.ShapeDtypeStruct((96, 128), F32),
+            jax.ShapeDtypeStruct((96, 128), F32),
+        ),
         in_specs=[smem, smem, vmem],
-        out_specs=vmem,
+        out_specs=(vmem, vmem, vmem),
         scratch_shapes=[pltpu.VMEM((64, 40, 128), F32)] * 3 + COUPLINGS,
         compiler_params=VMEM,
     )(scalars, occupations, own)
@@ -623,6 +634,7 @@
     fx, va, vb, up, g, v, r1, v2, r2, v3, r3, wide = refs[1:13]
     couplings = refs[13:]
     low = lanes_low((8, 128))
+    low3 = lanes_low((3, 128))
     slab, factor = scalars[0], OMEGA * (occ[scalars[1]] / 64.0)
 
     for s in range(8):
@@ -647,10 +659,16 @@
 
     def fill():
         for src in range(64):
-            p, o, n = (factor * jnp.square(ref[src]) for ref in (prev_ref, y_ref, next_ref))
-            fx[src, 8:16, :] = swap(jnp.where(low, o, p))
+            o = factor * jnp.square(y_ref[src])
+            turned = swap(o)
+            rows = slice(src % 32 * 3, src % 32 * 3 + 3)
+            p, n = prev_ref[rows, :], next_ref[rows, :]
+            p, n = (p, swap(n)) if src < 32 else (swap(p), n)
+            fx[src, 8:16, :] = jnp.where(low, 0.0, turned)
+            fx[src, 13:16, :] = jnp.where(low3, p, turned[5:8])
             fx[src, 16:24, :] = o
-            fx[src, 24:32, :] = swap(jnp.where(low, n, o))
+            fx[src, 24:32, :] = jnp.where(low, turned, 0.0)
+            fx[src, 24:27, :] = jnp.where(low3, turned[0:3], n)
             out_ref[src, 0:8, :] = y_ref[src]
 
     fill()
@@ -711,14 +729,10 @@
     )(*ins)
 
 
-def exchange(value, axes, dim, width, order=None):
-    order = order or list(range(8))
-    up = [(order[i], order[i + 1]) for i in range(7)]
+def exchange(to_next, to_last):
+    up = [(SLAB_DEVICE[i], SLAB_DEVICE[i + 1]) for i in range(7)]
     down = [(j, i) for i, j in up]
-    length = value.shape[dim]
-    before = lax.ppermute(lax.slice_in_dim(value, length - width, length, axis=dim), axes, up)
-    after = lax.ppermute(lax.slice_in_dim(value, 0, width, axis=dim), axes, down)
-    return before, after
+    return lax.ppermute(to_next, GROUP, up), lax.ppermute(to_last, GROUP, down)
 
 
 def local(
@@ -744,7 +758,7 @@
     older = pot = None
     for k in range(0, DEGREE, 2):
         first, last = k == 0, k == DEGREE - 2
-        halo = exchange(own, GROUP, 1, own.shape[1], SLAB_DEVICE)
+        halo = exchange(own, own)
         outs = list(
             double_step(
                 first, last, coefs[k], coefs[k + 1], lists, strength, halo, own, older, pot, tiles, mats
@@ -757,8 +771,8 @@
             older = outs.pop(0)
 
     scalars = jnp.stack([slab, 2 * lax.axis_index("yhi") + lax.axis_index("xhi")]).astype(jnp.int32)
-    halo = exchange(own, GROUP, 1, 8, SLAB_DEVICE)
-    sent = source_step(scalars, occupations, own)
+    sent, last_planes, first_planes = source_step(scalars, occupations, own)
+    halo = exchange(last_planes, first_planes)
     got = lax.all_to_all(sent, GROUP, 0, 0, tiled=True)
     packed = finish_step(scalars, occupations, got, halo, own)
     back = lax.all_to_all(packed, PLANE, 0, 0, tiled=True)

time: 163 us -> 158 us (0.969)
  waiting for transfers between devices: 41.1 us -> 36.4 us
    ppermute x10, waiting for transfers between devices: 29.8 us -> 25.1 us  [the longest x5 16.3 us: exchange(): lax.ppermute(to_next, GROUP, up)]
    all_to_all x1, starting transfers between devices: 5.15 us -> 3.38 us  [local(): got = lax.all_to_all(sent, GROUP, 0, 0, tiled=True)]
where the time goes in v6:
time: 158 us; the launch traced here: 157 us
  blocking collectives  46.8 us (30%)
  starting transfers between devices  37.2 us (24%)
  waiting for transfers between devices  36.4 us (23%)
  Pallas kernels  29.5 us (19%)
  local copies, waits for them, and re-layouts  3.96 us (3%)
  other arithmetic  2.54 us (2%)
    all_to_all x1, blocking collectives, local(): back = lax.all_to_all(packed, PLANE, 0, 0, tiled=True)  24.5 us
    all_to_all x1, blocking collectives, local(): hartree = jnp.sum(lax.all_to_all(part, BAND, 0, 0, tiled=True), axis=0)  22.3 us
    pallas_call x4, Pallas kernels, double_step(): pl.pallas_call(functools.partial(double_kernel, first, last, coef1, coef2...  16.8 us
    ppermute x5, waiting for transfers between devices, exchange(): lax.ppermute(to_next, GROUP, up)  16.3 us
    ppermute x5, starting transfers between devices, exchange(): lax.ppermute(to_last, GROUP, down)  12 us
    all_to_all x1, waiting for transfers between devices, local(): own = lax.all_to_all(packed, PLANE, 0, 0, tiled=True)  11.2 us
    ppermute x5, starting transfers between devices, exchange(): lax.ppermute(to_next, GROUP, up)  11.1 us
    all_to_all x1, starting transfers between devices, local(): own = lax.all_to_all(packed, PLANE, 0, 0, tiled=True)  10.7 us
  transfers between devices with their start and end apart: 12, of which 11 were waited for; matrix products, arithmetic and copies ran while one was open for 2% of the time, Pallas kernels for 2%

profile of v6, /device:TPU:6, one launch (start us, length us, event | category | flops | bytes accessed | tf_op | source)
XLA Modules:
  0.0 157.3 jit_solution(7929140362655286293)
XLA Ops:
  3.5 10.7 %all-to-all-start = ((f32[64,16,128]{2,1,0:T(8,128)}), f32[64,16,128]{2,1,0:T(8,128)S(1)}, u32[]{:S(2)}, u32[]{:S(2)}) async-start(f32[64,16,128]{2,1,0:T(8,128)} %shard_map.113), calls=%async_computation | async-start | bytes 1048576 | tf_op jit(solution)/shard_map/all_to_all | solution.py:749
  17.1 3.1 %shard_map.114.refs_0_.refs_2_ = f32[64,2,8,128]{3,2,1,0:T(8,128)S(1)} custom-call(f32[64,4,512]{2,1,0:T(4,128)S(1)} %copy-done.2, bf16[512,128]{1,0:T(8,128)(2,1)S(1)} %copy-done.4), custom_call_target="tpu_custom_call" | custom-call | tf_op jit(solution)/shard_map/pallas_call | solution.py:140
  20.6 11.2 %all-to-all-done.own_ref = f32[64,16,128]{2,1,0:T(8,128)S(1)} async-done(((f32[64,16,128]{2,1,0:T(8,128)}), f32[64,16,128]{2,1,0:T(8,128)S(1)}, u32[]{:S(2)}, u32[]{:S(2)}) %all-to-all-start) | async-done | bytes 524320 | tf_op jit(solution)/shard_map/all_to_all | solution.py:749
  31.8 2.6 %collective-permute-start.1 = (f32[64,16,128]{2,1,0:T(8,128)S(1)}, f32[64,16,128]{2,1,0:T(8,128)S(1)}, u32[]{:S(2)}, u32[]{:S(2)}) collective-permute-start(f32[64,16,128]{2,1,0:T(8,128)S(1)} %all-to-all-done.own_ref), channel_id=1, source_target_pairs={{8,0},{1,8},{9,1},{3,9},{11,3},{2,11},{10,2},{12,4},{5,12},{13,5},... | collective-permute-start | bytes 1572872 | tf_op jit(solution)/shard_map/ppermute | solution.py:735
  37.2 3.9 %collective-permute-done.1.next_ref = f32[64,16,128]{2,1,0:T(8,128)S(1)} collective-permute-done((f32[64,16,128]{2,1,0:T(8,128)S(1)}, f32[64,16,128]{2,1,0:T(8,128)S(1)}, u32[]{:S(2)}, u32[]{:S(2)}) %collective-permute-start.1) | collective-permute-done | bytes 524320 | tf_op jit(solution)/shard_map/ppermute | solution.py:735
  41.1 3.8 %collective-permute-done.prev_ref = f32[64,16,128]{2,1,0:T(8,128)S(1)} collective-permute-done((f32[64,16,128]{2,1,0:T(8,128)S(1)}, f32[64,16,128]{2,1,0:T(8,128)S(1)}, u32[]{:S(2)}, u32[]{:S(2)}) %collective-permute-start) | collective-permute-done | bytes 524320 | tf_op jit(solution)/shard_map/ppermute | solution.py:735
  44.9 4.1 %shard_map.115 = (f32[64,8,128]{2,1,0:T(8,128)S(1)}, f32[64,24,128]{2,1,0:T(8,128)S(1)}, f32[64,24,128]{2,1,0:T(8,128)S(1)}) custom-call(s32[9,64]{1,0:T(8,128)S(1)} %stack.39.lists, f32[4,64]{1,0:T(4,128)S(1)} %select_reduce_fusion.strength, f32[64,16,128]{2,1,0:T(8,128)S(1)} %collective-permute-done.prev_ref, f32[64,16,128]{2,1,0:T(8,128)S(1)} %all-to-all-done.own_ref, ...), custom_call_target="tpu_custom_call" | custom-call | tf_op jit(solution)/shard_map/pallas_call | solution.py:324
  49.0 1.9 %collective-permute-start.3 = (f32[64,8,128]{2,1,0:T(8,128)S(1)}, f32[64,8,128]{2,1,0:T(8,128)S(1)}, u32[]{:S(2)}, u32[]{:S(2)}) collective-permute-start(f32[64,8,128]{2,1,0:T(8,128)S(1)} %get-tuple-element.50.own_ref), channel_id=1, source_target_pairs={{8,0},{1,8},{9,1},{3,9},{11,3},{2,11},{10,2},{12,4},{5,12},{13,5},... | collective-permute-start | bytes 786440 | tf_op jit(solution)/shard_map/ppermute | solution.py:735
  50.9 2.4 %collective-permute-start.2 = (f32[64,8,128]{2,1,0:T(8,128)S(1)}, f32[64,8,128]{2,1,0:T(8,128)S(1)}, u32[]{:S(2)}, u32[]{:S(2)}) collective-permute-start(f32[64,8,128]{2,1,0:T(8,128)S(1)} %get-tuple-element.50.own_ref), channel_id=1, source_target_pairs={{0,8},{8,1},{1,9},{9,3},{3,11},{11,2},{2,10},{4,12},{12,5},{5,13},... | collective-permute-start | bytes 786440 | tf_op jit(solution)/shard_map/ppermute | solution.py:735
  54.8 3.8 %collective-permute-done.2.prev_ref = f32[64,8,128]{2,1,0:T(8,128)S(1)} collective-permute-done((f32[64,8,128]{2,1,0:T(8,128)S(1)}, f32[64,8,128]{2,1,0:T(8,128)S(1)}, u32[]{:S(2)}, u32[]{:S(2)}) %collective-permute-start.2) | collective-permute-done | bytes 262176 | tf_op jit(solution)/shard_map/ppermute | solution.py:735
  58.6 4.2 %shard_map.116 = (f32[64,8,128]{2,1,0:T(8,128)S(1)}, f32[64,24,128]{2,1,0:T(8,128)S(1)}) custom-call(s32[9,64]{1,0:T(8,128)S(1)} %stack.39.lists, f32[4,64]{1,0:T(4,128)S(1)} %select_reduce_fusion.strength, f32[64,8,128]{2,1,0:T(8,128)S(1)} %collective-permute-done.2.prev_ref, f32[64,8,128]{2,1,0:T(8,128)S(1)} %get-tuple-element.50.own_ref, ...), custom_call_target="tpu_custom_call" | custom-call | tf_op jit(solution)/shard_map/pallas_call | solution.py:324
  64.8 2.4 %collective-permute-start.4 = (f32[64,8,128]{2,1,0:T(8,128)S(1)}, f32[64,8,128]{2,1,0:T(8,128)S(1)}, u32[]{:S(2)}, u32[]{:S(2)}) collective-permute-start(f32[64,8,128]{2,1,0:T(8,128)S(1)} %get-tuple-element.53.own_ref), channel_id=1, source_target_pairs={{0,8},{8,1},{1,9},{9,3},{3,11},{11,2},{2,10},{4,12},{12,5},{5,13},... | collective-permute-start | bytes 786440 | tf_op jit(solution)/shard_map/ppermute | solution.py:735
  68.7 3.8 %collective-permute-done.4.prev_ref = f32[64,8,128]{2,1,0:T(8,128)S(1)} collective-permute-done((f32[64,8,128]{2,1,0:T(8,128)S(1)}, f32[64,8,128]{2,1,0:T(8,128)S(1)}, u32[]{:S(2)}, u32[]{:S(2)}) %collective-permute-start.4) | collective-permute-done | bytes 262176 | tf_op jit(solution)/shard_map/ppermute | solution.py:735
  72.5 4.4 %shard_map.117 = (f32[64,8,128]{2,1,0:T(8,128)S(1)}, f32[64,24,128]{2,1,0:T(8,128)S(1)}) custom-call(s32[9,64]{1,0:T(8,128)S(1)} %stack.39.lists, f32[4,64]{1,0:T(4,128)S(1)} %select_reduce_fusion.strength, f32[64,8,128]{2,1,0:T(8,128)S(1)} %collective-permute-done.4.prev_ref, f32[64,8,128]{2,1,0:T(8,128)S(1)} %get-tuple-element.53.own_ref, ...), custom_call_target="tpu_custom_call" | custom-call | tf_op jit(solution)/shard_map/pallas_call | solution.py:324
  78.8 2.4 %collective-permute-start.6 = (f32[64,8,128]{2,1,0:T(8,128)S(1)}, f32[64,8,128]{2,1,0:T(8,128)S(1)}, u32[]{:S(2)}, u32[]{:S(2)}) collective-permute-start(f32[64,8,128]{2,1,0:T(8,128)S(1)} %get-tuple-element.55.own_ref), channel_id=1, source_target_pairs={{0,8},{8,1},{1,9},{9,3},{3,11},{11,2},{2,10},{4,12},{12,5},{5,13},... | collective-permute-start | bytes 786440 | tf_op jit(solution)/shard_map/ppermute | solution.py:735
  82.7 3.8 %collective-permute-done.6.prev_ref = f32[64,8,128]{2,1,0:T(8,128)S(1)} collective-permute-done((f32[64,8,128]{2,1,0:T(8,128)S(1)}, f32[64,8,128]{2,1,0:T(8,128)S(1)}, u32[]{:S(2)}, u32[]{:S(2)}) %collective-permute-start.6) | collective-permute-done | bytes 262176 | tf_op jit(solution)/shard_map/ppermute | solution.py:735
  86.5 4.1 %shard_map.118.own_ref.y_ref = f32[64,8,128]{2,1,0:T(8,128)S(1)} custom-call(s32[9,64]{1,0:T(8,128)S(1)} %stack.39.lists, f32[4,64]{1,0:T(4,128)S(1)} %select_reduce_fusion.strength, f32[64,8,128]{2,1,0:T(8,128)S(1)} %collective-permute-done.6.prev_ref, f32[64,8,128]{2,1,0:T(8,128)S(1)} %get-tuple-element.55.own_ref, ...), custom_call_target="tpu_custom_call" | custom-call | tf_op jit(solution)/shard_map/pallas_call | solution.py:324
  90.6 2.7 %shard_map.119 = (f32[8,80,128]{2,1,0:T(8,128)}, f32[96,128]{1,0:T(8,128)S(1)}, f32[96,128]{1,0:T(8,128)S(1)}) custom-call(s32[2]{0:T(128)S(1)} %pad_add_fusion.scalars, f32[8]{0:T(128)S(1)} %copy-done.6, f32[64,8,128]{2,1,0:T(8,128)S(1)} %shard_map.118.own_ref.y_ref), custom_call_target="tpu_custom_call" | custom-call | tf_op jit(solution)/shard_map/pallas_call | solution.py:551
  93.3 3.4 %all-to-all-start.1 = ((f32[8,80,128]{2,1,0:T(8,128)}), f32[8,80,128]{2,1,0:T(8,128)S(1)}, u32[]{:S(2)}, u32[]{:S(2)}) async-start(f32[8,80,128]{2,1,0:T(8,128)} %get-tuple-element.57), calls=%async_computation.1 | async-start | bytes 655360 | tf_op jit(solution)/shard_map/all_to_all | solution.py:776
  96.7 2.0 %collective-permute-start.8 = (f32[96,128]{1,0:T(8,128)S(1)}, f32[96,128]{1,0:T(8,128)S(1)}, u32[]{:S(2)}, u32[]{:S(2)}) collective-permute-start(f32[96,128]{1,0:T(8,128)S(1)} %get-tuple-element.58), channel_id=1, source_target_pairs={{0,8},{8,1},{1,9},{9,3},{3,11},{11,2},{2,10},{4,12},{12,5},{5,13},... | collective-permute-start | bytes 147464 | tf_op jit(solution)/shard_map/ppermute | solution.py:735
  98.7 3.6 %collective-permute-start.9 = (f32[96,128]{1,0:T(8,128)S(1)}, f32[96,128]{1,0:T(8,128)S(1)}, u32[]{:S(2)}, u32[]{:S(2)}) collective-permute-start(f32[96,128]{1,0:T(8,128)S(1)} %get-tuple-element.59), channel_id=1, source_target_pairs={{8,0},{1,8},{9,1},{3,9},{11,3},{2,11},{10,2},{12,4},{5,12},{13,5},... | collective-permute-start | bytes 147464 | tf_op jit(solution)/shard_map/ppermute | solution.py:735
  104.0 4.8 %shard_map.120 = f32[64,16,128]{2,1,0:T(8,128)S(1)} custom-call(s32[2]{0:T(128)S(1)} %pad_add_fusion.scalars, f32[8]{0:T(128)S(1)} %copy-done.6, f32[8,80,128]{2,1,0:T(8,128)S(1)} %all-to-all-done.1.got_ref, f32[96,128]{1,0:T(8,128)S(1)} %collective-permute-done.8.prev_ref, f32[64,8,128]{2,1,0:T(8,128)S(1)} %shard_map.118.own_ref.y_ref, ...), custom_call_target="tpu_custom_call" | custom-call | tf_op jit(solution)/shard_map/pallas_call | solution.py:708
  108.9 24.5 %all_to_all.20.in_ref = f32[64,16,128]{2,1,0:T(8,128)S(1)} all-to-all(f32[64,16,128]{2,1,0:T(8,128)S(1)} %shard_map.120), channel_id=1, replica_groups=mesh['z'=8,'yhi'=4,'core'=2,'xhi'=2,'xlo'=2,'ylo'=2] {'yhi','core','xhi'..., dimensions={0} | all-to-all | bytes 1048576 | tf_op jit(solution)/shard_map/all_to_all | solution.py:778
  134.3 22.3 %all_to_all.21 = f32[8,64,128]{2,1,0:T(8,128)S(1)} all-to-all(f32[8,64,128]{2,1,0:T(8,128)S(1)} %get-tuple-element.61), channel_id=1, replica_groups=mesh['z'=8,'yhi'=4,'core'=2,'xhi'=2,'xlo'=2,'ylo'=2] {'z'}, dimensions={0} | all-to-all | bytes 524288 | tf_op jit(solution)/shard_map/all_to_all | solution.py:780
  (43 shorter events, 20.3 us)
Async XLA Ops:
  0.6 1.0 copy-start.3
  1.6 0.8 copy-start.5
  3.5 13.6 %copy-start.2 = (f32[64,4,512]{2,1,0:T(4,128)S(1)}, f32[64,4,512]{2,1,0:T(4,128)}, u32[]{:S(2)}) copy-start(f32[64,4,512]{2,1,0:T(4,128)} %proj_ref.1) | copy-start | bytes 1572868
  3.5 13.6 %copy-start.4 = (bf16[512,128]{1,0:T(8,128)(2,1)S(1)}, bf16[512,128]{1,0:T(8,128)(2,1)}, u32[]{:S(2)}) copy-start(bf16[512,128]{1,0:T(8,128)(2,1)} %constant.129.clone.pick_ref) | copy-start | bytes 393220
  3.5 28.3 %all-to-all-start = ((f32[64,16,128]{2,1,0:T(8,128)}), f32[64,16,128]{2,1,0:T(8,128)S(1)}, u32[]{:S(2)}, u32[]{:S(2)}) async-start(f32[64,16,128]{2,1,0:T(8,128)} %shard_map.113), calls=%async_computation | async-start | bytes 1048576 | tf_op jit(solution)/shard_map/all_to_all | solution.py:749
  14.2 0.7 copy-start.8
  17.1 27.8 %copy-start = (bf16[128,640]{1,0:T(8,128)(2,1)S(1)}, bf16[128,640]{1,0:T(8,128)(2,1)}, u32[]{:S(2)}) copy-start(bf16[128,640]{1,0:T(8,128)(2,1)} %constant.128.clone.refs_2_.refs_4_) | copy-start | bytes 491524
  17.1 27.8 %copy-start.1 = (bf16[128,640]{1,0:T(8,128)(2,1)S(1)}, bf16[128,640]{1,0:T(8,128)(2,1)}, u32[]{:S(2)}) copy-start(bf16[128,640]{1,0:T(8,128)(2,1)} %constant.127.clone.refs_1_.refs_3_) | copy-start | bytes 491524
  31.8 9.3 %collective-permute-start.1 = (f32[64,16,128]{2,1,0:T(8,128)S(1)}, f32[64,16,128]{2,1,0:T(8,128)S(1)}, u32[]{:S(2)}, u32[]{:S(2)}) collective-permute-start(f32[64,16,128]{2,1,0:T(8,128)S(1)} %all-to-all-done.own_ref), channel_id=1, source_target_pairs={{8,0},{1,8},{9,1},{3,9},{11,3},{2,11},{10,2},{12,4},{5,12},{13,5},... | collective-permute-start | bytes 1572872 | tf_op jit(solution)/shard_map/ppermute | solution.py:735
  34.4 10.5 %collective-permute-start = (f32[64,16,128]{2,1,0:T(8,128)S(1)}, f32[64,16,128]{2,1,0:T(8,128)S(1)}, u32[]{:S(2)}, u32[]{:S(2)}) collective-permute-start(f32[64,16,128]{2,1,0:T(8,128)S(1)} %all-to-all-done.own_ref), channel_id=1, source_target_pairs={{0,8},{8,1},{1,9},{9,3},{3,11},{11,2},{2,10},{4,12},{12,5},{5,13},... | collective-permute-start | bytes 1572872 | tf_op jit(solution)/shard_map/ppermute | solution.py:735
  36.4 0.7 copy-start.7
  49.0 5.8 %collective-permute-start.3 = (f32[64,8,128]{2,1,0:T(8,128)S(1)}, f32[64,8,128]{2,1,0:T(8,128)S(1)}, u32[]{:S(2)}, u32[]{:S(2)}) collective-permute-start(f32[64,8,128]{2,1,0:T(8,128)S(1)} %get-tuple-element.50.own_ref), channel_id=1, source_target_pairs={{8,0},{1,8},{9,1},{3,9},{11,3},{2,11},{10,2},{12,4},{5,12},{13,5},... | collective-permute-start | bytes 786440 | tf_op jit(solution)/shard_map/ppermute | solution.py:735
  50.9 7.7 %collective-permute-start.2 = (f32[64,8,128]{2,1,0:T(8,128)S(1)}, f32[64,8,128]{2,1,0:T(8,128)S(1)}, u32[]{:S(2)}, u32[]{:S(2)}) collective-permute-start(f32[64,8,128]{2,1,0:T(8,128)S(1)} %get-tuple-element.50.own_ref), channel_id=1, source_target_pairs={{0,8},{8,1},{1,9},{9,3},{3,11},{11,2},{2,10},{4,12},{12,5},{5,13},... | collective-permute-start | bytes 786440 | tf_op jit(solution)/shard_map/ppermute | solution.py:735
  62.9 5.8 %collective-permute-start.5 = (f32[64,8,128]{2,1,0:T(8,128)S(1)}, f32[64,8,128]{2,1,0:T(8,128)S(1)}, u32[]{:S(2)}, u32[]{:S(2)}) collective-permute-start(f32[64,8,128]{2,1,0:T(8,128)S(1)} %get-tuple-element.53.own_ref), channel_id=1, source_target_pairs={{8,0},{1,8},{9,1},{3,9},{11,3},{2,11},{10,2},{12,4},{5,12},{13,5},... | collective-permute-start | bytes 786440 | tf_op jit(solution)/shard_map/ppermute | solution.py:735
  64.8 7.7 %collective-permute-start.4 = (f32[64,8,128]{2,1,0:T(8,128)S(1)}, f32[64,8,128]{2,1,0:T(8,128)S(1)}, u32[]{:S(2)}, u32[]{:S(2)}) collective-permute-start(f32[64,8,128]{2,1,0:T(8,128)S(1)} %get-tuple-element.53.own_ref), channel_id=1, source_target_pairs={{0,8},{8,1},{1,9},{9,3},{3,11},{11,2},{2,10},{4,12},{12,5},{5,13},... | collective-permute-start | bytes 786440 | tf_op jit(solution)/shard_map/ppermute | solution.py:735
  76.9 5.8 %collective-permute-start.7 = (f32[64,8,128]{2,1,0:T(8,128)S(1)}, f32[64,8,128]{2,1,0:T(8,128)S(1)}, u32[]{:S(2)}, u32[]{:S(2)}) collective-permute-start(f32[64,8,128]{2,1,0:T(8,128)S(1)} %get-tuple-element.55.own_ref), channel_id=1, source_target_pairs={{8,0},{1,8},{9,1},{3,9},{11,3},{2,11},{10,2},{12,4},{5,12},{13,5},... | collective-permute-start | bytes 786440 | tf_op jit(solution)/shard_map/ppermute | solution.py:735
  78.8 7.7 %collective-permute-start.6 = (f32[64,8,128]{2,1,0:T(8,128)S(1)}, f32[64,8,128]{2,1,0:T(8,128)S(1)}, u32[]{:S(2)}, u32[]{:S(2)}) collective-permute-start(f32[64,8,128]{2,1,0:T(8,128)S(1)} %get-tuple-element.55.own_ref), channel_id=1, source_target_pairs={{0,8},{8,1},{1,9},{9,3},{3,11},{11,2},{2,10},{4,12},{12,5},{5,13},... | collective-permute-start | bytes 786440 | tf_op jit(solution)/shard_map/ppermute | solution.py:735
  86.5 4.1 %copy-start.6 = (f32[8]{0:T(128)S(1)}, f32[8]{0:T(128)}, u32[]{:S(2)}) copy-start(f32[8]{0:T(128)} %occ.3) | copy-start | bytes 100
  93.3 10.7 %all-to-all-start.1 = ((f32[8,80,128]{2,1,0:T(8,128)}), f32[8,80,128]{2,1,0:T(8,128)S(1)}, u32[]{:S(2)}, u32[]{:S(2)}) async-start(f32[8,80,128]{2,1,0:T(8,128)} %get-tuple-element.57), calls=%async_computation.1 | async-start | bytes 655360 | tf_op jit(solution)/shard_map/all_to_all | solution.py:776
  96.7 6.6 %collective-permute-start.8 = (f32[96,128]{1,0:T(8,128)S(1)}, f32[96,128]{1,0:T(8,128)S(1)}, u32[]{:S(2)}, u32[]{:S(2)}) collective-permute-start(f32[96,128]{1,0:T(8,128)S(1)} %get-tuple-element.58), channel_id=1, source_target_pairs={{0,8},{8,1},{1,9},{9,3},{3,11},{11,2},{2,10},{4,12},{12,5},{5,13},... | collective-permute-start | bytes 147464 | tf_op jit(solution)/shard_map/ppermute | solution.py:735
  98.7 5.3 %collective-permute-start.9 = (f32[96,128]{1,0:T(8,128)S(1)}, f32[96,128]{1,0:T(8,128)S(1)}, u32[]{:S(2)}, u32[]{:S(2)}) collective-permute-start(f32[96,128]{1,0:T(8,128)S(1)} %get-tuple-element.59), channel_id=1, source_target_pairs={{8,0},{1,8},{9,1},{3,9},{11,3},{2,11},{10,2},{12,4},{5,12},{13,5},... | collective-permute-start | bytes 147464 | tf_op jit(solution)/shard_map/ppermute | solution.py:735

commit v7 on v6

--- a/solution.py
+++ b/solution.py
@@ -34,7 +34,7 @@
 CHIPS = ((0, 0), (0, 1), (1, 1), (1, 0))
 SLAB_DEVICE = [c * 4 + xl * 2 + yl for xl, yl in CHIPS for c in (0, 1)]
 VMEM = pltpu.CompilerParams(vmem_limit_bytes=12 * 1024 * 1024)
-HEAD = 3
+HEAD = 4
 F32 = jnp.float32
 BF16 = jnp.bfloat16
 
@@ -340,7 +340,7 @@
 def atom_lists(slab, proj_strength, atom_block, atom_offset):
     number = jnp.arange(64, dtype=jnp.int32)
     dz = atom_offset[:, 2] - 16 * slab
-    near = jnp.logical_and(dz >= -15, dz <= 23)
+    near = jnp.logical_and(dz >= -14, dz <= 22)
     before = jnp.sum(
         jnp.logical_and(near[None, :], number[None, :] < number[:, None]).astype(jnp.int32), axis=1
     )

time: 158 us -> 159 us (level)
  no operation moved by 1% of the time
where the time goes in v7:
time: 159 us; the launch traced here: 158 us
  blocking collectives  46.8 us (29%)
  starting transfers between devices  37.6 us (24%)
  waiting for transfers between devices  36 us (23%)
  Pallas kernels  30.2 us (19%)
  local copies, waits for them, and re-layouts  3.96 us (2%)
  other arithmetic  2.54 us (2%)
    all_to_all x1, blocking collectives, local(): back = lax.all_to_all(packed, PLANE, 0, 0, tiled=True)  24.5 us
    all_to_all x1, blocking collectives, local(): hartree = jnp.sum(lax.all_to_all(part, BAND, 0, 0, tiled=True), axis=0)  22.3 us
    pallas_call x4, Pallas kernels, double_step(): pl.pallas_call(functools.partial(double_kernel, first, last, coef1, coef2...  17.5 us
    ppermute x5, waiting for transfers between devices, exchange(): lax.ppermute(to_next, GROUP, up)  16.1 us
    ppermute x5, starting transfers between devices, exchange(): lax.ppermute(to_last, GROUP, down)  12.2 us
    ppermute x5, starting transfers between devices, exchange(): lax.ppermute(to_next, GROUP, up)  11.3 us
    all_to_all x1, waiting for transfers between devices, local(): own = lax.all_to_all(packed, PLANE, 0, 0, tiled=True)  11.2 us
    all_to_all x1, starting transfers between devices, local(): own = lax.all_to_all(packed, PLANE, 0, 0, tiled=True)  10.7 us
  transfers between devices with their start and end apart: 12, of which 11 were waited for; matrix products, arithmetic and copies ran while one was open for 2% of the time, Pallas kernels for 2%

profile of v7, /device:TPU:6, one launch (start us, length us, event | category | flops | bytes accessed | tf_op | source)
XLA Modules:
  0.0 158.0 jit_solution(17397326680284973739)
XLA Ops:
  3.5 10.7 %all-to-all-start = ((f32[64,16,128]{2,1,0:T(8,128)}), f32[64,16,128]{2,1,0:T(8,128)S(1)}, u32[]{:S(2)}, u32[]{:S(2)}) async-start(f32[64,16,128]{2,1,0:T(8,128)} %shard_map.113), calls=%async_computation | async-start | bytes 1048576 | tf_op jit(solution)/shard_map/all_to_all | solution.py:749
  17.1 3.1 %shard_map.114.refs_0_.refs_2_ = f32[64,2,8,128]{3,2,1,0:T(8,128)S(1)} custom-call(f32[64,4,512]{2,1,0:T(4,128)S(1)} %copy-done.2, bf16[512,128]{1,0:T(8,128)(2,1)S(1)} %copy-done.4), custom_call_target="tpu_custom_call" | custom-call | tf_op jit(solution)/shard_map/pallas_call | solution.py:140
  20.6 11.2 %all-to-all-done.own_ref = f32[64,16,128]{2,1,0:T(8,128)S(1)} async-done(((f32[64,16,128]{2,1,0:T(8,128)}), f32[64,16,128]{2,1,0:T(8,128)S(1)}, u32[]{:S(2)}, u32[]{:S(2)}) %all-to-all-start) | async-done | bytes 524320 | tf_op jit(solution)/shard_map/all_to_all | solution.py:749
  31.8 2.6 %collective-permute-start.1 = (f32[64,16,128]{2,1,0:T(8,128)S(1)}, f32[64,16,128]{2,1,0:T(8,128)S(1)}, u32[]{:S(2)}, u32[]{:S(2)}) collective-permute-start(f32[64,16,128]{2,1,0:T(8,128)S(1)} %all-to-all-done.own_ref), channel_id=1, source_target_pairs={{8,0},{1,8},{9,1},{3,9},{11,3},{2,11},{10,2},{12,4},{5,12},{13,5},... | collective-permute-start | bytes 1572872 | tf_op jit(solution)/shard_map/ppermute | solution.py:735
  34.4 1.9 %collective-permute-start = (f32[64,16,128]{2,1,0:T(8,128)S(1)}, f32[64,16,128]{2,1,0:T(8,128)S(1)}, u32[]{:S(2)}, u32[]{:S(2)}) collective-permute-start(f32[64,16,128]{2,1,0:T(8,128)S(1)} %all-to-all-done.own_ref), channel_id=1, source_target_pairs={{0,8},{8,1},{1,9},{9,3},{3,11},{11,2},{2,10},{4,12},{12,5},{5,13},... | collective-permute-start | bytes 1572872 | tf_op jit(solution)/shard_map/ppermute | solution.py:735
  37.2 3.9 %collective-permute-done.1.next_ref = f32[64,16,128]{2,1,0:T(8,128)S(1)} collective-permute-done((f32[64,16,128]{2,1,0:T(8,128)S(1)}, f32[64,16,128]{2,1,0:T(8,128)S(1)}, u32[]{:S(2)}, u32[]{:S(2)}) %collective-permute-start.1) | collective-permute-done | bytes 524320 | tf_op jit(solution)/shard_map/ppermute | solution.py:735
  41.1 3.8 %collective-permute-done.prev_ref = f32[64,16,128]{2,1,0:T(8,128)S(1)} collective-permute-done((f32[64,16,128]{2,1,0:T(8,128)S(1)}, f32[64,16,128]{2,1,0:T(8,128)S(1)}, u32[]{:S(2)}, u32[]{:S(2)}) %collective-permute-start) | collective-permute-done | bytes 524320 | tf_op jit(solution)/shard_map/ppermute | solution.py:735
  44.9 4.3 %shard_map.115 = (f32[64,8,128]{2,1,0:T(8,128)S(1)}, f32[64,24,128]{2,1,0:T(8,128)S(1)}, f32[64,24,128]{2,1,0:T(8,128)S(1)}) custom-call(s32[9,64]{1,0:T(8,128)S(1)} %stack.39.lists, f32[4,64]{1,0:T(4,128)S(1)} %select_reduce_fusion.strength, f32[64,16,128]{2,1,0:T(8,128)S(1)} %collective-permute-done.prev_ref, f32[64,16,128]{2,1,0:T(8,128)S(1)} %all-to-all-done.own_ref, ...), custom_call_target="tpu_custom_call" | custom-call | tf_op jit(solution)/shard_map/pallas_call | solution.py:324
  51.2 2.4 %collective-permute-start.2 = (f32[64,8,128]{2,1,0:T(8,128)S(1)}, f32[64,8,128]{2,1,0:T(8,128)S(1)}, u32[]{:S(2)}, u32[]{:S(2)}) collective-permute-start(f32[64,8,128]{2,1,0:T(8,128)S(1)} %get-tuple-element.50.own_ref), channel_id=1, source_target_pairs={{0,8},{8,1},{1,9},{9,3},{3,11},{11,2},{2,10},{4,12},{12,5},{5,13},... | collective-permute-start | bytes 786440 | tf_op jit(solution)/shard_map/ppermute | solution.py:735
  55.0 3.8 %collective-permute-done.2.prev_ref = f32[64,8,128]{2,1,0:T(8,128)S(1)} collective-permute-done((f32[64,8,128]{2,1,0:T(8,128)S(1)}, f32[64,8,128]{2,1,0:T(8,128)S(1)}, u32[]{:S(2)}, u32[]{:S(2)}) %collective-permute-start.2) | collective-permute-done | bytes 262176 | tf_op jit(solution)/shard_map/ppermute | solution.py:735
  58.9 4.5 %shard_map.116 = (f32[64,8,128]{2,1,0:T(8,128)S(1)}, f32[64,24,128]{2,1,0:T(8,128)S(1)}) custom-call(s32[9,64]{1,0:T(8,128)S(1)} %stack.39.lists, f32[4,64]{1,0:T(4,128)S(1)} %select_reduce_fusion.strength, f32[64,8,128]{2,1,0:T(8,128)S(1)} %collective-permute-done.2.prev_ref, f32[64,8,128]{2,1,0:T(8,128)S(1)} %get-tuple-element.50.own_ref, ...), custom_call_target="tpu_custom_call" | custom-call | tf_op jit(solution)/shard_map/pallas_call | solution.py:324
  65.3 2.6 %collective-permute-start.4 = (f32[64,8,128]{2,1,0:T(8,128)S(1)}, f32[64,8,128]{2,1,0:T(8,128)S(1)}, u32[]{:S(2)}, u32[]{:S(2)}) collective-permute-start(f32[64,8,128]{2,1,0:T(8,128)S(1)} %get-tuple-element.53.own_ref), channel_id=1, source_target_pairs={{0,8},{8,1},{1,9},{9,3},{3,11},{11,2},{2,10},{4,12},{12,5},{5,13},... | collective-permute-start | bytes 786440 | tf_op jit(solution)/shard_map/ppermute | solution.py:735
  69.1 3.8 %collective-permute-done.4.prev_ref = f32[64,8,128]{2,1,0:T(8,128)S(1)} collective-permute-done((f32[64,8,128]{2,1,0:T(8,128)S(1)}, f32[64,8,128]{2,1,0:T(8,128)S(1)}, u32[]{:S(2)}, u32[]{:S(2)}) %collective-permute-start.4) | collective-permute-done | bytes 262176 | tf_op jit(solution)/shard_map/ppermute | solution.py:735
  72.9 4.4 %shard_map.117 = (f32[64,8,128]{2,1,0:T(8,128)S(1)}, f32[64,24,128]{2,1,0:T(8,128)S(1)}) custom-call(s32[9,64]{1,0:T(8,128)S(1)} %stack.39.lists, f32[4,64]{1,0:T(4,128)S(1)} %select_reduce_fusion.strength, f32[64,8,128]{2,1,0:T(8,128)S(1)} %collective-permute-done.4.prev_ref, f32[64,8,128]{2,1,0:T(8,128)S(1)} %get-tuple-element.53.own_ref, ...), custom_call_target="tpu_custom_call" | custom-call | tf_op jit(solution)/shard_map/pallas_call | solution.py:324
  79.3 2.4 %collective-permute-start.6 = (f32[64,8,128]{2,1,0:T(8,128)S(1)}, f32[64,8,128]{2,1,0:T(8,128)S(1)}, u32[]{:S(2)}, u32[]{:S(2)}) collective-permute-start(f32[64,8,128]{2,1,0:T(8,128)S(1)} %get-tuple-element.55.own_ref), channel_id=1, source_target_pairs={{0,8},{8,1},{1,9},{9,3},{3,11},{11,2},{2,10},{4,12},{12,5},{5,13},... | collective-permute-start | bytes 786440 | tf_op jit(solution)/shard_map/ppermute | solution.py:735
  83.2 3.8 %collective-permute-done.6.prev_ref = f32[64,8,128]{2,1,0:T(8,128)S(1)} collective-permute-done((f32[64,8,128]{2,1,0:T(8,128)S(1)}, f32[64,8,128]{2,1,0:T(8,128)S(1)}, u32[]{:S(2)}, u32[]{:S(2)}) %collective-permute-start.6) | collective-permute-done | bytes 262176 | tf_op jit(solution)/shard_map/ppermute | solution.py:735
  87.0 4.3 %shard_map.118.own_ref.y_ref = f32[64,8,128]{2,1,0:T(8,128)S(1)} custom-call(s32[9,64]{1,0:T(8,128)S(1)} %stack.39.lists, f32[4,64]{1,0:T(4,128)S(1)} %select_reduce_fusion.strength, f32[64,8,128]{2,1,0:T(8,128)S(1)} %collective-permute-done.6.prev_ref, f32[64,8,128]{2,1,0:T(8,128)S(1)} %get-tuple-element.55.own_ref, ...), custom_call_target="tpu_custom_call" | custom-call | tf_op jit(solution)/shard_map/pallas_call | solution.py:324
  91.3 2.7 %shard_map.119 = (f32[8,80,128]{2,1,0:T(8,128)}, f32[96,128]{1,0:T(8,128)S(1)}, f32[96,128]{1,0:T(8,128)S(1)}) custom-call(s32[2]{0:T(128)S(1)} %pad_add_fusion.scalars, f32[8]{0:T(128)S(1)} %copy-done.6, f32[64,8,128]{2,1,0:T(8,128)S(1)} %shard_map.118.own_ref.y_ref), custom_call_target="tpu_custom_call" | custom-call | tf_op jit(solution)/shard_map/pallas_call | solution.py:551
  94.1 3.4 %all-to-all-start.1 = ((f32[8,80,128]{2,1,0:T(8,128)}), f32[8,80,128]{2,1,0:T(8,128)S(1)}, u32[]{:S(2)}, u32[]{:S(2)}) async-start(f32[8,80,128]{2,1,0:T(8,128)} %get-tuple-element.57), calls=%async_computation.1 | async-start | bytes 655360 | tf_op jit(solution)/shard_map/all_to_all | solution.py:776
  97.4 2.0 %collective-permute-start.8 = (f32[96,128]{1,0:T(8,128)S(1)}, f32[96,128]{1,0:T(8,128)S(1)}, u32[]{:S(2)}, u32[]{:S(2)}) collective-permute-start(f32[96,128]{1,0:T(8,128)S(1)} %get-tuple-element.58), channel_id=1, source_target_pairs={{0,8},{8,1},{1,9},{9,3},{3,11},{11,2},{2,10},{4,12},{12,5},{5,13},... | collective-permute-start | bytes 147464 | tf_op jit(solution)/shard_map/ppermute | solution.py:735
  99.4 3.8 %collective-permute-start.9 = (f32[96,128]{1,0:T(8,128)S(1)}, f32[96,128]{1,0:T(8,128)S(1)}, u32[]{:S(2)}, u32[]{:S(2)}) collective-permute-start(f32[96,128]{1,0:T(8,128)S(1)} %get-tuple-element.59), channel_id=1, source_target_pairs={{8,0},{1,8},{9,1},{3,9},{11,3},{2,11},{10,2},{12,4},{5,12},{13,5},... | collective-permute-start | bytes 147464 | tf_op jit(solution)/shard_map/ppermute | solution.py:735
  104.8 4.8 %shard_map.120 = f32[64,16,128]{2,1,0:T(8,128)S(1)} custom-call(s32[2]{0:T(128)S(1)} %pad_add_fusion.scalars, f32[8]{0:T(128)S(1)} %copy-done.6, f32[8,80,128]{2,1,0:T(8,128)S(1)} %all-to-all-done.1.got_ref, f32[96,128]{1,0:T(8,128)S(1)} %collective-permute-done.8.prev_ref, f32[64,8,128]{2,1,0:T(8,128)S(1)} %shard_map.118.own_ref.y_ref, ...), custom_call_target="tpu_custom_call" | custom-call | tf_op jit(solution)/shard_map/pallas_call | solution.py:708
  109.6 24.5 %all_to_all.20.in_ref = f32[64,16,128]{2,1,0:T(8,128)S(1)} all-to-all(f32[64,16,128]{2,1,0:T(8,128)S(1)} %shard_map.120), channel_id=1, replica_groups=mesh['z'=8,'yhi'=4,'core'=2,'xhi'=2,'xlo'=2,'ylo'=2] {'yhi','core','xhi'..., dimensions={0} | all-to-all | bytes 1048576 | tf_op jit(solution)/shard_map/all_to_all | solution.py:778
  135.0 22.3 %all_to_all.21 = f32[8,64,128]{2,1,0:T(8,128)S(1)} all-to-all(f32[8,64,128]{2,1,0:T(8,128)S(1)} %get-tuple-element.61), channel_id=1, replica_groups=mesh['z'=8,'yhi'=4,'core'=2,'xhi'=2,'xlo'=2,'ylo'=2] {'z'}, dimensions={0} | all-to-all | bytes 524288 | tf_op jit(solution)/shard_map/all_to_all | solution.py:780
  (43 shorter events, 19.9 us)
Async XLA Ops:
  0.6 1.0 copy-start.3
  1.6 0.8 copy-start.5
  3.5 13.6 %copy-start.2 = (f32[64,4,512]{2,1,0:T(4,128)S(1)}, f32[64,4,512]{2,1,0:T(4,128)}, u32[]{:S(2)}) copy-start(f32[64,4,512]{2,1,0:T(4,128)} %proj_ref.1) | copy-start | bytes 1572868
  3.5 13.6 %copy-start.4 = (bf16[512,128]{1,0:T(8,128)(2,1)S(1)}, bf16[512,128]{1,0:T(8,128)(2,1)}, u32[]{:S(2)}) copy-start(bf16[512,128]{1,0:T(8,128)(2,1)} %constant.129.clone.pick_ref) | copy-start | bytes 393220
  3.5 28.3 %all-to-all-start = ((f32[64,16,128]{2,1,0:T(8,128)}), f32[64,16,128]{2,1,0:T(8,128)S(1)}, u32[]{:S(2)}, u32[]{:S(2)}) async-start(f32[64,16,128]{2,1,0:T(8,128)} %shard_map.113), calls=%async_computation | async-start | bytes 1048576 | tf_op jit(solution)/shard_map/all_to_all | solution.py:749
  14.2 0.7 copy-start.8
  17.1 27.8 %copy-start = (bf16[128,640]{1,0:T(8,128)(2,1)S(1)}, bf16[128,640]{1,0:T(8,128)(2,1)}, u32[]{:S(2)}) copy-start(bf16[128,640]{1,0:T(8,128)(2,1)} %constant.128.clone.refs_2_.refs_4_) | copy-start | bytes 491524
  17.1 27.8 %copy-start.1 = (bf16[128,640]{1,0:T(8,128)(2,1)S(1)}, bf16[128,640]{1,0:T(8,128)(2,1)}, u32[]{:S(2)}) copy-start(bf16[128,640]{1,0:T(8,128)(2,1)} %constant.127.clone.refs_1_.refs_3_) | copy-start | bytes 491524
  31.8 9.3 %collective-permute-start.1 = (f32[64,16,128]{2,1,0:T(8,128)S(1)}, f32[64,16,128]{2,1,0:T(8,128)S(1)}, u32[]{:S(2)}, u32[]{:S(2)}) collective-permute-start(f32[64,16,128]{2,1,0:T(8,128)S(1)} %all-to-all-done.own_ref), channel_id=1, source_target_pairs={{8,0},{1,8},{9,1},{3,9},{11,3},{2,11},{10,2},{12,4},{5,12},{13,5},... | collective-permute-start | bytes 1572872 | tf_op jit(solution)/shard_map/ppermute | solution.py:735
  34.4 10.5 %collective-permute-start = (f32[64,16,128]{2,1,0:T(8,128)S(1)}, f32[64,16,128]{2,1,0:T(8,128)S(1)}, u32[]{:S(2)}, u32[]{:S(2)}) collective-permute-start(f32[64,16,128]{2,1,0:T(8,128)S(1)} %all-to-all-done.own_ref), channel_id=1, source_target_pairs={{0,8},{8,1},{1,9},{9,3},{3,11},{11,2},{2,10},{4,12},{12,5},{5,13},... | collective-permute-start | bytes 1572872 | tf_op jit(solution)/shard_map/ppermute | solution.py:735
  36.4 0.7 copy-start.7
  49.2 5.8 %collective-permute-start.3 = (f32[64,8,128]{2,1,0:T(8,128)S(1)}, f32[64,8,128]{2,1,0:T(8,128)S(1)}, u32[]{:S(2)}, u32[]{:S(2)}) collective-permute-start(f32[64,8,128]{2,1,0:T(8,128)S(1)} %get-tuple-element.50.own_ref), channel_id=1, source_target_pairs={{8,0},{1,8},{9,1},{3,9},{11,3},{2,11},{10,2},{12,4},{5,12},{13,5},... | collective-permute-start | bytes 786440 | tf_op jit(solution)/shard_map/ppermute | solution.py:735
  51.2 7.7 %collective-permute-start.2 = (f32[64,8,128]{2,1,0:T(8,128)S(1)}, f32[64,8,128]{2,1,0:T(8,128)S(1)}, u32[]{:S(2)}, u32[]{:S(2)}) collective-permute-start(f32[64,8,128]{2,1,0:T(8,128)S(1)} %get-tuple-element.50.own_ref), channel_id=1, source_target_pairs={{0,8},{8,1},{1,9},{9,3},{3,11},{11,2},{2,10},{4,12},{12,5},{5,13},... | collective-permute-start | bytes 786440 | tf_op jit(solution)/shard_map/ppermute | solution.py:735
  63.3 5.8 %collective-permute-start.5 = (f32[64,8,128]{2,1,0:T(8,128)S(1)}, f32[64,8,128]{2,1,0:T(8,128)S(1)}, u32[]{:S(2)}, u32[]{:S(2)}) collective-permute-start(f32[64,8,128]{2,1,0:T(8,128)S(1)} %get-tuple-element.53.own_ref), channel_id=1, source_target_pairs={{8,0},{1,8},{9,1},{3,9},{11,3},{2,11},{10,2},{12,4},{5,12},{13,5},... | collective-permute-start | bytes 786440 | tf_op jit(solution)/shard_map/ppermute | solution.py:735
  65.3 7.7 %collective-permute-start.4 = (f32[64,8,128]{2,1,0:T(8,128)S(1)}, f32[64,8,128]{2,1,0:T(8,128)S(1)}, u32[]{:S(2)}, u32[]{:S(2)}) collective-permute-start(f32[64,8,128]{2,1,0:T(8,128)S(1)} %get-tuple-element.53.own_ref), channel_id=1, source_target_pairs={{0,8},{8,1},{1,9},{9,3},{3,11},{11,2},{2,10},{4,12},{12,5},{5,13},... | collective-permute-start | bytes 786440 | tf_op jit(solution)/shard_map/ppermute | solution.py:735
  77.4 5.8 %collective-permute-start.7 = (f32[64,8,128]{2,1,0:T(8,128)S(1)}, f32[64,8,128]{2,1,0:T(8,128)S(1)}, u32[]{:S(2)}, u32[]{:S(2)}) collective-permute-start(f32[64,8,128]{2,1,0:T(8,128)S(1)} %get-tuple-element.55.own_ref), channel_id=1, source_target_pairs={{8,0},{1,8},{9,1},{3,9},{11,3},{2,11},{10,2},{12,4},{5,12},{13,5},... | collective-permute-start | bytes 786440 | tf_op jit(solution)/shard_map/ppermute | solution.py:735
  79.3 7.7 %collective-permute-start.6 = (f32[64,8,128]{2,1,0:T(8,128)S(1)}, f32[64,8,128]{2,1,0:T(8,128)S(1)}, u32[]{:S(2)}, u32[]{:S(2)}) collective-permute-start(f32[64,8,128]{2,1,0:T(8,128)S(1)} %get-tuple-element.55.own_ref), channel_id=1, source_target_pairs={{0,8},{8,1},{1,9},{9,3},{3,11},{11,2},{2,10},{4,12},{12,5},{5,13},... | collective-permute-start | bytes 786440 | tf_op jit(solution)/shard_map/ppermute | solution.py:735
  87.0 4.3 %copy-start.6 = (f32[8]{0:T(128)S(1)}, f32[8]{0:T(128)}, u32[]{:S(2)}) copy-start(f32[8]{0:T(128)} %occ.3) | copy-start | bytes 100
  94.1 10.7 %all-to-all-start.1 = ((f32[8,80,128]{2,1,0:T(8,128)}), f32[8,80,128]{2,1,0:T(8,128)S(1)}, u32[]{:S(2)}, u32[]{:S(2)}) async-start(f32[8,80,128]{2,1,0:T(8,128)} %get-tuple-element.57), calls=%async_computation.1 | async-start | bytes 655360 | tf_op jit(solution)/shard_map/all_to_all | solution.py:776
  97.4 6.6 %collective-permute-start.8 = (f32[96,128]{1,0:T(8,128)S(1)}, f32[96,128]{1,0:T(8,128)S(1)}, u32[]{:S(2)}, u32[]{:S(2)}) collective-permute-start(f32[96,128]{1,0:T(8,128)S(1)} %get-tuple-element.58), channel_id=1, source_target_pairs={{0,8},{8,1},{1,9},{9,3},{3,11},{11,2},{2,10},{4,12},{12,5},{5,13},... | collective-permute-start | bytes 147464 | tf_op jit(solution)/shard_map/ppermute | solution.py:735
  99.4 5.3 %collective-permute-start.9 = (f32[96,128]{1,0:T(8,128)S(1)}, f32[96,128]{1,0:T(8,128)S(1)}, u32[]{:S(2)}, u32[]{:S(2)}) collective-permute-start(f32[96,128]{1,0:T(8,128)S(1)} %get-tuple-element.59), channel_id=1, source_target_pairs={{8,0},{1,8},{9,1},{3,9},{11,3},{2,11},{10,2},{12,4},{5,12},{13,5},... | collective-permute-start | bytes 147464 | tf_op jit(solution)/shard_map/ppermute | solution.py:735
